TPU v7x, 32 devices: a whole 2x2x4 slice. The times are simulated.
32 devices in a mesh: groups: 2 (over x), pairs: 16 (over z, y, core).
Axes of the slice: x: 2, y: 2, z: 4, core: 2. Of those that a mesh axis runs over, the one named last changes fastest.
Arguments:
- fitted_ints: bfloat16 [32, 1024, 4096], P(None, None, ('groups', 'pairs')), parts along dimension 2, may hold values from -1 to 1
- pno_basis: bfloat16 [128, 256, 64], P(('groups', 'pairs')), parts along dimension 0, may hold values from -0.375 to 0.375
- pair_occ: int32 [128, 2], P(('groups', 'pairs')), parts along dimension 0, may hold values from 0 to 31
- pair_dom: int32 [128, 256], P(('groups', 'pairs')), parts along dimension 0, may hold values from 0 to 1023, as said below
- pno_count: int32 [128], P(('groups', 'pairs')), parts along dimension 0, may hold values from 32 to 64
- pno_energy: float32 [128, 64], P(('groups', 'pairs')), parts along dimension 0, may hold values from 0.3 to 3
- occ_energy: float32 [64], P('groups'), parts along dimension 0, may hold values from -2 to -0.5
- amps: float32 [128, 64, 64], P(('groups', 'pairs')), parts along dimension 0, may hold values from -2 to 2
- cpl_pair: int32 [128, 8], P(('groups', 'pairs')), parts along dimension 0, may hold values from 0 to 63
- cpl_weight: float32 [128, 8], P(('groups', 'pairs')), parts along dimension 0, may hold values from -0.5 to 0.5
- intersections: bfloat16 [128, 8, 64, 64], P(('groups', 'pairs')), parts along dimension 0, may hold values from -1 to 1
Outputs:
- new_amps: float32 [128, 64, 64], P(('groups', 'pairs')), parts along dimension 0
- pair_ints: float32 [128, 64, 64], P(('groups', 'pairs')), parts along dimension 0
There are 2 independent parts, one for each index of `groups`. A program takes and returns all parts, laid end to end along the dimension named above; each array names one. Nothing has to cross between parts.
Inputs may be any that keep to these rules, and one draw needn't show every extreme that they name: `pair_dom`: each row holds 256 different PAO indices.
All inputs are finite; a program needn't handle non-finite values.
Results may differ from a plain program's by a relative error of at most 0.003.
Values may be sent and summed in bfloat16 or wider, within the bound.
No kernel may reach another device: no remote copies, remote signals or barrier semaphores. Data moves between devices by JAX's collectives and lax.ppermute only.
A program may use at most 128 MiB of HBM per device.

v0:
```python
import math

import jax
import jax.numpy as jnp
from jax import lax
from jax.sharding import PartitionSpec as P


def select_rows(fitted_ints, occ_list, dom_list):
    npair = occ_list.shape[0]
    domain = dom_list.shape[1]
    nocc = fitted_ints.shape[0]
    npao = fitted_ints.shape[1]
    aux_dev = fitted_ints.shape[2]
    block = math.gcd(npair, 16)
    occ_iota = jnp.arange(nocc, dtype=jnp.int32)
    pao_iota = jnp.arange(npao, dtype=jnp.int32)

    def one_block(items):
        occ_b, dom_b = items
        occ_hits = (occ_b[:, :, None] == occ_iota[None, None, :]).astype(jnp.bfloat16)
        slabs = jnp.einsum(
            "bto,oak->btak", occ_hits, fitted_ints, preferred_element_type=jnp.float32
        ).astype(jnp.bfloat16)
        dom_hits = (dom_b[:, :, None] == pao_iota[None, None, :]).astype(jnp.bfloat16)
        return jnp.einsum(
            "bda,btak->btdk", dom_hits, slabs, preferred_element_type=jnp.float32
        ).astype(jnp.bfloat16)

    picked = lax.map(
        one_block, (occ_list.reshape(-1, block, 2), dom_list.reshape(-1, block, domain))
    )
    return picked.reshape(npair, 2, domain, aux_dev)


def shards(
    fitted_ints,
    pno_basis,
    pair_occ,
    pair_dom,
    pno_count,
    pno_energy,
    occ_energy,
    amps,
    cpl_pair,
    cpl_weight,
    intersections,
):
    ndev = lax.axis_size("pairs")
    per_dev = pno_basis.shape[0]
    npno = pno_basis.shape[2]
    occ_all, dom_all = (
        lax.all_gather(pair_occ, "pairs", axis=0, tiled=True),
        lax.all_gather(pair_dom, "pairs", axis=0, tiled=True),
    )
    picked = select_rows(fitted_ints, occ_all, dom_all)
    aux_dev = picked.shape[3]
    sent = picked.reshape(ndev, per_dev, 2, picked.shape[2], aux_dev)
    arrived = lax.all_to_all(sent, "pairs", split_axis=0, concat_axis=0, tiled=True)
    fitted = jnp.einsum(
        "sptak,pae->sptke", arrived, pno_basis, preferred_element_type=jnp.float32
    ).astype(jnp.bfloat16)
    exch = jnp.einsum(
        "spke,spkf->pef", fitted[:, :, 0], fitted[:, :, 1], preferred_element_type=jnp.float32
    )
    targets = cpl_pair.reshape(-1)
    empty = jnp.zeros((targets.shape[0], npno * npno), jnp.float32)
    piece = lax.all_gather(amps.astype(jnp.bfloat16), "pairs", axis=0, tiled=True).astype(
        jnp.float32
    )
    count = piece.shape[0]
    hits = (targets[:, None] == jnp.arange(count, dtype=jnp.int32)[None, :]).astype(jnp.float32)
    chosen = empty + jnp.dot(hits, piece.reshape(count, -1), precision=lax.Precision.HIGHEST)
    chosen = (
        chosen.reshape(cpl_pair.shape[0], cpl_pair.shape[1], npno, npno)
        * cpl_weight[:, :, None, None]
    )
    sfull = intersections.astype(jnp.float32)
    half = jnp.einsum("pcae,pcef->pcaf", sfull, chosen, precision=lax.Precision.HIGHEST)
    coupled = jnp.einsum("pcaf,pcbf->pab", half, sfull, precision=lax.Precision.HIGHEST)
    occ_pair = occ_energy[pair_occ[:, 0]] + occ_energy[pair_occ[:, 1]]
    denom = pno_energy[:, :, None] + pno_energy[:, None, :] - occ_pair[:, None, None]
    resid = exch + denom * amps + coupled
    index = jnp.arange(npno, dtype=jnp.int32)
    live = (index[None, :] < pno_count[:, None]).astype(jnp.float32)
    mask = live[:, :, None] * live[:, None, :]
    new_amps = mask * (amps - resid / (denom + 0.5))
    return (new_amps, mask * exch)


def solution(mesh):
    in_specs = (
        P(None, None, ("groups", "pairs")),
        P(("groups", "pairs"), None, None),
        P(("groups", "pairs"), None),
        P(("groups", "pairs"), None),
        P(("groups", "pairs")),
        P(("groups", "pairs"), None),
        P("groups"),
        P(("groups", "pairs"), None, None),
        P(("groups", "pairs"), None),
        P(("groups", "pairs"), None),
        P(("groups", "pairs"), None, None, None),
    )
    out_specs = (P(("groups", "pairs"), None, None), P(("groups", "pairs"), None, None))
    return jax.shard_map(shards, mesh=mesh, in_specs=in_specs, out_specs=out_specs, check_vma=False)
```

profile of v0, /device:TPU:9, one launch (start us, length us, event | category | flops | bytes accessed | tf_op | source)
XLA Modules:
  0.0 336.5 jit_solution(10444010149213248425)
XLA Ops:
  0.7 12.0 %copy.24 = bf16[32,1024,128]{2,0,1:T(8,128)(2,1)} copy(bf16[32,1024,128]{2,1,0:T(8,128)(2,1)} %param.13) | data formatting | bytes 16777216
  12.7 19.5 %all-gather.1 = s32[16,4,256]{2,1,0:T(4,128)S(1)} all-gather(s32[1,4,256]{2,1,0:T(4,128)S(1)} %bitcast.100), channel_id=1, replica_groups=mesh['groups'=2,'pairs'=16] {'pairs'}, dimensions={0}, use_global_device_ids=true | all-gather | bytes 69632 | tf_op jit(solution)/shard_map/all_gather | solution.py:54
  32.3 17.4 %all-gather = s32[16,4,2]{1,2,0:T(2,128)S(1)} all-gather(s32[1,4,2]{1,2,0:T(2,128)S(1)} %bitcast.101), channel_id=1, replica_groups=mesh['groups'=2,'pairs'=16] {'pairs'}, dimensions={0}, use_global_device_ids=true | all-gather | bytes 544 | tf_op jit(solution)/shard_map/all_gather | solution.py:53
  49.8 71.6 %while.11 = (s32[]{:T(128)}, bf16[4,16,2,256,128]{4,3,2,1,0:T(8,128)(2,1)}, s32[4,16,2]{1,0,2:T(4,128)S(1)}, bf16[32,1024,128]{2,0,1:T(8,128)(2,1)}, s32[4,16,256]{2,1,0:T(8,128)S(1)}, /*index=5*/s32[]{:T(128)}) while((s32[]{:T(128)}, bf16[4,16,2,256,128]{4,3,2,1,0:T(8,128)(2,1)}, s32[4,16,2]{1,0,2:T(4,128)S(1)}, ...), condition=%wide.region_1.2_spmd.clone, body=%wide.region_0.1_spmd.clone.sunk | while | flops 2425357312 | bytes 35701708 | solution.py:30
  49.8 5.7 %fusion.50 = bf16[16,2,1024,128]{3,0,2,1:T(8,128)(2,1)S(1)} fusion(bf16[32,1024,128]{2,0,1:T(8,128)(2,1)} %get-tuple-element.130, s32[16,2]{0,1:T(2,128)S(1)} %bitcast.99), kind=kOutput, calls=%fused_computation.11.clone.1 | convolution fusion | flops 272630784 | bytes 16777344 | tf_op jit(solution)/shard_map/while/body/eval_jaxpr/bto,oak->btak/dot_general | solution.py:22
  55.5 7.6 %convert_bitcast_fusion.3 = bf16[1,16,2,256,128]{3,4,2,1,0:T(8,128)(2,1)} fusion(s32[16,256]{1,0:T(8,128)S(1)} %dynamic-slice_bitcast_fusion.2, bf16[16,2,1024,128]{3,0,2,1:T(8,128)(2,1)S(1)} %fusion.50), kind=kOutput, calls=%fused_computation.12.clone.1 | convolution fusion | flops 2152726528 | bytes 10502144 | tf_op jit(solution)/shard_map/while/body/eval_jaxpr/bda,btak->btdk/dot_general | solution.py:26
  63.1 3.0 copy.54
  66.2 1.5 constant_dynamic-update-slice_fusion.2
  67.7 5.8 %fusion.50 = bf16[16,2,1024,128]{3,0,2,1:T(8,128)(2,1)S(1)} fusion(bf16[32,1024,128]{2,0,1:T(8,128)(2,1)} %get-tuple-element.130, s32[16,2]{0,1:T(2,128)S(1)} %bitcast.99), kind=kOutput, calls=%fused_computation.11.clone.1 | convolution fusion | flops 272630784 | bytes 16777344 | tf_op jit(solution)/shard_map/while/body/eval_jaxpr/bto,oak->btak/dot_general | solution.py:22
  73.5 7.6 %convert_bitcast_fusion.3 = bf16[1,16,2,256,128]{3,4,2,1,0:T(8,128)(2,1)} fusion(s32[16,256]{1,0:T(8,128)S(1)} %dynamic-slice_bitcast_fusion.2, bf16[16,2,1024,128]{3,0,2,1:T(8,128)(2,1)S(1)} %fusion.50), kind=kOutput, calls=%fused_computation.12.clone.1 | convolution fusion | flops 2152726528 | bytes 10502144 | tf_op jit(solution)/shard_map/while/body/eval_jaxpr/bda,btak->btdk/dot_general | solution.py:26
  81.1 3.0 copy.54
  84.1 1.5 constant_dynamic-update-slice_fusion.2
  85.6 5.8 %fusion.50 = bf16[16,2,1024,128]{3,0,2,1:T(8,128)(2,1)S(1)} fusion(bf16[32,1024,128]{2,0,1:T(8,128)(2,1)} %get-tuple-element.130, s32[16,2]{0,1:T(2,128)S(1)} %bitcast.99), kind=kOutput, calls=%fused_computation.11.clone.1 | convolution fusion | flops 272630784 | bytes 16777344 | tf_op jit(solution)/shard_map/while/body/eval_jaxpr/bto,oak->btak/dot_general | solution.py:22
  91.4 7.6 %convert_bitcast_fusion.3 = bf16[1,16,2,256,128]{3,4,2,1,0:T(8,128)(2,1)} fusion(s32[16,256]{1,0:T(8,128)S(1)} %dynamic-slice_bitcast_fusion.2, bf16[16,2,1024,128]{3,0,2,1:T(8,128)(2,1)S(1)} %fusion.50), kind=kOutput, calls=%fused_computation.12.clone.1 | convolution fusion | flops 2152726528 | bytes 10502144 | tf_op jit(solution)/shard_map/while/body/eval_jaxpr/bda,btak->btdk/dot_general | solution.py:26
  99.0 3.0 copy.54
  102.0 1.5 constant_dynamic-update-slice_fusion.2
  103.5 5.7 %fusion.50 = bf16[16,2,1024,128]{3,0,2,1:T(8,128)(2,1)S(1)} fusion(bf16[32,1024,128]{2,0,1:T(8,128)(2,1)} %get-tuple-element.130, s32[16,2]{0,1:T(2,128)S(1)} %bitcast.99), kind=kOutput, calls=%fused_computation.11.clone.1 | convolution fusion | flops 272630784 | bytes 16777344 | tf_op jit(solution)/shard_map/while/body/eval_jaxpr/bto,oak->btak/dot_general | solution.py:22
  109.3 7.6 %convert_bitcast_fusion.3 = bf16[1,16,2,256,128]{3,4,2,1,0:T(8,128)(2,1)} fusion(s32[16,256]{1,0:T(8,128)S(1)} %dynamic-slice_bitcast_fusion.2, bf16[16,2,1024,128]{3,0,2,1:T(8,128)(2,1)S(1)} %fusion.50), kind=kOutput, calls=%fused_computation.12.clone.1 | convolution fusion | flops 2152726528 | bytes 10502144 | tf_op jit(solution)/shard_map/while/body/eval_jaxpr/bda,btak->btdk/dot_general | solution.py:26
  116.9 3.0 copy.54
  119.9 1.4 constant_dynamic-update-slice_fusion.2
  121.4 7.7 %all-to-all-start = ((bf16[16,4,2,256,128]{4,3,2,1,0:T(8,128)(2,1)}), bf16[16,4,2,256,128]{4,3,2,1,0:T(8,128)(2,1)}, u32[]{:S(2)}, u32[]{:S(2)}) async-start(bf16[16,4,2,256,128]{4,3,2,1,0:T(8,128)(2,1)} %bitcast.98), calls=%async_computation | async-start | bytes 16777216 | tf_op jit(solution)/shard_map/all_to_all | solution.py:59
  130.5 194.9 %all_gather.11 = bf16[64,64,64]{2,1,0:T(8,128)(2,1)S(1)} all-gather(bf16[4,64,64]{2,1,0:T(8,128)(2,1)S(1)} %convert_element_type.37), channel_id=1, replica_groups=mesh['groups'=2,'pairs'=16] {'pairs'}, dimensions={0}, use_global_device_ids=true | all-gather | bytes 557056 | tf_op jit(solution)/shard_map/all_gather | solution.py:68
  328.9 4.9 %convert_bitcast_fusion.1 = bf16[16,4,2,128,64]{3,4,2,0,1:T(8,128)(2,1)S(1)} fusion(bf16[16,4,2,256,128]{4,3,2,1,0:T(8,128)(2,1)} %all-to-all-done, bf16[4,256,64]{1,2,0:T(8,128)(2,1)S(1)} %copy-done.3), kind=kOutput, calls=%fused_computation.21 | convolution fusion | flops 537919488 | bytes 10616832 | tf_op jit(solution)/shard_map/sptak,pae->sptke/dot_general | solution.py:60
  334.9 1.7 fusion.28
  (44 shorter events, 6.0 us)
Async XLA Ops:
  0.6 327.2 %copy-start = (bf16[4,8,64,64]{3,2,1,0:T(8,128)(2,1)S(1)}, bf16[4,8,64,64]{3,2,1,0:T(8,128)(2,1)}, u32[]{:S(2)}) copy-start(bf16[4,8,64,64]{3,2,1,0:T(8,128)(2,1)} %param.23) | copy-start | bytes 786436
  0.7 12.1 %copy-start.5 = (s32[4,256]{1,0:T(4,128)S(1)}, s32[4,256]{1,0:T(4,128)}, u32[]{:S(2)}) copy-start(s32[4,256]{1,0:T(4,128)} %param.16) | copy-start | bytes 12292
  0.7 31.6 %copy-start.6 = (s32[4,2]{0,1:T(2,128)S(1)}, s32[4,2]{0,1:T(2,128)}, u32[]{:S(2)}) copy-start(s32[4,2]{0,1:T(2,128)} %param.15) | copy-start | bytes 100
  121.4 7.8 %copy-start.1 = (f32[32]{0:T(128)S(1)}, f32[32]{0:T(128)}, u32[]{:S(2)}) copy-start(f32[32]{0:T(128)} %param.19) | copy-start | bytes 388
  121.4 9.1 %copy-start.2 = (f32[4,64,64]{2,1,0:T(8,128)S(1)}, f32[4,64,64]{2,1,0:T(8,128)}, u32[]{:S(2)}) copy-start(f32[4,64,64]{2,1,0:T(8,128)} %param.20) | copy-start | bytes 196612
  121.4 205.2 %copy-start.9 = (s32[4]{0:T(128)S(1)}, s32[4]{0:T(128)}, u32[]{:S(2)}) copy-start(s32[4]{0:T(128)} %param.17) | copy-start | bytes 52
  121.4 205.3 %copy-start.7 = (f32[4,8]{1,0:T(4,128)S(1)}, f32[4,8]{1,0:T(4,128)}, u32[]{:S(2)}) copy-start(f32[4,8]{1,0:T(4,128)} %param.22) | copy-start | bytes 388
  121.4 205.3 %copy-start.8 = (s32[4,8]{1,0:T(4,128)S(1)}, s32[4,8]{1,0:T(4,128)}, u32[]{:S(2)}) copy-start(s32[4,8]{1,0:T(4,128)} %param.21) | copy-start | bytes 388
  121.4 207.5 %all-to-all-start = ((bf16[16,4,2,256,128]{4,3,2,1,0:T(8,128)(2,1)}), bf16[16,4,2,256,128]{4,3,2,1,0:T(8,128)(2,1)}, u32[]{:S(2)}, u32[]{:S(2)}) async-start(bf16[16,4,2,256,128]{4,3,2,1,0:T(8,128)(2,1)} %bitcast.98), calls=%async_computation | async-start | bytes 16777216 | tf_op jit(solution)/shard_map/all_to_all | solution.py:59
  129.1 199.7 %copy-start.3 = (bf16[4,256,64]{1,2,0:T(8,128)(2,1)S(1)}, bf16[4,256,64]{1,2,0:T(8,128)(2,1)}, u32[]{:S(2)}) copy-start(bf16[4,256,64]{1,2,0:T(8,128)(2,1)} %param.14) | copy-start | bytes 393220
  328.8 6.0 %copy-start.4 = (f32[4,64]{1,0:T(4,128)S(1)}, f32[4,64]{1,0:T(4,128)}, u32[]{:S(2)}) copy-start(f32[4,64]{1,0:T(4,128)} %param.18) | copy-start | bytes 3076
where the time goes:
time: 337 us
  blocking collectives  232 us (69%)
  matrix products  63.1 us (19%)
  local copies, waits for them, and re-layouts  32.8 us (10%)
  starting transfers between devices  7.72 us (2%)
    all_gather x1, blocking collectives, shards(): lax.all_gather(amps.astype(jnp.bfloat16), 'pairs', axis=0, tiled=True)  195 us
    dot_general x4, matrix products, one_block(): jnp.einsum('bda,btak->btdk', dom_hits, slabs, preferred_element_type=jnp....  30.4 us
    dot_general x4, matrix products, one_block(): jnp.einsum('bto,oak->btak', occ_hits, fitted_ints, preferred_element_type...  23 us
    all_gather x1, blocking collectives, shards(): lax.all_gather(pair_dom, 'pairs', axis=0, tiled=True)  19.5 us
    dynamic_update_slice x8, local copies, waits for them, and re-layouts, select_rows(): lax.map(one_block, (occ_list.reshape(-1, block, 2), dom_list.reshape(-1,...  18 us
    all_gather x1, blocking collectives, shards(): lax.all_gather(pair_occ, 'pairs', axis=0, tiled=True)  17.4 us
    unnamed x21, local copies, waits for them, and re-layouts  12.1 us
    all_to_all x1, starting transfers between devices, shards(): lax.all_to_all(sent, 'pairs', split_axis=0, concat_axis=0, tiled=True)  7.72 us
  transfers between devices with their start and end apart: 1, of which 0 were waited for; matrix products, arithmetic and copies ran while one was open for 1% of the time, Pallas kernels for 0%

commit v1 on v0

v1 whole, which is shorter than its diff:
```python
import functools

import jax
import jax.numpy as jnp
from jax import lax
from jax.experimental import pallas as pl
from jax.experimental.pallas import tpu as pltpu
from jax.sharding import PartitionSpec as P

NT = (((1,), (1,)), ((), ()))
VMEM = pl.BlockSpec(memory_space=pltpu.VMEM)
SMEM = pl.BlockSpec(memory_space=pltpu.SMEM)
LIMIT = 24 * 1024 * 1024
ROWS = 16
GROUP = 8


def code(index):
    low = 128 + jnp.bitwise_and(index, 127)
    return lax.shift_left(low, lax.shift_right_logical(index, 7)).astype(jnp.float32).astype(jnp.bfloat16)


def pack_kernel(basis_ref, dom_ref, occ_ref, amps_ref, out_ref):
    per, dom, npno = basis_ref.shape
    for p in range(per):
        out_ref[p * npno : (p + 1) * npno, :] = basis_ref[p].T
    base = per * npno
    out_ref[base : base + npno, :] = jnp.concatenate(
        [amps_ref[p].astype(jnp.bfloat16) for p in range(per)], axis=1
    )
    lane = lax.broadcasted_iota(jnp.int32, (1, dom), 1)
    orbitals = jnp.zeros((1, dom), jnp.int32)
    for p in range(per):
        for t in range(2):
            orbitals = jnp.where(lane == 2 * p + t, occ_ref[p, t], orbitals)
    tail = jnp.concatenate(
        [
            code(dom_ref[...]).astype(jnp.float32),
            orbitals.astype(jnp.float32),
            jnp.zeros((ROWS - per - 1, dom), jnp.float32),
        ],
        axis=0,
    )
    out_ref[base + npno :, :] = tail.astype(jnp.bfloat16)


def exch_kernel(count, per, npno, *refs):
    blocks, fitted_ref, out_ref = refs[:count], refs[count], refs[count + 1]
    held_ref, occ_ref, b_ref, f_ref, sem = refs[count + 2 :]
    npao, width = fitted_ref.shape[1:]
    dom = blocks[0].shape[1]
    base = (per + 1) * npno
    for k in range(count):
        tail = blocks[k][base : base + ROWS, :].astype(jnp.float32)
        held_ref[k : k + 1, :] = tail[per : per + 1, :128].astype(jnp.int32)
    copy = pltpu.make_async_copy(held_ref, occ_ref, sem)
    copy.start()
    codes = code(lax.broadcasted_iota(jnp.int32, (1, npao), 1))
    zero, one = jnp.bfloat16(0), jnp.bfloat16(1)

    def expand(slot, pair):
        k, p = divmod(pair, per)
        row = blocks[k][base + p : base + p + 1, :]
        column = jnp.broadcast_to(row, (128, dom)).T
        hits = jnp.concatenate(
            [jnp.where(column == codes[:, q : q + 128], one, zero) for q in range(0, npao, 128)], axis=1
        )
        b_ref[slot] = jnp.dot(
            blocks[k][p * npno : (p + 1) * npno, :], hits, preferred_element_type=jnp.float32
        ).astype(jnp.bfloat16)

    def fit(slot, pair):
        k, p = divmod(pair, per)
        slabs = jnp.concatenate([fitted_ref[occ_ref[k, 2 * p + t]] for t in range(2)], axis=1)
        f_ref[slot] = jnp.dot(b_ref[slot], slabs, preferred_element_type=jnp.float32).astype(jnp.bfloat16)

    def contract(slot, pair):
        k, p = divmod(pair, per)
        both = f_ref[slot]
        out_ref[k, :, p * npno : (p + 1) * npno] = lax.dot_general(
            both[:, :width], both[:, width:], NT, preferred_element_type=jnp.float32
        )

    pairs = count * per
    for first in range(0, pairs, GROUP):
        group = list(enumerate(range(first, min(first + GROUP, pairs))))
        for slot, pair in group:
            expand(slot, pair)
        if first == 0:
            copy.wait()
        for slot, pair in group:
            fit(slot, pair)
        for slot, pair in group:
            contract(slot, pair)


def coupled_kernel(count, *refs):
    blocks = refs[:count]
    where_ref, weight_ref, inter_ref, occ_ref, count_ref, occ_energy_ref, energy_ref, amps_ref = refs[count : count + 8]
    kept_ref, factor_ref, live_ref, all_ref, half_ref = refs[count + 8 :]
    per, ncpl, npno = inter_ref.shape[:3]
    base = per * npno
    for k in range(count):
        rows = blocks[k][base : base + npno, :]
        for p in range(per):
            all_ref[k * per + p] = rows[:, p * npno : (p + 1) * npno]
    for p in range(per):
        for c in range(ncpl):
            half_ref[p * ncpl + c] = weight_ref[p, c] * jnp.dot(
                inter_ref[p, c], all_ref[where_ref[p, c]], preferred_element_type=jnp.float32
            )
    row = lax.broadcasted_iota(jnp.int32, (npno, npno), 0)
    col = lax.broadcasted_iota(jnp.int32, (npno, npno), 1)
    for p in range(per):
        total = jnp.zeros((npno, npno), jnp.float32)
        for c in range(ncpl):
            half = half_ref[p * ncpl + c]
            high = half.astype(jnp.bfloat16)
            low = (half - high.astype(jnp.float32)).astype(jnp.bfloat16)
            inter = inter_ref[p, c]
            total = total + lax.dot_general(high, inter, NT, preferred_element_type=jnp.float32)
            total = total + lax.dot_general(low, inter, NT, preferred_element_type=jnp.float32)
        here = slice(p * npno, (p + 1) * npno)
        across = jnp.broadcast_to(energy_ref[p : p + 1, :], (npno, npno))
        occ_pair = occ_energy_ref[occ_ref[p, 0]] + occ_energy_ref[occ_ref[p, 1]]
        denom = across.T + across - occ_pair
        live = jnp.where((row < count_ref[p]) & (col < count_ref[p]), jnp.float32(1), jnp.float32(0))
        factor = live / (denom + 0.5)
        amps = amps_ref[p]
        kept_ref[:, here] = live * amps - factor * (denom * amps + total)
        factor_ref[:, here] = factor
        live_ref[:, here] = live


def finish_kernel(own_ref, came_ref, kept_ref, factor_ref, live_ref, new_ref, ints_ref):
    per, npno = new_ref.shape[:2]
    exch = own_ref[...] + came_ref[...]
    new = kept_ref[...] - exch * factor_ref[...]
    ints = exch * live_ref[...]
    for p in range(per):
        new_ref[p] = new[:, p * npno : (p + 1) * npno]
        ints_ref[p] = ints[:, p * npno : (p + 1) * npno]


def shards(
    fitted_ints,
    pno_basis,
    pair_occ,
    pair_dom,
    pno_count,
    pno_energy,
    occ_energy,
    amps,
    cpl_pair,
    cpl_weight,
    intersections,
):
    ndev = lax.axis_size("pairs")
    per, dom, npno = pno_basis.shape
    ncpl = cpl_pair.shape[1]
    npao, width = fitted_ints.shape[1:]
    params = pltpu.CompilerParams(vmem_limit_bytes=LIMIT)
    me = lax.axis_index("pairs")
    steps = [1 << b for b in reversed(range(1, ndev.bit_length() - 1))]

    def swap(array, mask):
        return lax.ppermute(array, "pairs", [(d, d ^ mask) for d in range(ndev)])

    block = pl.pallas_call(
        pack_kernel,
        out_shape=jax.ShapeDtypeStruct(((per + 1) * npno + ROWS, dom), jnp.bfloat16),
        in_specs=[VMEM, VMEM, SMEM, VMEM],
        out_specs=VMEM,
        compiler_params=params,
    )(pno_basis, pair_dom, pair_occ, amps)

    blocks = {0: block}
    for mask in steps:
        for m in sorted(blocks):
            blocks[m ^ mask] = swap(blocks[m], mask)
    for m in sorted(blocks):
        blocks[m ^ 1] = swap(blocks[m], 1)

    def exchange(which):
        count = len(which)
        out = pl.pallas_call(
            functools.partial(exch_kernel, count, per, npno),
            out_shape=jax.ShapeDtypeStruct((count, npno, per * npno), jnp.float32),
            in_specs=[VMEM] * (count + 1),
            out_specs=VMEM,
            scratch_shapes=[
                pltpu.VMEM((8, 128), jnp.int32),
                pltpu.SMEM((8, 128), jnp.int32),
                pltpu.VMEM((GROUP, npno, npao), jnp.bfloat16),
                pltpu.VMEM((GROUP, npno, 2 * width), jnp.bfloat16),
                pltpu.SemaphoreType.DMA,
            ],
            compiler_params=params,
            cost_estimate=pl.CostEstimate(
                flops=2 * count * per * npno * npao * (dom + 2 * width),
                bytes_accessed=8 << 20,
                transcendentals=0,
            ),
        )(*[blocks[m] for m in which], fitted_ints)
        return out

    even = [0]
    for mask in steps:
        even += [m ^ mask for m in even]
    total = {}
    for first in range(0, len(even), 2):
        mine = even[first : first + 2]
        part = exchange(mine + [m ^ 1 for m in mine])
        n = len(mine)
        came = swap(part[n:], 1)
        for k, m in enumerate(mine):
            total[m] = part[k] + came[k]

    where = jnp.bitwise_xor(cpl_pair // per, me) * per + cpl_pair % per
    kept, factor, live = pl.pallas_call(
        functools.partial(coupled_kernel, ndev),
        out_shape=[jax.ShapeDtypeStruct((npno, per * npno), jnp.float32)] * 3,
        in_specs=[VMEM] * ndev + [SMEM, SMEM, VMEM, SMEM, SMEM, SMEM, VMEM, VMEM],
        out_specs=[VMEM] * 3,
        scratch_shapes=[
            pltpu.VMEM((ndev * per, npno, npno), jnp.bfloat16),
            pltpu.VMEM((per * ncpl, npno, npno), jnp.float32),
        ],
        compiler_params=params,
    )(
        *[blocks[m] for m in range(ndev)],
        where,
        cpl_weight,
        intersections,
        pair_occ,
        pno_count,
        occ_energy,
        pno_energy,
        amps,
    )

    came = None
    for mask in reversed(steps):
        send = [m for m in even if m & mask and m in total]
        got = swap(tuple(total[m] for m in send), mask)
        for m, array in zip(send, got):
            if m ^ mask == 0 and mask == steps[0]:
                came = array
            else:
                total[m ^ mask] = total[m ^ mask] + array
            del total[m]

    return pl.pallas_call(
        finish_kernel,
        out_shape=[jax.ShapeDtypeStruct((per, npno, npno), jnp.float32)] * 2,
        in_specs=[VMEM] * 5,
        out_specs=[VMEM] * 2,
        compiler_params=params,
    )(total[0], came, kept, factor, live)


def solution(mesh):
    both = ("groups", "pairs")
    in_specs = (
        P(None, None, both),
        P(both, None, None),
        P(both, None),
        P(both, None),
        P(both),
        P(both, None),
        P("groups"),
        P(both, None, None),
        P(both, None),
        P(both, None),
        P(both, None, None, None),
    )
    out_specs = (P(both, None, None), P(both, None, None))

    def run(*args):
        return tuple(jax.shard_map(shards, mesh=mesh, in_specs=in_specs, out_specs=out_specs, check_vma=False)(*args))

    return run
```

time: 337 us -> 77.4 us (0.23)
  the two profiles are of different devices: /device:TPU:9 before, /device:TPU:0 now
where the time goes in v1:
time: 77.4 us; the launch traced here: 77.1 us
  starting transfers between devices  23.4 us (30%)
  waiting for transfers between devices  20.9 us (27%)
  Pallas kernels  19.8 us (26%)
  local copies, waits for them, and re-layouts  9.09 us (12%)
  other arithmetic  3.09 us (4%)
  between operations  0.84 us (1%)
    ppermute x26, starting transfers between devices, swap(): return lax.ppermute(array, 'pairs', [(d, d ^ mask) for d in range(ndev)])  23.4 us
    ppermute x26, waiting for transfers between devices, swap(): return lax.ppermute(array, 'pairs', [(d, d ^ mask) for d in range(ndev)])  20.9 us
    pallas_call x4, Pallas kernels, exchange(): pl.pallas_call(functools.partial(exch_kernel, count, per, npno), out_shap...  16.5 us
    unnamed x22, local copies, waits for them, and re-layouts  8.39 us
    pallas_call x1, Pallas kernels, shards(): pl.pallas_call(functools.partial(coupled_kernel, ndev), out_shape=[jax.Sh...  1.77 us
    add x2, other arithmetic, shards(): total[m ^ mask] = total[m ^ mask] + array  1.71 us
  transfers between devices with their start and end apart: 26, of which 8 were waited for; matrix products, arithmetic and copies ran while one was open for 4% of the time, Pallas kernels for 24%

profile of v1, /device:TPU:0, one launch (start us, length us, event | category | flops | bytes accessed | tf_op | source)
XLA Modules:
  0.0 77.1 jit_solution(2364216233276611009)
XLA Ops:
  1.4 1.1 %copy.13.basis_ref = bf16[4,256,64]{2,1,0:T(8,128)(2,1)S(1)} copy(bf16[4,256,64]{1,2,0:T(8,128)(2,1)} %param.12) | data formatting | bytes 262144 | tf_op args[1]
  4.8 4.1 %collective-permute-start = (bf16[336,256]{1,0:T(8,128)(2,1)S(1)}, bf16[336,256]{1,0:T(8,128)(2,1)S(1)}, u32[]{:S(2)}, u32[]{:S(2)}) collective-permute-start(bf16[336,256]{1,0:T(8,128)(2,1)S(1)} %shard_map.122.refs_0_), channel_id=1, source_target_pairs={{0,8},{1,9},{2,10},{3,11},{4,12},{5,13},{6,14},{7,15},{8,0},{9,1},... | collective-permute-start | bytes 516104 | tf_op jit(solution)/shard_map/ppermute | solution.py:167
  8.9 1.6 %collective-permute-start.10 = (bf16[336,256]{1,0:T(8,128)(2,1)S(1)}, bf16[336,256]{1,0:T(8,128)(2,1)S(1)}, u32[]{:S(2)}, u32[]{:S(2)}) collective-permute-start(bf16[336,256]{1,0:T(8,128)(2,1)S(1)} %shard_map.122.refs_0_), channel_id=1, source_target_pairs={{0,4},{1,5},{2,6},{3,7},{4,0},{5,1},{6,2},{7,3},{8,12},{9,13},{10,... | collective-permute-start | bytes 516104 | tf_op jit(solution)/shard_map/ppermute | solution.py:167
  10.4 6.6 %collective-permute-done.refs_1_.refs_8_ = bf16[336,256]{1,0:T(8,128)(2,1)S(1)} collective-permute-done((bf16[336,256]{1,0:T(8,128)(2,1)S(1)}, bf16[336,256]{1,0:T(8,128)(2,1)S(1)}, u32[]{:S(2)}, u32[]{:S(2)}) %collective-permute-start) | collective-permute-done | bytes 172064 | tf_op jit(solution)/shard_map/ppermute | solution.py:167
  17.7 1.5 %collective-permute-start.4 = (bf16[336,256]{1,0:T(8,128)(2,1)S(1)}, bf16[336,256]{1,0:T(8,128)(2,1)S(1)}, u32[]{:S(2)}, u32[]{:S(2)}) collective-permute-start(bf16[336,256]{1,0:T(8,128)(2,1)S(1)} %shard_map.122.refs_0_), channel_id=1, source_target_pairs={{0,2},{1,3},{2,0},{3,1},{4,6},{5,7},{6,4},{7,5},{8,10},{9,11},{10,... | collective-permute-start | bytes 516104 | tf_op jit(solution)/shard_map/ppermute | solution.py:167
  19.7 2.8 %collective-permute-done.11.refs_1_.refs_12_ = bf16[336,256]{1,0:T(8,128)(2,1)S(1)} collective-permute-done((bf16[336,256]{1,0:T(8,128)(2,1)S(1)}, bf16[336,256]{1,0:T(8,128)(2,1)S(1)}, u32[]{:S(2)}, u32[]{:S(2)}) %collective-permute-start.11) | collective-permute-done | bytes 172064 | tf_op jit(solution)/shard_map/ppermute | solution.py:167
  22.5 1.5 %collective-permute-start.16 = (bf16[336,256]{1,0:T(8,128)(2,1)S(1)}, bf16[336,256]{1,0:T(8,128)(2,1)S(1)}, u32[]{:S(2)}, u32[]{:S(2)}) collective-permute-start(bf16[336,256]{1,0:T(8,128)(2,1)S(1)} %collective-permute-done.11.refs_1_.refs_12_), channel_id=1, source_target_pairs={{0,2},{1,3},{2,0},{3,1},{4,6},{5,7},{6,4},{7,5},{8,10},{9,11},{10,... | collective-permute-start | bytes 516104 | tf_op jit(solution)/shard_map/ppermute | solution.py:167
  24.9 1.5 %collective-permute-start.5 = (bf16[336,256]{1,0:T(8,128)(2,1)S(1)}, bf16[336,256]{1,0:T(8,128)(2,1)S(1)}, u32[]{:S(2)}, u32[]{:S(2)}) collective-permute-start(bf16[336,256]{1,0:T(8,128)(2,1)S(1)} %collective-permute-done.refs_1_.refs_8_), channel_id=1, source_target_pairs={{0,2},{1,3},{2,0},{3,1},{4,6},{5,7},{6,4},{7,5},{8,10},{9,11},{10,... | collective-permute-start | bytes 516104 | tf_op jit(solution)/shard_map/ppermute | solution.py:167
  26.4 2.2 %collective-permute-done.15.refs_0_.refs_6_ = bf16[336,256]{1,0:T(8,128)(2,1)S(1)} collective-permute-done((bf16[336,256]{1,0:T(8,128)(2,1)S(1)}, bf16[336,256]{1,0:T(8,128)(2,1)S(1)}, u32[]{:S(2)}, u32[]{:S(2)}) %collective-permute-start.15) | collective-permute-done | bytes 172064 | tf_op jit(solution)/shard_map/ppermute | solution.py:167
  28.6 3.7 %collective-permute-done.16.refs_1_.refs_14_ = bf16[336,256]{1,0:T(8,128)(2,1)S(1)} collective-permute-done((bf16[336,256]{1,0:T(8,128)(2,1)S(1)}, bf16[336,256]{1,0:T(8,128)(2,1)S(1)}, u32[]{:S(2)}, u32[]{:S(2)}) %collective-permute-start.16) | collective-permute-done | bytes 172064 | tf_op jit(solution)/shard_map/ppermute | solution.py:167
  32.9 3.4 %copy-done = bf16[32,1024,128]{2,1,0:T(8,128)(2,1)S(1)} copy-done((bf16[32,1024,128]{2,1,0:T(8,128)(2,1)S(1)}, bf16[32,1024,128]{2,1,0:T(8,128)(2,1)}, u32[]{:S(2)}) %copy-start) | copy-done | bytes 8388632
  36.3 4.1 %shard_map.123 = f32[4,64,256]{2,1,0:T(8,128)S(1)} custom-call(bf16[336,256]{1,0:T(8,128)(2,1)S(1)} %shard_map.122.refs_0_, bf16[336,256]{1,0:T(8,128)(2,1)S(1)} %collective-permute-done.refs_1_.refs_8_, bf16[336,256]{1,0:T(8,128)(2,1)S(1)} %collective-permute-done.1.refs_2_.refs_1_, bf16[336,256]{1,0:T(8,128)(2,1)S(1)} %collective-permute-done.2.refs_3_.refs_9_, ...), custom_call_target="tpu_custom_call" | custom-call | flops 1073741824 | bytes 8388608 | tf_op jit(solution)/shard_map/pallas_call | solution.py:186
  42.0 4.1 %shard_map.126 = f32[4,64,256]{2,1,0:T(8,128)S(1)} custom-call(bf16[336,256]{1,0:T(8,128)(2,1)S(1)} %collective-permute-done.15.refs_0_.refs_6_, bf16[336,256]{1,0:T(8,128)(2,1)S(1)} %collective-permute-done.16.refs_1_.refs_14_, bf16[336,256]{1,0:T(8,128)(2,1)S(1)} %collective-permute-done.17.refs_2_.refs_7_, ...), custom_call_target="tpu_custom_call" | custom-call | flops 1073741824 | bytes 8388608 | tf_op jit(solution)/shard_map/pallas_call | solution.py:186
  46.4 4.1 %shard_map.125 = f32[4,64,256]{2,1,0:T(8,128)S(1)} custom-call(bf16[336,256]{1,0:T(8,128)(2,1)S(1)} %collective-permute-done.10.refs_0_.refs_4_, bf16[336,256]{1,0:T(8,128)(2,1)S(1)} %collective-permute-done.11.refs_1_.refs_12_, bf16[336,256]{1,0:T(8,128)(2,1)S(1)} %collective-permute-done.12.refs_2_.refs_5_, ...), custom_call_target="tpu_custom_call" | custom-call | flops 1073741824 | bytes 8388608 | tf_op jit(solution)/shard_map/pallas_call | solution.py:186
  51.1 4.1 %shard_map.124 = f32[4,64,256]{2,1,0:T(8,128)S(1)} custom-call(bf16[336,256]{1,0:T(8,128)(2,1)S(1)} %collective-permute-done.4.refs_0_.refs_2_, bf16[336,256]{1,0:T(8,128)(2,1)S(1)} %collective-permute-done.5.refs_1_.refs_10_, bf16[336,256]{1,0:T(8,128)(2,1)S(1)} %collective-permute-done.6.refs_2_.refs_3_, ...), custom_call_target="tpu_custom_call" | custom-call | flops 1073741824 | bytes 8388608 | tf_op jit(solution)/shard_map/pallas_call | solution.py:186
  55.4 1.6 %collective-permute-start.20 = (f32[64,256]{1,0:T(8,128)S(1)}, f32[64,256]{1,0:T(8,128)S(1)}, u32[]{:S(2)}, u32[]{:S(2)}) collective-permute-start(f32[64,256]{1,0:T(8,128)S(1)} %get-tuple-element.15), channel_id=1, source_target_pairs={{0,2},{1,3},{2,0},{3,1},{4,6},{5,7},{6,4},{7,5},{8,10},{9,11},{10,... | collective-permute-start | bytes 196616 | tf_op jit(solution)/shard_map/ppermute | solution.py:167
  58.1 1.5 %collective-permute-start.22 = (f32[64,256]{1,0:T(8,128)}, f32[64,256]{1,0:T(8,128)}, u32[]{:S(2)}, u32[]{:S(2)}) collective-permute-start(f32[64,256]{1,0:T(8,128)} %get-tuple-element.10), channel_id=1, source_target_pairs={{0,2},{1,3},{2,0},{3,1},{4,6},{5,7},{6,4},{7,5},{8,10},{9,11},{10,... | collective-permute-start | bytes 196616 | tf_op jit(solution)/shard_map/ppermute | solution.py:167
  60.2 1.6 %collective-permute-done.23 = f32[64,256]{1,0:T(8,128)S(1)} collective-permute-done((f32[64,256]{1,0:T(8,128)S(1)}, f32[64,256]{1,0:T(8,128)S(1)}, u32[]{:S(2)}, u32[]{:S(2)}) %collective-permute-start.23) | collective-permute-done | bytes 65568 | tf_op jit(solution)/shard_map/ppermute | solution.py:167
  62.4 1.1 %collective-permute-start.21 = (f32[64,256]{1,0:T(8,128)}, f32[64,256]{1,0:T(8,128)}, u32[]{:S(2)}, u32[]{:S(2)}) collective-permute-start(f32[64,256]{1,0:T(8,128)} %get-tuple-element.13), channel_id=1, source_target_pairs={{0,4},{1,5},{2,6},{3,7},{4,0},{5,1},{6,2},{7,3},{8,12},{9,13},{10,... | collective-permute-start | bytes 196616 | tf_op jit(solution)/shard_map/ppermute | solution.py:167
  64.5 2.5 %collective-permute-done.21 = f32[64,256]{1,0:T(8,128)} collective-permute-done((f32[64,256]{1,0:T(8,128)}, f32[64,256]{1,0:T(8,128)}, u32[]{:S(2)}, u32[]{:S(2)}) %collective-permute-start.21) | collective-permute-done | bytes 65568 | tf_op jit(solution)/shard_map/ppermute | solution.py:167
  67.0 1.1 %collective-permute-done.24 = f32[64,256]{1,0:T(8,128)} collective-permute-done((f32[64,256]{1,0:T(8,128)}, f32[64,256]{1,0:T(8,128)}, u32[]{:S(2)}, u32[]{:S(2)}) %collective-permute-start.24) | collective-permute-done | bytes 65568 | tf_op jit(solution)/shard_map/ppermute | solution.py:167
  68.1 1.0 %fusion.6 = (f32[64,256]{1,0:T(8,128)S(1)}, f32[64,256]{1,0:T(8,128)S(1)}) fusion(f32[64,256]{1,0:T(8,128)} %collective-permute-done.24, f32[64,256]{1,0:T(8,128)} %collective-permute-done.22, f32[2,64,256]{2,1,0:T(8,128)} %collective-permute-done.3, f32[4,64,256]{2,1,0:T(8,128)S(1)} %shard_map.123, f32[64,256]{1,0:T(8,128)} %collective-permute-done.21, ...), kind=kLoop, calls=%fused_computation.10 | loop fusion | flops 98304 | bytes 655360 | tf_op jit(solution)/shard_map/add | solution.py:250
  69.1 3.0 %collective-permute-start.25 = (f32[64,256]{1,0:T(8,128)S(1)}, f32[64,256]{1,0:T(8,128)S(1)}, u32[]{:S(2)}, u32[]{:S(2)}) collective-permute-start(f32[64,256]{1,0:T(8,128)S(1)} %get-tuple-element.8), channel_id=1, source_target_pairs={{0,8},{1,9},{2,10},{3,11},{4,12},{5,13},{6,14},{7,15},{8,0},{9,1},... | collective-permute-start | bytes 196616 | tf_op jit(solution)/shard_map/ppermute | solution.py:167
  74.5 1.8 %shard_map.127 = (f32[64,256]{1,0:T(8,128)S(1)}, f32[64,256]{1,0:T(8,128)S(1)}, f32[64,256]{1,0:T(8,128)S(1)}) custom-call(bf16[336,256]{1,0:T(8,128)(2,1)S(1)} %shard_map.122.refs_0_, bf16[336,256]{1,0:T(8,128)(2,1)S(1)} %collective-permute-done.1.refs_2_.refs_1_, bf16[336,256]{1,0:T(8,128)(2,1)S(1)} %collective-permute-done.4.refs_0_.refs_2_, ...), custom_call_target="tpu_custom_call" | custom-call | tf_op jit(solution)/shard_map/pallas_call | solution.py:220
  (66 shorter events, 14.5 us)
Async XLA Ops:
  4.8 12.3 %collective-permute-start = (bf16[336,256]{1,0:T(8,128)(2,1)S(1)}, bf16[336,256]{1,0:T(8,128)(2,1)S(1)}, u32[]{:S(2)}, u32[]{:S(2)}) collective-permute-start(bf16[336,256]{1,0:T(8,128)(2,1)S(1)} %shard_map.122.refs_0_), channel_id=1, source_target_pairs={{0,8},{1,9},{2,10},{3,11},{4,12},{5,13},{6,14},{7,15},{8,0},{9,1},... | collective-permute-start | bytes 516104 | tf_op jit(solution)/shard_map/ppermute | solution.py:167
  8.9 10.3 %collective-permute-start.10 = (bf16[336,256]{1,0:T(8,128)(2,1)S(1)}, bf16[336,256]{1,0:T(8,128)(2,1)S(1)}, u32[]{:S(2)}, u32[]{:S(2)}) collective-permute-start(bf16[336,256]{1,0:T(8,128)(2,1)S(1)} %shard_map.122.refs_0_), channel_id=1, source_target_pairs={{0,4},{1,5},{2,6},{3,7},{4,0},{5,1},{6,2},{7,3},{8,12},{9,13},{10,... | collective-permute-start | bytes 516104 | tf_op jit(solution)/shard_map/ppermute | solution.py:167
  17.0 5.5 %collective-permute-start.11 = (bf16[336,256]{1,0:T(8,128)(2,1)S(1)}, bf16[336,256]{1,0:T(8,128)(2,1)S(1)}, u32[]{:S(2)}, u32[]{:S(2)}) collective-permute-start(bf16[336,256]{1,0:T(8,128)(2,1)S(1)} %collective-permute-done.refs_1_.refs_8_), channel_id=1, source_target_pairs={{0,4},{1,5},{2,6},{3,7},{4,0},{5,1},{6,2},{7,3},{8,12},{9,13},{10,... | collective-permute-start | bytes 516104 | tf_op jit(solution)/shard_map/ppermute | solution.py:167
  17.7 7.3 %collective-permute-start.4 = (bf16[336,256]{1,0:T(8,128)(2,1)S(1)}, bf16[336,256]{1,0:T(8,128)(2,1)S(1)}, u32[]{:S(2)}, u32[]{:S(2)}) collective-permute-start(bf16[336,256]{1,0:T(8,128)(2,1)S(1)} %shard_map.122.refs_0_), channel_id=1, source_target_pairs={{0,2},{1,3},{2,0},{3,1},{4,6},{5,7},{6,4},{7,5},{8,10},{9,11},{10,... | collective-permute-start | bytes 516104 | tf_op jit(solution)/shard_map/ppermute | solution.py:167
  19.2 9.4 %collective-permute-start.15 = (bf16[336,256]{1,0:T(8,128)(2,1)S(1)}, bf16[336,256]{1,0:T(8,128)(2,1)S(1)}, u32[]{:S(2)}, u32[]{:S(2)}) collective-permute-start(bf16[336,256]{1,0:T(8,128)(2,1)S(1)} %collective-permute-done.10.refs_0_.refs_4_), channel_id=1, source_target_pairs={{0,2},{1,3},{2,0},{3,1},{4,6},{5,7},{6,4},{7,5},{8,10},{9,11},{10,... | collective-permute-start | bytes 516104 | tf_op jit(solution)/shard_map/ppermute | solution.py:167
  22.5 9.8 %collective-permute-start.16 = (bf16[336,256]{1,0:T(8,128)(2,1)S(1)}, bf16[336,256]{1,0:T(8,128)(2,1)S(1)}, u32[]{:S(2)}, u32[]{:S(2)}) collective-permute-start(bf16[336,256]{1,0:T(8,128)(2,1)S(1)} %collective-permute-done.11.refs_1_.refs_12_), channel_id=1, source_target_pairs={{0,2},{1,3},{2,0},{3,1},{4,6},{5,7},{6,4},{7,5},{8,10},{9,11},{10,... | collective-permute-start | bytes 516104 | tf_op jit(solution)/shard_map/ppermute | solution.py:167
  24.0 8.3 %collective-permute-start.1 = (bf16[336,256]{1,0:T(8,128)(2,1)S(1)}, bf16[336,256]{1,0:T(8,128)(2,1)S(1)}, u32[]{:S(2)}, u32[]{:S(2)}) collective-permute-start(bf16[336,256]{1,0:T(8,128)(2,1)S(1)} %shard_map.122.refs_0_), channel_id=1, source_target_pairs={{0,1},{1,0},{2,3},{3,2},{4,5},{5,4},{6,7},{7,6},{8,9},{9,8},{10,11... | collective-permute-start | bytes 516104 | tf_op jit(solution)/shard_map/ppermute | solution.py:167
  24.0 8.8 %collective-permute-start.2 = (bf16[336,256]{1,0:T(8,128)(2,1)S(1)}, bf16[336,256]{1,0:T(8,128)(2,1)S(1)}, u32[]{:S(2)}, u32[]{:S(2)}) collective-permute-start(bf16[336,256]{1,0:T(8,128)(2,1)S(1)} %collective-permute-done.refs_1_.refs_8_), channel_id=1, source_target_pairs={{0,1},{1,0},{2,3},{3,2},{4,5},{5,4},{6,7},{7,6},{8,9},{9,8},{10,11... | collective-permute-start | bytes 516104 | tf_op jit(solution)/shard_map/ppermute | solution.py:167
  24.9 16.2 %collective-permute-start.5 = (bf16[336,256]{1,0:T(8,128)(2,1)S(1)}, bf16[336,256]{1,0:T(8,128)(2,1)S(1)}, u32[]{:S(2)}, u32[]{:S(2)}) collective-permute-start(bf16[336,256]{1,0:T(8,128)(2,1)S(1)} %collective-permute-done.refs_1_.refs_8_), channel_id=1, source_target_pairs={{0,2},{1,3},{2,0},{3,1},{4,6},{5,7},{6,4},{7,5},{8,10},{9,11},{10,... | collective-permute-start | bytes 516104 | tf_op jit(solution)/shard_map/ppermute | solution.py:167
  28.6 12.9 %collective-permute-start.17 = (bf16[336,256]{1,0:T(8,128)(2,1)S(1)}, bf16[336,256]{1,0:T(8,128)(2,1)S(1)}, u32[]{:S(2)}, u32[]{:S(2)}) collective-permute-start(bf16[336,256]{1,0:T(8,128)(2,1)S(1)} %collective-permute-done.15.refs_0_.refs_6_), channel_id=1, source_target_pairs={{0,1},{1,0},{2,3},{3,2},{4,5},{5,4},{6,7},{7,6},{8,9},{9,8},{10,11... | collective-permute-start | bytes 516104 | tf_op jit(solution)/shard_map/ppermute | solution.py:167
  32.3 9.3 %collective-permute-start.18 = (bf16[336,256]{1,0:T(8,128)(2,1)S(1)}, bf16[336,256]{1,0:T(8,128)(2,1)S(1)}, u32[]{:S(2)}, u32[]{:S(2)}) collective-permute-start(bf16[336,256]{1,0:T(8,128)(2,1)S(1)} %collective-permute-done.16.refs_1_.refs_14_), channel_id=1, source_target_pairs={{0,1},{1,0},{2,3},{3,2},{4,5},{5,4},{6,7},{7,6},{8,9},{9,8},{10,11... | collective-permute-start | bytes 516104 | tf_op jit(solution)/shard_map/ppermute | solution.py:167
  32.3 13.9 %collective-permute-start.12 = (bf16[336,256]{1,0:T(8,128)(2,1)S(1)}, bf16[336,256]{1,0:T(8,128)(2,1)S(1)}, u32[]{:S(2)}, u32[]{:S(2)}) collective-permute-start(bf16[336,256]{1,0:T(8,128)(2,1)S(1)} %collective-permute-done.10.refs_0_.refs_4_), channel_id=1, source_target_pairs={{0,1},{1,0},{2,3},{3,2},{4,5},{5,4},{6,7},{7,6},{8,9},{9,8},{10,11... | collective-permute-start | bytes 516104 | tf_op jit(solution)/shard_map/ppermute | solution.py:167
  32.8 13.6 %collective-permute-start.13 = (bf16[336,256]{1,0:T(8,128)(2,1)S(1)}, bf16[336,256]{1,0:T(8,128)(2,1)S(1)}, u32[]{:S(2)}, u32[]{:S(2)}) collective-permute-start(bf16[336,256]{1,0:T(8,128)(2,1)S(1)} %collective-permute-done.11.refs_1_.refs_12_), channel_id=1, source_target_pairs={{0,1},{1,0},{2,3},{3,2},{4,5},{5,4},{6,7},{7,6},{8,9},{9,8},{10,11... | collective-permute-start | bytes 516104 | tf_op jit(solution)/shard_map/ppermute | solution.py:167
  41.1 10.0 %collective-permute-start.6 = (bf16[336,256]{1,0:T(8,128)(2,1)S(1)}, bf16[336,256]{1,0:T(8,128)(2,1)S(1)}, u32[]{:S(2)}, u32[]{:S(2)}) collective-permute-start(bf16[336,256]{1,0:T(8,128)(2,1)S(1)} %collective-permute-done.4.refs_0_.refs_2_), channel_id=1, source_target_pairs={{0,1},{1,0},{2,3},{3,2},{4,5},{5,4},{6,7},{7,6},{8,9},{9,8},{10,11... | collective-permute-start | bytes 516104 | tf_op jit(solution)/shard_map/ppermute | solution.py:167
  41.5 22.9 %collective-permute-start.3 = (f32[2,64,256]{2,1,0:T(8,128)}, f32[2,64,256]{2,1,0:T(8,128)}, u32[]{:S(2)}, u32[]{:S(2)}) collective-permute-start(f32[2,64,256]{2,1,0:T(8,128)} %slice.81), channel_id=1, source_target_pairs={{0,1},{1,0},{2,3},{3,2},{4,5},{5,4},{6,7},{7,6},{8,9},{9,8},{10,11... | collective-permute-start | bytes 393224 | tf_op jit(solution)/shard_map/ppermute | solution.py:167
  41.6 9.5 %collective-permute-start.7 = (bf16[336,256]{1,0:T(8,128)(2,1)S(1)}, bf16[336,256]{1,0:T(8,128)(2,1)S(1)}, u32[]{:S(2)}, u32[]{:S(2)}) collective-permute-start(bf16[336,256]{1,0:T(8,128)(2,1)S(1)} %collective-permute-done.5.refs_1_.refs_10_), channel_id=1, source_target_pairs={{0,1},{1,0},{2,3},{3,2},{4,5},{5,4},{6,7},{7,6},{8,9},{9,8},{10,11... | collective-permute-start | bytes 516104 | tf_op jit(solution)/shard_map/ppermute | solution.py:167
  46.3 9.1 %collective-permute-start.19 = (f32[2,64,256]{2,1,0:T(8,128)S(1)}, f32[2,64,256]{2,1,0:T(8,128)S(1)}, u32[]{:S(2)}, u32[]{:S(2)}) collective-permute-start(f32[2,64,256]{2,1,0:T(8,128)S(1)} %slice.90), channel_id=1, source_target_pairs={{0,1},{1,0},{2,3},{3,2},{4,5},{5,4},{6,7},{7,6},{8,9},{9,8},{10,11... | collective-permute-start | bytes 393224 | tf_op jit(solution)/shard_map/ppermute | solution.py:167
  50.6 9.1 %collective-permute-start.14 = (f32[2,64,256]{2,1,0:T(8,128)S(1)}, f32[2,64,256]{2,1,0:T(8,128)S(1)}, u32[]{:S(2)}, u32[]{:S(2)}) collective-permute-start(f32[2,64,256]{2,1,0:T(8,128)S(1)} %slice.87), channel_id=1, source_target_pairs={{0,1},{1,0},{2,3},{3,2},{4,5},{5,4},{6,7},{7,6},{8,9},{9,8},{10,11... | collective-permute-start | bytes 393224 | tf_op jit(solution)/shard_map/ppermute | solution.py:167
  55.4 4.8 %collective-permute-start.20 = (f32[64,256]{1,0:T(8,128)S(1)}, f32[64,256]{1,0:T(8,128)S(1)}, u32[]{:S(2)}, u32[]{:S(2)}) collective-permute-start(f32[64,256]{1,0:T(8,128)S(1)} %get-tuple-element.15), channel_id=1, source_target_pairs={{0,2},{1,3},{2,0},{3,1},{4,6},{5,7},{6,4},{7,5},{8,10},{9,11},{10,... | collective-permute-start | bytes 196616 | tf_op jit(solution)/shard_map/ppermute | solution.py:167
  57.0 4.8 %collective-permute-start.23 = (f32[64,256]{1,0:T(8,128)S(1)}, f32[64,256]{1,0:T(8,128)S(1)}, u32[]{:S(2)}, u32[]{:S(2)}) collective-permute-start(f32[64,256]{1,0:T(8,128)S(1)} %get-tuple-element.14), channel_id=1, source_target_pairs={{0,2},{1,3},{2,0},{3,1},{4,6},{5,7},{6,4},{7,5},{8,10},{9,11},{10,... | collective-permute-start | bytes 196616 | tf_op jit(solution)/shard_map/ppermute | solution.py:167
  58.1 6.3 %collective-permute-start.22 = (f32[64,256]{1,0:T(8,128)}, f32[64,256]{1,0:T(8,128)}, u32[]{:S(2)}, u32[]{:S(2)}) collective-permute-start(f32[64,256]{1,0:T(8,128)} %get-tuple-element.10), channel_id=1, source_target_pairs={{0,2},{1,3},{2,0},{3,1},{4,6},{5,7},{6,4},{7,5},{8,10},{9,11},{10,... | collective-permute-start | bytes 196616 | tf_op jit(solution)/shard_map/ppermute | solution.py:167
  59.7 4.8 %collective-permute-start.9 = (f32[64,256]{1,0:T(8,128)}, f32[64,256]{1,0:T(8,128)}, u32[]{:S(2)}, u32[]{:S(2)}) collective-permute-start(f32[64,256]{1,0:T(8,128)} %get-tuple-element.11), channel_id=1, source_target_pairs={{0,2},{1,3},{2,0},{3,1},{4,6},{5,7},{6,4},{7,5},{8,10},{9,11},{10,... | collective-permute-start | bytes 196616 | tf_op jit(solution)/shard_map/ppermute | solution.py:167
  62.4 4.6 %collective-permute-start.21 = (f32[64,256]{1,0:T(8,128)}, f32[64,256]{1,0:T(8,128)}, u32[]{:S(2)}, u32[]{:S(2)}) collective-permute-start(f32[64,256]{1,0:T(8,128)} %get-tuple-element.13), channel_id=1, source_target_pairs={{0,4},{1,5},{2,6},{3,7},{4,0},{5,1},{6,2},{7,3},{8,12},{9,13},{10,... | collective-permute-start | bytes 196616 | tf_op jit(solution)/shard_map/ppermute | solution.py:167
  69.1 7.1 %collective-permute-start.25 = (f32[64,256]{1,0:T(8,128)S(1)}, f32[64,256]{1,0:T(8,128)S(1)}, u32[]{:S(2)}, u32[]{:S(2)}) collective-permute-start(f32[64,256]{1,0:T(8,128)S(1)} %get-tuple-element.8), channel_id=1, source_target_pairs={{0,8},{1,9},{2,10},{3,11},{4,12},{5,13},{6,14},{7,15},{8,0},{9,1},... | collective-permute-start | bytes 196616 | tf_op jit(solution)/shard_map/ppermute | solution.py:167
  (12 other events, 125.8 us)

commit v2 on v1

v2 whole, which is shorter than its diff:
```python
import functools

import jax
import jax.numpy as jnp
from jax import lax
from jax.experimental import pallas as pl
from jax.experimental.pallas import tpu as pltpu
from jax.sharding import PartitionSpec as P

NT = (((1,), (1,)), ((), ()))
VMEM = pl.BlockSpec(memory_space=pltpu.VMEM)
HBM = pl.BlockSpec(memory_space=pltpu.HBM)
SMEM = pl.BlockSpec(memory_space=pltpu.SMEM)
SENT = jnp.bfloat16
LIMIT = 16 << 20
ROWS = 16
CALL = 2
COST = 300_000_000
GROUP = 16


def code(index):
    low = 128 + jnp.bitwise_and(index, 127)
    return lax.shift_left(low, lax.shift_right_logical(index, 7)).astype(jnp.float32).astype(jnp.bfloat16)


def pack_kernel(basis_ref, dom_ref, occ_ref, amps_ref, out_ref, again_ref, dom_in, occ_in, amps_in, sems):
    per, npno, dom = basis_ref.shape
    base = per * npno
    copies = [
        pltpu.make_async_copy(amps_ref, amps_in, sems.at[0]),
        pltpu.make_async_copy(dom_ref, dom_in, sems.at[1]),
        pltpu.make_async_copy(occ_ref, occ_in, sems.at[2]),
    ]
    for p in range(per):
        for k, ref in enumerate((out_ref, again_ref)):
            rows = ref.at[pl.ds(p * npno, npno)]
            copies.append(pltpu.make_async_copy(basis_ref.at[p], rows, sems.at[3 + 2 * p + k]))
    for copy in copies:
        copy.start()
    for copy in copies:
        copy.wait()
    lane = lax.broadcasted_iota(jnp.int32, (1, dom), 1)
    orbitals = jnp.zeros((1, dom), jnp.int32)
    for p in range(per):
        for t in range(2):
            orbitals = jnp.where(lane == 2 * p + t, occ_in[t, p], orbitals)
    tail = jnp.concatenate(
        [
            code(dom_in[...]).astype(jnp.float32),
            orbitals.astype(jnp.float32),
            jnp.zeros((ROWS - per - 1, dom), jnp.float32),
        ],
        axis=0,
    )
    for ref in (out_ref, again_ref):
        ref[base : base + npno, :] = jnp.concatenate(
            [amps_in[p].astype(jnp.bfloat16) for p in range(per)], axis=1
        )
        ref[base + npno :, :] = tail.astype(jnp.bfloat16)


def read_orbitals(blocks, per, npno, held_ref, occ_ref, sem):
    base = (per + 1) * npno
    for k, block in enumerate(blocks):
        tail = block[base : base + ROWS, :].astype(jnp.float32)
        held_ref[k : k + 1, :] = tail[per : per + 1, :128].astype(jnp.int32)
    return pltpu.make_async_copy(held_ref, occ_ref, sem)


def contract(both, width):
    return lax.dot_general(both[:, :width], both[:, width:], NT, preferred_element_type=jnp.float32)


def expand(block, p, codes, out_ref, at):
    npno, dom = out_ref.shape[1], block.shape[1]
    base = block.shape[0] - ROWS + p
    column = jnp.broadcast_to(block[base : base + 1, :], (128, dom)).T
    zero, one = jnp.bfloat16(0), jnp.bfloat16(1)
    hits = jnp.concatenate(
        [jnp.where(column == codes[:, q : q + 128], one, zero) for q in range(0, codes.shape[1], 128)], axis=1
    )
    out_ref[at] = jnp.dot(
        block[p * npno : (p + 1) * npno, :], hits, preferred_element_type=jnp.float32
    ).astype(jnp.bfloat16)


def fit(wide, fitted_ref, orbitals, f_ref, at):
    slabs = jnp.concatenate([fitted_ref[o] for o in orbitals], axis=1)
    f_ref[at] = jnp.dot(wide, slabs, preferred_element_type=jnp.float32).astype(jnp.bfloat16)


def batches(count):
    return [range(first, min(first + GROUP, count)) for first in range(0, count, GROUP)]


def exch_kernel(count, per, npno, *refs):
    blocks, fitted_ref = refs[:count], refs[count]
    outs, (held_ref, occ_ref, wide_ref, f_ref, sem) = refs[-7:-5], refs[-5:]
    npao, width = fitted_ref.shape[1:]
    orbitals = read_orbitals(blocks, per, npno, held_ref, occ_ref, sem)
    orbitals.start()
    codes = code(lax.broadcasted_iota(jnp.int32, (1, npao), 1))
    for group in batches(count * per):
        for at, pair in enumerate(group):
            k, p = divmod(pair, per)
            expand(blocks[k], p, codes, wide_ref, at)
        if group[0] == 0:
            orbitals.wait()
        for at, pair in enumerate(group):
            k, p = divmod(pair, per)
            fit(wide_ref[at], fitted_ref, [occ_ref[k, 2 * p + t] for t in range(2)], f_ref, at)
        for at, pair in enumerate(group):
            k, p = divmod(pair, per)
            half, k = divmod(k, count // 2)
            outs[half][k, :, p * npno : (p + 1) * npno] = contract(f_ref[at], width)


def gate_kernel(*refs):
    pass


def sum_kernel(plan, *refs):
    outs = refs[len(refs) - len(plan) :]
    for out_ref, terms in zip(outs, plan):
        for k, (first, *others) in enumerate(terms):
            total = refs[first[0]][first[1]].astype(jnp.float32)
            for ref, at in others:
                total = total + refs[ref][at].astype(jnp.float32)
            out_ref[k] = total.astype(out_ref.dtype)


def coupled_kernel(count, *refs):
    blocks, refs = refs[:count], refs[count:]
    where_ref, weight_ref, inter_ref, occ_ref, count_ref, occ_energy_ref, energy_ref, amps_ref = refs[:8]
    kept_ref, factor_ref, live_ref, all_ref, half_ref = refs[8:]
    per, ncpl, npno = inter_ref.shape[:3]
    for k in range(count):
        rows = blocks[k][per * npno : (per + 1) * npno, :]
        for p in range(per):
            all_ref[k * per + p] = rows[:, p * npno : (p + 1) * npno]
    for p in range(per):
        for c in range(ncpl):
            half_ref[p * ncpl + c] = weight_ref[p, c] * jnp.dot(
                inter_ref[p, c], all_ref[where_ref[p, c]], preferred_element_type=jnp.float32
            )
    row = lax.broadcasted_iota(jnp.int32, (npno, npno), 0)
    col = lax.broadcasted_iota(jnp.int32, (npno, npno), 1)
    for p in range(per):
        total = jnp.zeros((npno, npno), jnp.float32)
        for c in range(ncpl):
            half = half_ref[p * ncpl + c]
            high = half.astype(jnp.bfloat16)
            low = (half - high.astype(jnp.float32)).astype(jnp.bfloat16)
            inter = inter_ref[p, c]
            total = total + lax.dot_general(high, inter, NT, preferred_element_type=jnp.float32)
            total = total + lax.dot_general(low, inter, NT, preferred_element_type=jnp.float32)
        here = slice(p * npno, (p + 1) * npno)
        across = jnp.broadcast_to(energy_ref[p : p + 1, :], (npno, npno))
        occ_pair = occ_energy_ref[occ_ref[0, p]] + occ_energy_ref[occ_ref[1, p]]
        denom = across.T + across - occ_pair
        live = jnp.where((row < count_ref[p]) & (col < count_ref[p]), jnp.float32(1), jnp.float32(0))
        factor = live / (denom + 0.5)
        amps = amps_ref[p]
        kept_ref[:, here] = live * amps - factor * (denom * amps + total)
        factor_ref[:, here] = factor
        live_ref[:, here] = live


def finish_kernel(own_ref, came_ref, kept_ref, factor_ref, live_ref, new_ref, ints_ref):
    per, npno = new_ref.shape[:2]
    exch = own_ref[0] + came_ref[0].astype(jnp.float32)
    new = kept_ref[...] - exch * factor_ref[...]
    ints = exch * live_ref[...]
    for p in range(per):
        new_ref[p] = new[:, p * npno : (p + 1) * npno]
        ints_ref[p] = ints[:, p * npno : (p + 1) * npno]


def shards(
    fitted_ints,
    pno_basis,
    pair_occ,
    pair_dom,
    pno_count,
    pno_energy,
    occ_energy,
    amps,
    cpl_pair,
    cpl_weight,
    intersections,
):
    ndev = lax.axis_size("pairs")
    per, dom, npno = pno_basis.shape
    ncpl = cpl_pair.shape[1]
    npao, width = fitted_ints.shape[1:]
    params = pltpu.CompilerParams(vmem_limit_bytes=LIMIT)
    me = lax.axis_index("pairs")
    steps = [1 << b for b in reversed(range(1, ndev.bit_length() - 1))]

    def swap(array, mask):
        return lax.ppermute(array, "pairs", [(d, d ^ mask) for d in range(ndev)])

    first_block, block = pl.pallas_call(
        pack_kernel,
        out_shape=[jax.ShapeDtypeStruct(((per + 1) * npno + ROWS, dom), jnp.bfloat16)] * 2,
        in_specs=[HBM] * 4,
        out_specs=[VMEM] * 2,
        scratch_shapes=[
            pltpu.VMEM((per, dom), jnp.int32),
            pltpu.SMEM((2, per), jnp.int32),
            pltpu.VMEM((per, npno, npno), jnp.float32),
            pltpu.SemaphoreType.DMA((3 + 2 * per,)),
        ],
        compiler_params=pltpu.CompilerParams(vmem_limit_bytes=62 << 20),
    )(jnp.swapaxes(pno_basis, 1, 2), pair_dom, pair_occ.T, amps)

    def estimate(flops):
        return pl.CostEstimate(flops=flops, bytes_accessed=1 << 20, transcendentals=0)

    def gate(array, after=(), flops=0, held=False):
        return pl.pallas_call(
            gate_kernel,
            out_shape=jax.ShapeDtypeStruct(array.shape, array.dtype),
            in_specs=[HBM] * (1 + len(after)) + [VMEM] * held,
            out_specs=HBM,
            input_output_aliases={0: 0},
            compiler_params=params,
            cost_estimate=estimate(flops),
        )(array, *after, *[fitted_ints] * held)

    mine, came, chain, back = {}, {}, [], []

    def exchange(which, cost=COST):
        count = 2 * len(which)
        after = chain[-1:] + back[:-1][-1:]
        out = pl.pallas_call(
            functools.partial(exch_kernel, count, per, npno),
            out_shape=[jax.ShapeDtypeStruct((len(which), npno, per * npno), jnp.float32)] * 2,
            in_specs=[VMEM] * (count + 1) + [HBM] * len(after),
            out_specs=[VMEM] * 2,
            scratch_shapes=[
                pltpu.VMEM((8, 128), jnp.int32),
                pltpu.SMEM((8, 128), jnp.int32),
                pltpu.VMEM((GROUP, npno, npao), jnp.bfloat16),
                pltpu.VMEM((GROUP, npno, 2 * width), jnp.bfloat16),
                pltpu.SemaphoreType.DMA,
            ],
            compiler_params=params,
            cost_estimate=estimate(cost * count * per),
        )(*[blocks[m] for m in which], *[blocks[m ^ 1] for m in which], fitted_ints, *after)
        chain.append(out[0])
        got = swap(out[1], 1)
        back.append(got)
        for k, m in enumerate(which):
            mine[m], came[m] = (out[0], k), (got, k)

    def add_up(plan, dtypes, after=()):
        arrays = []
        for terms in plan:
            for term in terms:
                for array, _ in term:
                    if not any(array is a for a in arrays):
                        arrays.append(array)
        number = lambda array: [array is a for a in arrays].index(True)
        return pl.pallas_call(
            functools.partial(
                sum_kernel, [[[(number(array), at) for array, at in term] for term in terms] for terms in plan]
            ),
            out_shape=[
                jax.ShapeDtypeStruct((len(terms), npno, per * npno), dtype) for terms, dtype in zip(plan, dtypes)
            ],
            in_specs=[VMEM] * len(arrays) + [HBM] * len(after),
            out_specs=[VMEM] * len(plan),
            compiler_params=params,
        )(*arrays, *after)

    top, rest, last = steps[0], steps[1:], steps[-1]
    blocks = {top: swap(first_block, top)}
    block = blocks[0] = gate(block, (), 32 * COST)
    for mask in rest + [1]:
        blocks[mask] = swap(block, mask)
    exchange([0])
    for m in rest:
        blocks[m ^ 1] = swap(blocks[m], 1)
    exchange(rest[::-1])
    for m in rest[:-1]:
        blocks[m ^ last] = swap(blocks[m], last)
        blocks[m ^ last ^ 1] = swap(blocks[m ^ last], 1)
    blocks[top] = gate(blocks[top], chain[-1:], held=True)
    for mask in (rest[0], last):
        blocks[top ^ mask] = swap(blocks[top], mask)
    blocks[top ^ 1] = swap(blocks[top], 1)
    exchange([rest[0] ^ last, top])
    blocks[top ^ rest[0]] = gate(blocks[top ^ rest[0]], chain[-1:], held=True)
    even = [0, top]
    for mask in rest:
        for m in list(even):
            if m ^ mask not in blocks:
                blocks[m ^ mask] = swap(blocks[m], mask)
            even.append(m ^ mask)
    own = [0]
    for mask in steps[:-1]:
        own += [m ^ mask for m in own]
    far = [m ^ last for m in own]
    left = [m for m in far[:-1] + own if m not in mine]
    for m in left:
        if m ^ 1 not in blocks:
            blocks[m ^ 1] = swap(blocks[m], 1)
    for first in range(0, len(left), CALL):
        exchange(left[first : first + CALL])
    blocks[far[-1]] = gate(blocks[far[-1]], chain[-1:], 32 * COST)
    blocks[far[-1] ^ 1] = swap(blocks[far[-1]], 1)
    exchange(far[-1:])

    ready = add_up([[[mine[m], came[m]] for m in far[:-1]]], [SENT])[0]
    final = add_up([[[mine[m], came[m]] for m in far[-1:]]], [SENT])[0]
    terms = [[mine[m], came[m]] for m in own]
    ready, final = swap(ready, last), swap(final, last)
    for k, term in enumerate(terms):
        term.append((ready, k) if k < len(own) - 1 else (final, 0))

    away = jnp.bitwise_xor(cpl_pair // per, me)
    where = away * per + cpl_pair % per
    kept, factor, live = pl.pallas_call(
        functools.partial(coupled_kernel, ndev),
        out_shape=[jax.ShapeDtypeStruct((npno, per * npno), jnp.float32)] * 3,
        in_specs=[VMEM] * ndev + [SMEM, SMEM, VMEM, SMEM, SMEM, SMEM, VMEM, VMEM],
        out_specs=[VMEM] * 3,
        scratch_shapes=[
            pltpu.VMEM((ndev * per, npno, npno), jnp.bfloat16),
            pltpu.VMEM((per * ncpl, npno, npno), jnp.float32),
        ],
        compiler_params=params,
        cost_estimate=estimate(8 * COST),
    )(
        *[blocks[m] for m in range(ndev)],
        where,
        cpl_weight,
        intersections,
        pair_occ.T,
        pno_count,
        occ_energy,
        pno_energy,
        amps,
    )

    for mask in reversed(steps[:-1]):
        half = len(terms) // 2
        keep, send = add_up([terms[:half], terms[half:]], [jnp.float32, SENT], [kept] if mask == steps[-2] else [])
        send = swap(send, mask)
        terms = [[(keep, k), (send, k)] for k in range(half)]

    return pl.pallas_call(
        finish_kernel,
        out_shape=[jax.ShapeDtypeStruct((per, npno, npno), jnp.float32)] * 2,
        in_specs=[VMEM] * 5,
        out_specs=[VMEM] * 2,
        compiler_params=params,
    )(keep, send, kept, factor, live)


def solution(mesh):
    both = ("groups", "pairs")
    in_specs = (
        P(None, None, both),
        P(both, None, None),
        P(both, None),
        P(both, None),
        P(both),
        P(both, None),
        P("groups"),
        P(both, None, None),
        P(both, None),
        P(both, None),
        P(both, None, None, None),
    )
    out_specs = (P(both, None, None), P(both, None, None))

    def run(*args):
        return tuple(jax.shard_map(shards, mesh=mesh, in_specs=in_specs, out_specs=out_specs, check_vma=False)(*args))

    return run
```

time: 77.4 us -> 60.1 us (0.78)
  waiting for transfers between devices: 20.9 us -> 11.3 us
  local copies, waits for them, and re-layouts: 9.09 us -> 4.38 us
  other arithmetic: 3.09 us -> 0.01 us
  Pallas kernels: 19.8 us -> 22.2 us
  starting transfers between devices: 23.4 us -> 21 us
    ppermute x26 -> x24, waiting for transfers between devices: 20.9 us -> 11.3 us  [swap(): return lax.ppermute(array, 'pairs', [(d, d ^ mask) for d in range(ndev)])]
    unnamed x22 -> x42, local copies, waits for them, and re-layouts: 8.39 us -> 4.38 us
    add x5 -> x1, other arithmetic: 3.09 us -> 0.01 us  [shards(): where = away * per + cpl_pair % per]
    ppermute x26 -> x24, starting transfers between devices: 23.4 us -> 21 us  [swap(): return lax.ppermute(array, 'pairs', [(d, d ^ mask) for d in range(ndev)])]
    pallas_call x1 -> x9, Pallas kernels: 0.69 us -> 1.97 us  [the longest x1 1.85 us: shards(): pl.pallas_call(pack_kernel, out_shape=[jax.ShapeDtypeStruct(((per + 1) *...]
    pallas_call x4 -> x5, Pallas kernels: 16.5 us -> 17.7 us  [exchange(): pl.pallas_call(functools.partial(exch_kernel, count, per, npno), out_shap...]
  transfers between devices with their start and end apart: 26 -> 24, of which waited for: 8 -> 9; matrix products, arithmetic and copies ran while one was open for 4% -> 0% of each run, Pallas kernels for 24% -> 33%
where the time goes in v2:
time: 60.1 us; the launch traced here: 59.9 us
  Pallas kernels  22.2 us (37%)
  starting transfers between devices  21 us (35%)
  waiting for transfers between devices  11.3 us (19%)
  local copies, waits for them, and re-layouts  4.38 us (7%)
  between operations  0.97 us (2%)
    ppermute x24, starting transfers between devices, swap(): return lax.ppermute(array, 'pairs', [(d, d ^ mask) for d in range(ndev)])  21 us
    pallas_call x5, Pallas kernels, exchange(): pl.pallas_call(functools.partial(exch_kernel, count, per, npno), out_shap...  17.7 us
    ppermute x24, waiting for transfers between devices, swap(): return lax.ppermute(array, 'pairs', [(d, d ^ mask) for d in range(ndev)])  11.3 us
    unnamed x42, local copies, waits for them, and re-layouts  4.38 us
    pallas_call x1, Pallas kernels, shards(): pl.pallas_call(pack_kernel, out_shape=[jax.ShapeDtypeStruct(((per + 1) *...  1.85 us
    pallas_call x1, Pallas kernels, shards(): pl.pallas_call(functools.partial(coupled_kernel, ndev), out_shape=[jax.Sh...  1.77 us
  transfers between devices with their start and end apart: 24, of which 9 were waited for; matrix products, arithmetic and copies ran while one was open for 0% of the time, Pallas kernels for 33%

profile of v2, /device:TPU:0, one launch (start us, length us, event | category | flops | bytes accessed | tf_op | source)
XLA Modules:
  0.0 59.9 jit_solution(536353588994197635)
XLA Ops:
  0.6 1.9 %shard_map.122 = (bf16[336,256]{1,0:T(8,128)(2,1)}, bf16[336,256]{1,0:T(8,128)(2,1)}) custom-call(bf16[4,64,256]{2,1,0:T(8,128)(2,1)} %bitcast.4, s32[4,256]{1,0:T(4,128)} %dom_ref.1, s32[2,4]{1,0:T(2,128)} %bitcast.2, f32[4,64,64]{2,1,0:T(8,128)} %refs_23_.1), custom_call_target="tpu_custom_call" | custom-call | tf_op jit(solution)/shard_map/pallas_call | solution.py:204
  2.5 0.9 %copy-done.11 = bf16[336,256]{1,0:T(8,128)(2,1)S(1)} copy-done((bf16[336,256]{1,0:T(8,128)(2,1)S(1)}, bf16[336,256]{1,0:T(8,128)(2,1)}, u32[]{:S(2)}) %copy-start.11) | copy-done | bytes 172056
  3.4 3.0 %collective-permute-start.3 = (bf16[336,256]{1,0:T(8,128)(2,1)S(1)}, bf16[336,256]{1,0:T(8,128)(2,1)S(1)}, u32[]{:S(2)}, u32[]{:S(2)}) collective-permute-start(bf16[336,256]{1,0:T(8,128)(2,1)S(1)} %shard_map.123.refs_0_), channel_id=1, source_target_pairs={{0,4},{1,5},{2,6},{3,7},{4,0},{5,1},{6,2},{7,3},{8,12},{9,13},{10,... | collective-permute-start | bytes 516104 | tf_op jit(solution)/shard_map/ppermute | solution.py:202
  6.4 1.5 %collective-permute-start.2 = (bf16[336,256]{1,0:T(8,128)(2,1)S(1)}, bf16[336,256]{1,0:T(8,128)(2,1)S(1)}, u32[]{:S(2)}, u32[]{:S(2)}) collective-permute-start(bf16[336,256]{1,0:T(8,128)(2,1)S(1)} %shard_map.123.refs_0_), channel_id=1, source_target_pairs={{0,2},{1,3},{2,0},{3,1},{4,6},{5,7},{6,4},{7,5},{8,10},{9,11},{10,... | collective-permute-start | bytes 516104 | tf_op jit(solution)/shard_map/ppermute | solution.py:202
  8.0 2.6 %collective-permute-start.7 = (bf16[336,256]{1,0:T(8,128)(2,1)S(1)}, bf16[336,256]{1,0:T(8,128)(2,1)S(1)}, u32[]{:S(2)}, u32[]{:S(2)}) collective-permute-start(bf16[336,256]{1,0:T(8,128)(2,1)S(1)} %copy-done.20), channel_id=1, source_target_pairs={{0,8},{1,9},{2,10},{3,11},{4,12},{5,13},{6,14},{7,15},{8,0},{9,1},... | collective-permute-start | bytes 516104 | tf_op jit(solution)/shard_map/ppermute | solution.py:202
  10.8 1.7 %collective-permute-start.10 = (bf16[336,256]{1,0:T(8,128)(2,1)S(1)}, bf16[336,256]{1,0:T(8,128)(2,1)S(1)}, u32[]{:S(2)}, u32[]{:S(2)}) collective-permute-start(bf16[336,256]{1,0:T(8,128)(2,1)S(1)} %collective-permute-done.3.refs_1_.refs_4_), channel_id=1, source_target_pairs={{0,2},{1,3},{2,0},{3,1},{4,6},{5,7},{6,4},{7,5},{8,10},{9,11},{10,... | collective-permute-start | bytes 516104 | tf_op jit(solution)/shard_map/ppermute | solution.py:202
  12.7 2.5 %shard_map.124 = (f32[1,64,256]{2,1,0:T(8,128)S(1)}, f32[1,64,256]{2,1,0:T(8,128)S(1)}) custom-call(bf16[336,256]{1,0:T(8,128)(2,1)S(1)} %shard_map.123.refs_0_, bf16[336,256]{1,0:T(8,128)(2,1)S(1)} %collective-permute-done.refs_1_, bf16[32,1024,128]{2,1,0:T(8,128)(2,1)S(1)} %copy-done), custom_call_target="tpu_custom_call" | custom-call | flops 2400000000 | bytes 1048576 | tf_op jit(solution)/shard_map/pallas_call | solution.py:237
  15.3 4.0 %shard_map.125 = (f32[2,64,256]{2,1,0:T(8,128)S(1)}, f32[2,64,256]{2,1,0:T(8,128)S(1)}) custom-call(bf16[336,256]{1,0:T(8,128)(2,1)S(1)} %collective-permute-done.2.refs_0_.refs_2_, bf16[336,256]{1,0:T(8,128)(2,1)S(1)} %collective-permute-done.3.refs_1_.refs_4_, bf16[336,256]{1,0:T(8,128)(2,1)S(1)} %collective-permute-done.4.refs_2_.refs_3_, ...), custom_call_target="tpu_custom_call" | custom-call | flops 4800000000 | bytes 1048576 | tf_op jit(solution)/shard_map/pallas_call | solution.py:237
  20.2 1.6 %collective-permute-start.9 = (bf16[336,256]{1,0:T(8,128)(2,1)S(1)}, bf16[336,256]{1,0:T(8,128)(2,1)S(1)}, u32[]{:S(2)}, u32[]{:S(2)}) collective-permute-start(bf16[336,256]{1,0:T(8,128)(2,1)S(1)} %shard_map.126.refs_1_.refs_8_), channel_id=1, source_target_pairs={{0,4},{1,5},{2,6},{3,7},{4,0},{5,1},{6,2},{7,3},{8,12},{9,13},{10,... | collective-permute-start | bytes 516104 | tf_op jit(solution)/shard_map/ppermute | solution.py:202
  22.3 4.7 %shard_map.127 = (f32[2,64,256]{2,1,0:T(8,128)S(1)}, f32[2,64,256]{2,1,0:T(8,128)}) custom-call(bf16[336,256]{1,0:T(8,128)(2,1)S(1)} %collective-permute-done.10.refs_0_.refs_6_, bf16[336,256]{1,0:T(8,128)(2,1)S(1)} %shard_map.126.refs_1_.refs_8_, bf16[336,256]{1,0:T(8,128)(2,1)S(1)} %collective-permute-done.11.refs_2_.refs_7_, ...), custom_call_target="tpu_custom_call" | custom-call | flops 4800000000 | bytes 1048576 | tf_op jit(solution)/shard_map/pallas_call | solution.py:237
  27.1 0.9 %collective-permute-done.8.refs_0_.refs_10_ = bf16[336,256]{1,0:T(8,128)(2,1)S(1)} collective-permute-done((bf16[336,256]{1,0:T(8,128)(2,1)S(1)}, bf16[336,256]{1,0:T(8,128)(2,1)S(1)}, u32[]{:S(2)}, u32[]{:S(2)}) %collective-permute-start.8) | collective-permute-done | bytes 172064 | tf_op jit(solution)/shard_map/ppermute | solution.py:202
  29.6 4.0 %shard_map.129 = (f32[2,64,256]{2,1,0:T(8,128)S(1)}, f32[2,64,256]{2,1,0:T(8,128)S(1)}) custom-call(bf16[336,256]{1,0:T(8,128)(2,1)S(1)} %collective-permute-done.8.refs_0_.refs_10_, bf16[336,256]{1,0:T(8,128)(2,1)S(1)} %shard_map.128.refs_1_.refs_12_, bf16[336,256]{1,0:T(8,128)(2,1)S(1)} %collective-permute-done.13.refs_2_.refs_11_, ...), custom_call_target="tpu_custom_call" | custom-call | flops 4800000000 | bytes 1048576 | tf_op jit(solution)/shard_map/pallas_call | solution.py:237
  33.7 1.1 %collective-permute-done.18.refs_0_ = bf16[336,256]{1,0:T(8,128)(2,1)S(1)} collective-permute-done((bf16[336,256]{1,0:T(8,128)(2,1)S(1)}, bf16[336,256]{1,0:T(8,128)(2,1)S(1)}, u32[]{:S(2)}, u32[]{:S(2)}) %collective-permute-start.18) | collective-permute-done | bytes 172064 | tf_op jit(solution)/shard_map/ppermute | solution.py:202
  35.5 1.2 %collective-permute-done.16.refs_5_.refs_4_ = f32[2,64,256]{2,1,0:T(8,128)S(1)} collective-permute-done((f32[2,64,256]{2,1,0:T(8,128)}, f32[2,64,256]{2,1,0:T(8,128)S(1)}, u32[]{:S(2)}, u32[]{:S(2)}) %collective-permute-start.16) | collective-permute-done | bytes 131104 | tf_op jit(solution)/shard_map/ppermute | solution.py:202
  36.7 3.4 %copy-done.1 = bf16[32,1024,128]{2,1,0:T(8,128)(2,1)S(1)} copy-done((bf16[32,1024,128]{2,1,0:T(8,128)(2,1)S(1)}, bf16[32,1024,128]{2,1,0:T(8,128)(2,1)}, u32[]{:S(2)}) %copy-start.1) | copy-done | bytes 8388632
  40.1 2.5 %shard_map.132 = (f32[1,64,256]{2,1,0:T(8,128)S(1)}, f32[1,64,256]{2,1,0:T(8,128)S(1)}) custom-call(bf16[336,256]{1,0:T(8,128)(2,1)S(1)} %shard_map.131.refs_0_.refs_14_, bf16[336,256]{1,0:T(8,128)(2,1)S(1)} %collective-permute-done.19.refs_1_.refs_15_, bf16[32,1024,128]{2,1,0:T(8,128)(2,1)S(1)} %copy-done.1, ...), custom_call_target="tpu_custom_call" | custom-call | flops 2400000000 | bytes 1048576 | tf_op jit(solution)/shard_map/pallas_call | solution.py:237
  43.1 1.2 %collective-permute-start.17 = (bf16[3,64,256]{2,1,0:T(8,128)(2,1)S(1)}, bf16[3,64,256]{2,1,0:T(8,128)(2,1)S(1)}, u32[]{:S(2)}, u32[]{:S(2)}) collective-permute-start(bf16[3,64,256]{2,1,0:T(8,128)(2,1)S(1)} %shard_map.130), channel_id=1, source_target_pairs={{0,2},{1,3},{2,0},{3,1},{4,6},{5,7},{6,4},{7,5},{8,10},{9,11},{10,... | collective-permute-start | bytes 294920 | tf_op jit(solution)/shard_map/ppermute | solution.py:202
  44.2 1.0 %collective-permute-start.21 = (bf16[1,64,256]{2,1,0:T(8,128)(2,1)S(1)}, bf16[1,64,256]{2,1,0:T(8,128)(2,1)S(1)}, u32[]{:S(2)}, u32[]{:S(2)}) collective-permute-start(bf16[1,64,256]{2,1,0:T(8,128)(2,1)S(1)} %shard_map.133), channel_id=1, source_target_pairs={{0,2},{1,3},{2,0},{3,1},{4,6},{5,7},{6,4},{7,5},{8,10},{9,11},{10,... | collective-permute-start | bytes 98312 | tf_op jit(solution)/shard_map/ppermute | solution.py:202
  45.3 1.8 %shard_map.134 = (f32[64,256]{1,0:T(8,128)S(1)}, f32[64,256]{1,0:T(8,128)S(1)}, f32[64,256]{1,0:T(8,128)S(1)}) custom-call(bf16[336,256]{1,0:T(8,128)(2,1)S(1)} %copy-done.13, bf16[336,256]{1,0:T(8,128)(2,1)S(1)} %collective-permute-done.refs_1_, bf16[336,256]{1,0:T(8,128)(2,1)S(1)} %collective-permute-done.2.refs_0_.refs_2_, ...), custom_call_target="tpu_custom_call" | custom-call | flops 2400000000 | bytes 1048576 | tf_op jit(solution)/shard_map/pallas_call | solution.py:325
  47.1 1.3 %collective-permute-done.17.refs_2_ = bf16[3,64,256]{2,1,0:T(8,128)(2,1)S(1)} collective-permute-done((bf16[3,64,256]{2,1,0:T(8,128)(2,1)S(1)}, bf16[3,64,256]{2,1,0:T(8,128)(2,1)S(1)}, u32[]{:S(2)}, u32[]{:S(2)}) %collective-permute-start.17) | collective-permute-done | bytes 98336 | tf_op jit(solution)/shard_map/ppermute | solution.py:202
  48.8 0.9 %collective-permute-start.22 = (bf16[2,64,256]{2,1,0:T(8,128)(2,1)S(1)}, bf16[2,64,256]{2,1,0:T(8,128)(2,1)S(1)}, u32[]{:S(2)}, u32[]{:S(2)}) collective-permute-start(bf16[2,64,256]{2,1,0:T(8,128)(2,1)S(1)} %get-tuple-element.35), channel_id=1, source_target_pairs={{0,4},{1,5},{2,6},{3,7},{4,0},{5,1},{6,2},{7,3},{8,12},{9,13},{10,... | collective-permute-start | bytes 196616 | tf_op jit(solution)/shard_map/ppermute | solution.py:202
  49.7 3.5 %collective-permute-done.22.refs_1_ = bf16[2,64,256]{2,1,0:T(8,128)(2,1)S(1)} collective-permute-done((bf16[2,64,256]{2,1,0:T(8,128)(2,1)S(1)}, bf16[2,64,256]{2,1,0:T(8,128)(2,1)S(1)}, u32[]{:S(2)}, u32[]{:S(2)}) %collective-permute-start.22) | collective-permute-done | bytes 65568 | tf_op jit(solution)/shard_map/ppermute | solution.py:202
  53.2 3.7 %collective-permute-start.23 = (bf16[1,64,256]{2,1,0:T(8,128)(2,1)S(1)}, bf16[1,64,256]{2,1,0:T(8,128)(2,1)S(1)}, u32[]{:S(2)}, u32[]{:S(2)}) collective-permute-start(bf16[1,64,256]{2,1,0:T(8,128)(2,1)S(1)} %get-tuple-element.37), channel_id=1, source_target_pairs={{0,8},{1,9},{2,10},{3,11},{4,12},{5,13},{6,14},{7,15},{8,0},{9,1},... | collective-permute-start | bytes 98312 | tf_op jit(solution)/shard_map/ppermute | solution.py:202
  56.9 2.2 %collective-permute-done.23.came_ref = bf16[1,64,256]{2,1,0:T(8,128)(2,1)S(1)} collective-permute-done((bf16[1,64,256]{2,1,0:T(8,128)(2,1)S(1)}, bf16[1,64,256]{2,1,0:T(8,128)(2,1)S(1)}, u32[]{:S(2)}, u32[]{:S(2)}) %collective-permute-start.23) | collective-permute-done | bytes 32800 | tf_op jit(solution)/shard_map/ppermute | solution.py:202
  (83 shorter events, 5.9 us)
Async XLA Ops:
  3.4 7.4 %collective-permute-start.3 = (bf16[336,256]{1,0:T(8,128)(2,1)S(1)}, bf16[336,256]{1,0:T(8,128)(2,1)S(1)}, u32[]{:S(2)}, u32[]{:S(2)}) collective-permute-start(bf16[336,256]{1,0:T(8,128)(2,1)S(1)} %shard_map.123.refs_0_), channel_id=1, source_target_pairs={{0,4},{1,5},{2,6},{3,7},{4,0},{5,1},{6,2},{7,3},{8,12},{9,13},{10,... | collective-permute-start | bytes 516104 | tf_op jit(solution)/shard_map/ppermute | solution.py:202
  6.4 6.1 %collective-permute-start.2 = (bf16[336,256]{1,0:T(8,128)(2,1)S(1)}, bf16[336,256]{1,0:T(8,128)(2,1)S(1)}, u32[]{:S(2)}, u32[]{:S(2)}) collective-permute-start(bf16[336,256]{1,0:T(8,128)(2,1)S(1)} %shard_map.123.refs_0_), channel_id=1, source_target_pairs={{0,2},{1,3},{2,0},{3,1},{4,6},{5,7},{6,4},{7,5},{8,10},{9,11},{10,... | collective-permute-start | bytes 516104 | tf_op jit(solution)/shard_map/ppermute | solution.py:202
  8.0 4.8 %collective-permute-start = (bf16[336,256]{1,0:T(8,128)(2,1)S(1)}, bf16[336,256]{1,0:T(8,128)(2,1)S(1)}, u32[]{:S(2)}, u32[]{:S(2)}) collective-permute-start(bf16[336,256]{1,0:T(8,128)(2,1)S(1)} %shard_map.123.refs_0_), channel_id=1, source_target_pairs={{0,1},{1,0},{2,3},{3,2},{4,5},{5,4},{6,7},{7,6},{8,9},{9,8},{10,11... | collective-permute-start | bytes 516104 | tf_op jit(solution)/shard_map/ppermute | solution.py:202
  8.0 11.4 %collective-permute-start.7 = (bf16[336,256]{1,0:T(8,128)(2,1)S(1)}, bf16[336,256]{1,0:T(8,128)(2,1)S(1)}, u32[]{:S(2)}, u32[]{:S(2)}) collective-permute-start(bf16[336,256]{1,0:T(8,128)(2,1)S(1)} %copy-done.20), channel_id=1, source_target_pairs={{0,8},{1,9},{2,10},{3,11},{4,12},{5,13},{6,14},{7,15},{8,0},{9,1},... | collective-permute-start | bytes 516104 | tf_op jit(solution)/shard_map/ppermute | solution.py:202
  10.8 4.5 %collective-permute-start.5 = (bf16[336,256]{1,0:T(8,128)(2,1)S(1)}, bf16[336,256]{1,0:T(8,128)(2,1)S(1)}, u32[]{:S(2)}, u32[]{:S(2)}) collective-permute-start(bf16[336,256]{1,0:T(8,128)(2,1)S(1)} %collective-permute-done.3.refs_1_.refs_4_), channel_id=1, source_target_pairs={{0,1},{1,0},{2,3},{3,2},{4,5},{5,4},{6,7},{7,6},{8,9},{9,8},{10,11... | collective-permute-start | bytes 516104 | tf_op jit(solution)/shard_map/ppermute | solution.py:202
  10.8 8.9 %collective-permute-start.10 = (bf16[336,256]{1,0:T(8,128)(2,1)S(1)}, bf16[336,256]{1,0:T(8,128)(2,1)S(1)}, u32[]{:S(2)}, u32[]{:S(2)}) collective-permute-start(bf16[336,256]{1,0:T(8,128)(2,1)S(1)} %collective-permute-done.3.refs_1_.refs_4_), channel_id=1, source_target_pairs={{0,2},{1,3},{2,0},{3,1},{4,6},{5,7},{6,4},{7,5},{8,10},{9,11},{10,... | collective-permute-start | bytes 516104 | tf_op jit(solution)/shard_map/ppermute | solution.py:202
  12.5 2.8 %collective-permute-start.4 = (bf16[336,256]{1,0:T(8,128)(2,1)S(1)}, bf16[336,256]{1,0:T(8,128)(2,1)S(1)}, u32[]{:S(2)}, u32[]{:S(2)}) collective-permute-start(bf16[336,256]{1,0:T(8,128)(2,1)S(1)} %collective-permute-done.2.refs_0_.refs_2_), channel_id=1, source_target_pairs={{0,1},{1,0},{2,3},{3,2},{4,5},{5,4},{6,7},{7,6},{8,9},{9,8},{10,11... | collective-permute-start | bytes 516104 | tf_op jit(solution)/shard_map/ppermute | solution.py:202
  19.3 2.9 %collective-permute-start.12 = (bf16[336,256]{1,0:T(8,128)(2,1)S(1)}, bf16[336,256]{1,0:T(8,128)(2,1)S(1)}, u32[]{:S(2)}, u32[]{:S(2)}) collective-permute-start(bf16[336,256]{1,0:T(8,128)(2,1)S(1)} %shard_map.126.refs_1_.refs_8_), channel_id=1, source_target_pairs={{0,1},{1,0},{2,3},{3,2},{4,5},{5,4},{6,7},{7,6},{8,9},{9,8},{10,11... | collective-permute-start | bytes 516104 | tf_op jit(solution)/shard_map/ppermute | solution.py:202
  19.7 2.6 %collective-permute-start.11 = (bf16[336,256]{1,0:T(8,128)(2,1)S(1)}, bf16[336,256]{1,0:T(8,128)(2,1)S(1)}, u32[]{:S(2)}, u32[]{:S(2)}) collective-permute-start(bf16[336,256]{1,0:T(8,128)(2,1)S(1)} %collective-permute-done.10.refs_0_.refs_6_), channel_id=1, source_target_pairs={{0,1},{1,0},{2,3},{3,2},{4,5},{5,4},{6,7},{7,6},{8,9},{9,8},{10,11... | collective-permute-start | bytes 516104 | tf_op jit(solution)/shard_map/ppermute | solution.py:202
  19.9 2.4 %collective-permute-start.1 = (f32[1,64,256]{2,1,0:T(8,128)S(1)}, f32[1,64,256]{2,1,0:T(8,128)S(1)}, u32[]{:S(2)}, u32[]{:S(2)}) collective-permute-start(f32[1,64,256]{2,1,0:T(8,128)S(1)} %get-tuple-element.23), channel_id=1, source_target_pairs={{0,1},{1,0},{2,3},{3,2},{4,5},{5,4},{6,7},{7,6},{8,9},{9,8},{10,11... | collective-permute-start | bytes 196616 | tf_op jit(solution)/shard_map/ppermute | solution.py:202
  20.2 6.8 %collective-permute-start.9 = (bf16[336,256]{1,0:T(8,128)(2,1)S(1)}, bf16[336,256]{1,0:T(8,128)(2,1)S(1)}, u32[]{:S(2)}, u32[]{:S(2)}) collective-permute-start(bf16[336,256]{1,0:T(8,128)(2,1)S(1)} %shard_map.126.refs_1_.refs_8_), channel_id=1, source_target_pairs={{0,4},{1,5},{2,6},{3,7},{4,0},{5,1},{6,2},{7,3},{8,12},{9,13},{10,... | collective-permute-start | bytes 516104 | tf_op jit(solution)/shard_map/ppermute | solution.py:202
  21.8 6.2 %collective-permute-start.8 = (bf16[336,256]{1,0:T(8,128)(2,1)S(1)}, bf16[336,256]{1,0:T(8,128)(2,1)S(1)}, u32[]{:S(2)}, u32[]{:S(2)}) collective-permute-start(bf16[336,256]{1,0:T(8,128)(2,1)S(1)} %shard_map.126.refs_1_.refs_8_), channel_id=1, source_target_pairs={{0,2},{1,3},{2,0},{3,1},{4,6},{5,7},{6,4},{7,5},{8,10},{9,11},{10,... | collective-permute-start | bytes 516104 | tf_op jit(solution)/shard_map/ppermute | solution.py:202
  27.0 2.6 %collective-permute-start.14 = (bf16[336,256]{1,0:T(8,128)(2,1)S(1)}, bf16[336,256]{1,0:T(8,128)(2,1)S(1)}, u32[]{:S(2)}, u32[]{:S(2)}) collective-permute-start(bf16[336,256]{1,0:T(8,128)(2,1)S(1)} %shard_map.128.refs_1_.refs_12_), channel_id=1, source_target_pairs={{0,1},{1,0},{2,3},{3,2},{4,5},{5,4},{6,7},{7,6},{8,9},{9,8},{10,11... | collective-permute-start | bytes 516104 | tf_op jit(solution)/shard_map/ppermute | solution.py:202
  28.0 1.6 %collective-permute-start.13 = (bf16[336,256]{1,0:T(8,128)(2,1)S(1)}, bf16[336,256]{1,0:T(8,128)(2,1)S(1)}, u32[]{:S(2)}, u32[]{:S(2)}) collective-permute-start(bf16[336,256]{1,0:T(8,128)(2,1)S(1)} %collective-permute-done.8.refs_0_.refs_10_), channel_id=1, source_target_pairs={{0,1},{1,0},{2,3},{3,2},{4,5},{5,4},{6,7},{7,6},{8,9},{9,8},{10,11... | collective-permute-start | bytes 516104 | tf_op jit(solution)/shard_map/ppermute | solution.py:202
  28.0 1.6 %collective-permute-start.6 = (f32[2,64,256]{2,1,0:T(8,128)S(1)}, f32[2,64,256]{2,1,0:T(8,128)S(1)}, u32[]{:S(2)}, u32[]{:S(2)}) collective-permute-start(f32[2,64,256]{2,1,0:T(8,128)S(1)} %get-tuple-element.25), channel_id=1, source_target_pairs={{0,1},{1,0},{2,3},{3,2},{4,5},{5,4},{6,7},{7,6},{8,9},{9,8},{10,11... | collective-permute-start | bytes 393224 | tf_op jit(solution)/shard_map/ppermute | solution.py:202
  28.5 6.3 %collective-permute-start.18 = (bf16[336,256]{1,0:T(8,128)(2,1)S(1)}, bf16[336,256]{1,0:T(8,128)(2,1)S(1)}, u32[]{:S(2)}, u32[]{:S(2)}) collective-permute-start(bf16[336,256]{1,0:T(8,128)(2,1)S(1)} %shard_map.128.refs_1_.refs_12_), channel_id=1, source_target_pairs={{0,2},{1,3},{2,0},{3,1},{4,6},{5,7},{6,4},{7,5},{8,10},{9,11},{10,... | collective-permute-start | bytes 516104 | tf_op jit(solution)/shard_map/ppermute | solution.py:202
  34.9 1.9 %collective-permute-start.19 = (bf16[336,256]{1,0:T(8,128)(2,1)S(1)}, bf16[336,256]{1,0:T(8,128)(2,1)S(1)}, u32[]{:S(2)}, u32[]{:S(2)}) collective-permute-start(bf16[336,256]{1,0:T(8,128)(2,1)S(1)} %shard_map.131.refs_0_.refs_14_), channel_id=1, source_target_pairs={{0,1},{1,0},{2,3},{3,2},{4,5},{5,4},{6,7},{7,6},{8,9},{9,8},{10,11... | collective-permute-start | bytes 516104 | tf_op jit(solution)/shard_map/ppermute | solution.py:202
  35.0 1.8 %collective-permute-start.16 = (f32[2,64,256]{2,1,0:T(8,128)}, f32[2,64,256]{2,1,0:T(8,128)S(1)}, u32[]{:S(2)}, u32[]{:S(2)}) collective-permute-start(f32[2,64,256]{2,1,0:T(8,128)} %get-tuple-element.30), channel_id=1, source_target_pairs={{0,1},{1,0},{2,3},{3,2},{4,5},{5,4},{6,7},{7,6},{8,9},{9,8},{10,11... | collective-permute-start | bytes 393224 | tf_op jit(solution)/shard_map/ppermute | solution.py:202
  35.4 7.6 %collective-permute-start.15 = (f32[2,64,256]{2,1,0:T(8,128)}, f32[2,64,256]{2,1,0:T(8,128)S(1)}, u32[]{:S(2)}, u32[]{:S(2)}) collective-permute-start(f32[2,64,256]{2,1,0:T(8,128)} %copy-done.14), channel_id=1, source_target_pairs={{0,1},{1,0},{2,3},{3,2},{4,5},{5,4},{6,7},{7,6},{8,9},{9,8},{10,11... | collective-permute-start | bytes 393224 | tf_op jit(solution)/shard_map/ppermute | solution.py:202
  42.7 1.6 %collective-permute-start.20 = (f32[1,64,256]{2,1,0:T(8,128)S(1)}, f32[1,64,256]{2,1,0:T(8,128)S(1)}, u32[]{:S(2)}, u32[]{:S(2)}) collective-permute-start(f32[1,64,256]{2,1,0:T(8,128)S(1)} %get-tuple-element.32), channel_id=1, source_target_pairs={{0,1},{1,0},{2,3},{3,2},{4,5},{5,4},{6,7},{7,6},{8,9},{9,8},{10,11... | collective-permute-start | bytes 196616 | tf_op jit(solution)/shard_map/ppermute | solution.py:202
  43.1 5.4 %collective-permute-start.17 = (bf16[3,64,256]{2,1,0:T(8,128)(2,1)S(1)}, bf16[3,64,256]{2,1,0:T(8,128)(2,1)S(1)}, u32[]{:S(2)}, u32[]{:S(2)}) collective-permute-start(bf16[3,64,256]{2,1,0:T(8,128)(2,1)S(1)} %shard_map.130), channel_id=1, source_target_pairs={{0,2},{1,3},{2,0},{3,1},{4,6},{5,7},{6,4},{7,5},{8,10},{9,11},{10,... | collective-permute-start | bytes 294920 | tf_op jit(solution)/shard_map/ppermute | solution.py:202
  44.2 4.5 %collective-permute-start.21 = (bf16[1,64,256]{2,1,0:T(8,128)(2,1)S(1)}, bf16[1,64,256]{2,1,0:T(8,128)(2,1)S(1)}, u32[]{:S(2)}, u32[]{:S(2)}) collective-permute-start(bf16[1,64,256]{2,1,0:T(8,128)(2,1)S(1)} %shard_map.133), channel_id=1, source_target_pairs={{0,2},{1,3},{2,0},{3,1},{4,6},{5,7},{6,4},{7,5},{8,10},{9,11},{10,... | collective-permute-start | bytes 98312 | tf_op jit(solution)/shard_map/ppermute | solution.py:202
  48.8 4.3 %collective-permute-start.22 = (bf16[2,64,256]{2,1,0:T(8,128)(2,1)S(1)}, bf16[2,64,256]{2,1,0:T(8,128)(2,1)S(1)}, u32[]{:S(2)}, u32[]{:S(2)}) collective-permute-start(bf16[2,64,256]{2,1,0:T(8,128)(2,1)S(1)} %get-tuple-element.35), channel_id=1, source_target_pairs={{0,4},{1,5},{2,6},{3,7},{4,0},{5,1},{6,2},{7,3},{8,12},{9,13},{10,... | collective-permute-start | bytes 196616 | tf_op jit(solution)/shard_map/ppermute | solution.py:202
  53.2 6.0 %collective-permute-start.23 = (bf16[1,64,256]{2,1,0:T(8,128)(2,1)S(1)}, bf16[1,64,256]{2,1,0:T(8,128)(2,1)S(1)}, u32[]{:S(2)}, u32[]{:S(2)}) collective-permute-start(bf16[1,64,256]{2,1,0:T(8,128)(2,1)S(1)} %get-tuple-element.37), channel_id=1, source_target_pairs={{0,8},{1,9},{2,10},{3,11},{4,12},{5,13},{6,14},{7,15},{8,0},{9,1},... | collective-permute-start | bytes 98312 | tf_op jit(solution)/shard_map/ppermute | solution.py:202
  (21 other events, 150.7 us)

commit v3 on v2

--- a/solution.py
+++ b/solution.py
@@ -96,10 +96,12 @@
 
 def exch_kernel(count, per, npno, *refs):
     blocks, fitted_ref = refs[:count], refs[count]
-    outs, (held_ref, occ_ref, wide_ref, f_ref, sem) = refs[-7:-5], refs[-5:]
+    outs, amps_ref, (held_ref, occ_ref, wide_ref, f_ref, sem) = refs[-8:-6], refs[-6], refs[-5:]
     npao, width = fitted_ref.shape[1:]
     orbitals = read_orbitals(blocks, per, npno, held_ref, occ_ref, sem)
     orbitals.start()
+    for k in range(count):
+        amps_ref[k] = blocks[k][per * npno : (per + 1) * npno, :]
     codes = code(lax.broadcasted_iota(jnp.int32, (1, npao), 1))
     for group in batches(count * per):
         for at, pair in enumerate(group):
@@ -130,15 +132,15 @@
             out_ref[k] = total.astype(out_ref.dtype)
 
 
-def coupled_kernel(count, *refs):
-    blocks, refs = refs[:count], refs[count:]
+def coupled_kernel(orders, *refs):
+    amps_in, refs = refs[: len(orders)], refs[len(orders) :]
     where_ref, weight_ref, inter_ref, occ_ref, count_ref, occ_energy_ref, energy_ref, amps_ref = refs[:8]
-    kept_ref, factor_ref, live_ref, all_ref, half_ref = refs[8:]
+    kept_ref, factor_ref, live_ref, all_ref, half_ref = refs[-5:]
     per, ncpl, npno = inter_ref.shape[:3]
-    for k in range(count):
-        rows = blocks[k][per * npno : (per + 1) * npno, :]
-        for p in range(per):
-            all_ref[k * per + p] = rows[:, p * npno : (p + 1) * npno]
+    for order, ref in zip(orders, amps_in):
+        for k, m in enumerate(order):
+            for p in range(per):
+                all_ref[m * per + p] = ref[k, :, p * npno : (p + 1) * npno]
     for p in range(per):
         for c in range(ncpl):
             half_ref[p * ncpl + c] = weight_ref[p, c] * jnp.dot(
@@ -167,9 +169,9 @@
         live_ref[:, here] = live
 
 
-def finish_kernel(own_ref, came_ref, kept_ref, factor_ref, live_ref, new_ref, ints_ref):
+def finish_kernel(own_ref, came_ref, late_ref, kept_ref, factor_ref, live_ref, new_ref, ints_ref):
     per, npno = new_ref.shape[:2]
-    exch = own_ref[0] + came_ref[0].astype(jnp.float32)
+    exch = own_ref[0] + came_ref[0].astype(jnp.float32) + late_ref[0].astype(jnp.float32)
     new = kept_ref[...] - exch * factor_ref[...]
     ints = exch * live_ref[...]
     for p in range(per):
@@ -229,31 +231,7 @@
             cost_estimate=estimate(flops),
         )(array, *after, *[fitted_ints] * held)
 
-    mine, came, chain, back = {}, {}, [], []
-
-    def exchange(which, cost=COST):
-        count = 2 * len(which)
-        after = chain[-1:] + back[:-1][-1:]
-        out = pl.pallas_call(
-            functools.partial(exch_kernel, count, per, npno),
-            out_shape=[jax.ShapeDtypeStruct((len(which), npno, per * npno), jnp.float32)] * 2,
-            in_specs=[VMEM] * (count + 1) + [HBM] * len(after),
-            out_specs=[VMEM] * 2,
-            scratch_shapes=[
-                pltpu.VMEM((8, 128), jnp.int32),
-                pltpu.SMEM((8, 128), jnp.int32),
-                pltpu.VMEM((GROUP, npno, npao), jnp.bfloat16),
-                pltpu.VMEM((GROUP, npno, 2 * width), jnp.bfloat16),
-                pltpu.SemaphoreType.DMA,
-            ],
-            compiler_params=params,
-            cost_estimate=estimate(cost * count * per),
-        )(*[blocks[m] for m in which], *[blocks[m ^ 1] for m in which], fitted_ints, *after)
-        chain.append(out[0])
-        got = swap(out[1], 1)
-        back.append(got)
-        for k, m in enumerate(which):
-            mine[m], came[m] = (out[0], k), (got, k)
+    mine, chain, back, amps_of = {}, [], [], []
 
     def add_up(plan, dtypes, after=()):
         arrays = []
@@ -275,15 +253,49 @@
             compiler_params=params,
         )(*arrays, *after)
 
+    def exchange(which, cost=COST):
+        count = 2 * len(which)
+        after = chain[-1:] + (back[:-1][-1:] if far[-1] not in which else [])
+        out = pl.pallas_call(
+            functools.partial(exch_kernel, count, per, npno),
+            out_shape=[jax.ShapeDtypeStruct((len(which), npno, per * npno), jnp.float32)] * 2
+            + [jax.ShapeDtypeStruct((count, npno, dom), jnp.bfloat16)],
+            in_specs=[VMEM] * (count + 1) + [HBM] * len(after),
+            out_specs=[VMEM] * 3,
+            scratch_shapes=[
+                pltpu.VMEM((8, 128), jnp.int32),
+                pltpu.SMEM((8, 128), jnp.int32),
+                pltpu.VMEM((GROUP, npno, npao), jnp.bfloat16),
+                pltpu.VMEM((GROUP, npno, 2 * width), jnp.bfloat16),
+                pltpu.SemaphoreType.DMA,
+            ],
+            compiler_params=params,
+            cost_estimate=estimate(cost * count * per),
+        )(*[blocks[m] for m in which], *[blocks[m ^ 1] for m in which], fitted_ints, *after)
+        chain.append(out[0])
+        amps_of.append((out[2], list(which) + [m ^ 1 for m in which]))
+        got = swap(out[1], 1)
+        kinds = [[(k, m) for k, m in enumerate(which) if bool(m & steps[-1]) == far] for far in (False, True)]
+        types = [dtype for kind, dtype in zip(kinds, (jnp.float32, SENT)) if kind]
+        kinds = [kind for kind in kinds if kind]
+        sums = add_up([[[(out[0], k), (got, k)] for k, _ in kind] for kind in kinds], types)
+        for array, kind in zip(sums, kinds):
+            for at, (_, m) in enumerate(kind):
+                mine[m] = (array, at)
+        back.append(sums[0])
+
     top, rest, last = steps[0], steps[1:], steps[-1]
+    own = [0]
+    for mask in steps[:-1]:
+        own += [m ^ mask for m in own]
+    far = [m ^ last for m in own]
     blocks = {top: swap(first_block, top)}
     block = blocks[0] = gate(block, (), 32 * COST)
     for mask in rest + [1]:
         blocks[mask] = swap(block, mask)
-    exchange([0])
+    exchange([0], 0)
     for m in rest:
         blocks[m ^ 1] = swap(blocks[m], 1)
-    exchange(rest[::-1])
     for m in rest[:-1]:
         blocks[m ^ last] = swap(blocks[m], last)
         blocks[m ^ last ^ 1] = swap(blocks[m ^ last], 1)
@@ -291,41 +303,39 @@
     for mask in (rest[0], last):
         blocks[top ^ mask] = swap(blocks[top], mask)
     blocks[top ^ 1] = swap(blocks[top], 1)
+    exchange(rest[::-1])
+    blocks[top ^ rest[0]] = gate(blocks[top ^ rest[0]], chain[-1:], held=True)
     exchange([rest[0] ^ last, top])
-    blocks[top ^ rest[0]] = gate(blocks[top ^ rest[0]], chain[-1:], held=True)
     even = [0, top]
     for mask in rest:
         for m in list(even):
             if m ^ mask not in blocks:
                 blocks[m ^ mask] = swap(blocks[m], mask)
             even.append(m ^ mask)
-    own = [0]
-    for mask in steps[:-1]:
-        own += [m ^ mask for m in own]
-    far = [m ^ last for m in own]
     left = [m for m in far[:-1] + own if m not in mine]
     for m in left:
         if m ^ 1 not in blocks:
             blocks[m ^ 1] = swap(blocks[m], 1)
+    blocks[far[-1]] = gate(blocks[far[-1]], chain[-1:], held=True)
+    blocks[far[-1] ^ 1] = swap(blocks[far[-1]], 1)
     for first in range(0, len(left), CALL):
         exchange(left[first : first + CALL])
-    blocks[far[-1]] = gate(blocks[far[-1]], chain[-1:], 32 * COST)
-    blocks[far[-1] ^ 1] = swap(blocks[far[-1]], 1)
     exchange(far[-1:])
 
-    ready = add_up([[[mine[m], came[m]] for m in far[:-1]]], [SENT])[0]
-    final = add_up([[[mine[m], came[m]] for m in far[-1:]]], [SENT])[0]
-    terms = [[mine[m], came[m]] for m in own]
-    ready, final = swap(ready, last), swap(final, last)
-    for k, term in enumerate(terms):
-        term.append((ready, k) if k < len(own) - 1 else (final, 0))
+    ready = add_up([[[mine[m]] for m in far[:-1]]], [SENT])[0]
+    final = gate(mine[far[-1]][0], (), 32 * COST)
+    late = final
+    terms = [[mine[m]] for m in own]
+    ready, final = swap(ready, last), swap(final, far[-1])
+    for k in range(len(own) - 1):
+        terms[k].append((ready, k))
 
     away = jnp.bitwise_xor(cpl_pair // per, me)
     where = away * per + cpl_pair % per
     kept, factor, live = pl.pallas_call(
-        functools.partial(coupled_kernel, ndev),
+        functools.partial(coupled_kernel, [order for _, order in amps_of]),
         out_shape=[jax.ShapeDtypeStruct((npno, per * npno), jnp.float32)] * 3,
-        in_specs=[VMEM] * ndev + [SMEM, SMEM, VMEM, SMEM, SMEM, SMEM, VMEM, VMEM],
+        in_specs=[VMEM] * len(amps_of) + [SMEM, SMEM, VMEM, SMEM, SMEM, SMEM, VMEM, VMEM, HBM],
         out_specs=[VMEM] * 3,
         scratch_shapes=[
             pltpu.VMEM((ndev * per, npno, npno), jnp.bfloat16),
@@ -334,7 +344,7 @@
         compiler_params=params,
         cost_estimate=estimate(8 * COST),
     )(
-        *[blocks[m] for m in range(ndev)],
+        *[array for array, _ in amps_of],
         where,
         cpl_weight,
         intersections,
@@ -343,21 +353,22 @@
         occ_energy,
         pno_energy,
         amps,
+        late,
     )
 
     for mask in reversed(steps[:-1]):
         half = len(terms) // 2
-        keep, send = add_up([terms[:half], terms[half:]], [jnp.float32, SENT], [kept] if mask == steps[-2] else [])
+        keep, send = add_up([terms[:half], terms[half:]], [jnp.float32, SENT], [kept] if mask == top else [])
         send = swap(send, mask)
         terms = [[(keep, k), (send, k)] for k in range(half)]
 
     return pl.pallas_call(
         finish_kernel,
         out_shape=[jax.ShapeDtypeStruct((per, npno, npno), jnp.float32)] * 2,
-        in_specs=[VMEM] * 5,
+        in_specs=[VMEM] * 6,
         out_specs=[VMEM] * 2,
         compiler_params=params,
-    )(keep, send, kept, factor, live)
+    )(keep, send, final, kept, factor, live)
 
 
 def solution(mesh):

time: 60.1 us -> 57.2 us (0.952)
  starting transfers between devices: 21 us -> 19.2 us
  Pallas kernels: 22.2 us -> 21.5 us
    ppermute x24, starting transfers between devices: 21 us -> 19.2 us  [swap(): return lax.ppermute(array, 'pairs', [(d, d ^ mask) for d in range(ndev)])]
    pallas_call x5, Pallas kernels: 17.7 us -> 16.8 us  [exchange(): pl.pallas_call(functools.partial(exch_kernel, count, per, npno), out_shap...]
    unnamed x42 -> x24, local copies, waits for them, and re-layouts: 4.38 us -> 4.35 us
  transfers between devices with their start and end apart: 24 -> 24, of which waited for: 9 -> 7; matrix products, arithmetic and copies ran while one was open for 0% -> 0% of each run, Pallas kernels for 33% -> 33%
where the time goes in v3:
time: 57.2 us; the launch traced here: 57 us
  Pallas kernels  21.5 us (38%)
  starting transfers between devices  19.2 us (34%)
  waiting for transfers between devices  10.9 us (19%)
  local copies, waits for them, and re-layouts  4.35 us (8%)
  between operations  0.92 us (2%)
    ppermute x24, starting transfers between devices, swap(): return lax.ppermute(array, 'pairs', [(d, d ^ mask) for d in range(ndev)])  19.2 us
    pallas_call x5, Pallas kernels, exchange(): pl.pallas_call(functools.partial(exch_kernel, count, per, npno), out_shap...  16.8 us
    ppermute x24, waiting for transfers between devices, swap(): return lax.ppermute(array, 'pairs', [(d, d ^ mask) for d in range(ndev)])  10.9 us
    unnamed x24, local copies, waits for them, and re-layouts  4.35 us
    pallas_call x1, Pallas kernels, shards(): pl.pallas_call(functools.partial(coupled_kernel, [order for _, order in a...  1.91 us
    pallas_call x1, Pallas kernels, shards(): pl.pallas_call(pack_kernel, out_shape=[jax.ShapeDtypeStruct(((per + 1) *...  1.86 us
  transfers between devices with their start and end apart: 24, of which 7 were waited for; matrix products, arithmetic and copies ran while one was open for 0% of the time, Pallas kernels for 33%

profile of v3, /device:TPU:0, one launch (start us, length us, event | category | flops | bytes accessed | tf_op | source)
XLA Modules:
  0.0 57.0 jit_solution(5552707012522010769)
XLA Ops:
  0.6 1.9 %shard_map.122 = (bf16[336,256]{1,0:T(8,128)(2,1)}, bf16[336,256]{1,0:T(8,128)(2,1)}) custom-call(bf16[4,64,256]{2,1,0:T(8,128)(2,1)} %bitcast.4, s32[4,256]{1,0:T(4,128)} %dom_ref.1, s32[2,4]{1,0:T(2,128)} %bitcast.2, f32[4,64,64]{2,1,0:T(8,128)} %refs_12_.1), custom_call_target="tpu_custom_call" | custom-call | tf_op jit(solution)/shard_map/pallas_call | solution.py:206
  2.5 0.9 %copy-done.2 = bf16[336,256]{1,0:T(8,128)(2,1)S(1)} copy-done((bf16[336,256]{1,0:T(8,128)(2,1)S(1)}, bf16[336,256]{1,0:T(8,128)(2,1)}, u32[]{:S(2)}) %copy-start.2) | copy-done | bytes 172056
  3.4 3.0 %collective-permute-start.3 = (bf16[336,256]{1,0:T(8,128)(2,1)S(1)}, bf16[336,256]{1,0:T(8,128)(2,1)S(1)}, u32[]{:S(2)}, u32[]{:S(2)}) collective-permute-start(bf16[336,256]{1,0:T(8,128)(2,1)S(1)} %shard_map.123.refs_0_), channel_id=1, source_target_pairs={{0,4},{1,5},{2,6},{3,7},{4,0},{5,1},{6,2},{7,3},{8,12},{9,13},{10,... | collective-permute-start | bytes 516104 | tf_op jit(solution)/shard_map/ppermute | solution.py:204
  6.4 1.5 %collective-permute-start.2 = (bf16[336,256]{1,0:T(8,128)(2,1)S(1)}, bf16[336,256]{1,0:T(8,128)(2,1)S(1)}, u32[]{:S(2)}, u32[]{:S(2)}) collective-permute-start(bf16[336,256]{1,0:T(8,128)(2,1)S(1)} %shard_map.123.refs_0_), channel_id=1, source_target_pairs={{0,2},{1,3},{2,0},{3,1},{4,6},{5,7},{6,4},{7,5},{8,10},{9,11},{10,... | collective-permute-start | bytes 516104 | tf_op jit(solution)/shard_map/ppermute | solution.py:204
  8.0 2.6 %collective-permute-start.7 = (bf16[336,256]{1,0:T(8,128)(2,1)S(1)}, bf16[336,256]{1,0:T(8,128)(2,1)S(1)}, u32[]{:S(2)}, u32[]{:S(2)}) collective-permute-start(bf16[336,256]{1,0:T(8,128)(2,1)S(1)} %copy-done.11), channel_id=1, source_target_pairs={{0,8},{1,9},{2,10},{3,11},{4,12},{5,13},{6,14},{7,15},{8,0},{9,1},... | collective-permute-start | bytes 516104 | tf_op jit(solution)/shard_map/ppermute | solution.py:204
  10.8 1.7 %collective-permute-start.12 = (bf16[336,256]{1,0:T(8,128)(2,1)S(1)}, bf16[336,256]{1,0:T(8,128)(2,1)S(1)}, u32[]{:S(2)}, u32[]{:S(2)}) collective-permute-start(bf16[336,256]{1,0:T(8,128)(2,1)S(1)} %collective-permute-done.3.refs_1_), channel_id=1, source_target_pairs={{0,2},{1,3},{2,0},{3,1},{4,6},{5,7},{6,4},{7,5},{8,10},{9,11},{10,... | collective-permute-start | bytes 516104 | tf_op jit(solution)/shard_map/ppermute | solution.py:204
  13.0 2.5 %shard_map.124 = (f32[1,64,256]{2,1,0:T(8,128)S(1)}, f32[1,64,256]{2,1,0:T(8,128)S(1)}, bf16[2,64,256]{2,1,0:T(8,128)(2,1)S(1)}) custom-call(bf16[336,256]{1,0:T(8,128)(2,1)S(1)} %shard_map.123.refs_0_, bf16[336,256]{1,0:T(8,128)(2,1)S(1)} %collective-permute-done.refs_1_, bf16[32,1024,128]{2,1,0:T(8,128)(2,1)S(1)} %copy-done), custom_call_target="tpu_custom_call" | custom-call | bytes 1048576 | tf_op jit(solution)/shard_map/pallas_call | solution.py:259
  15.5 3.8 %collective-permute-done.7.refs_0_ = bf16[336,256]{1,0:T(8,128)(2,1)S(1)} collective-permute-done((bf16[336,256]{1,0:T(8,128)(2,1)S(1)}, bf16[336,256]{1,0:T(8,128)(2,1)S(1)}, u32[]{:S(2)}, u32[]{:S(2)}) %collective-permute-start.7) | collective-permute-done | bytes 172064 | tf_op jit(solution)/shard_map/ppermute | solution.py:204
  20.4 4.0 %shard_map.126 = (f32[2,64,256]{2,1,0:T(8,128)S(1)}, f32[2,64,256]{2,1,0:T(8,128)S(1)}, bf16[4,64,256]{2,1,0:T(8,128)(2,1)S(1)}) custom-call(bf16[336,256]{1,0:T(8,128)(2,1)S(1)} %collective-permute-done.2.refs_0_, bf16[336,256]{1,0:T(8,128)(2,1)S(1)} %collective-permute-done.3.refs_1_, bf16[336,256]{1,0:T(8,128)(2,1)S(1)} %collective-permute-done.4.refs_2_, ...), custom_call_target="tpu_custom_call" | custom-call | flops 4800000000 | bytes 1048576 | tf_op jit(solution)/shard_map/pallas_call | solution.py:259
  24.7 1.4 %collective-permute-done.9.refs_0_ = bf16[336,256]{1,0:T(8,128)(2,1)S(1)} collective-permute-done((bf16[336,256]{1,0:T(8,128)(2,1)S(1)}, bf16[336,256]{1,0:T(8,128)(2,1)S(1)}, u32[]{:S(2)}, u32[]{:S(2)}) %collective-permute-start.9) | collective-permute-done | bytes 172064 | tf_op jit(solution)/shard_map/ppermute | solution.py:204
  27.2 4.0 %shard_map.130 = (f32[2,64,256]{2,1,0:T(8,128)S(1)}, f32[2,64,256]{2,1,0:T(8,128)S(1)}, bf16[4,64,256]{2,1,0:T(8,128)(2,1)S(1)}) custom-call(bf16[336,256]{1,0:T(8,128)(2,1)S(1)} %collective-permute-done.12.refs_0_, bf16[336,256]{1,0:T(8,128)(2,1)S(1)} %shard_map.128.refs_1_, bf16[336,256]{1,0:T(8,128)(2,1)S(1)} %collective-permute-done.13.refs_2_, ...), custom_call_target="tpu_custom_call" | custom-call | flops 4800000000 | bytes 1048576 | tf_op jit(solution)/shard_map/pallas_call | solution.py:259
  31.3 0.8 %collective-permute-done.19.refs_0_ = bf16[336,256]{1,0:T(8,128)(2,1)S(1)} collective-permute-done((bf16[336,256]{1,0:T(8,128)(2,1)S(1)}, bf16[336,256]{1,0:T(8,128)(2,1)S(1)}, u32[]{:S(2)}, u32[]{:S(2)}) %collective-permute-start.19) | collective-permute-done | bytes 172064 | tf_op jit(solution)/shard_map/ppermute | solution.py:204
  32.1 4.0 %shard_map.131 = (f32[2,64,256]{2,1,0:T(8,128)S(1)}, f32[2,64,256]{2,1,0:T(8,128)S(1)}, bf16[4,64,256]{2,1,0:T(8,128)(2,1)S(1)}) custom-call(bf16[336,256]{1,0:T(8,128)(2,1)S(1)} %collective-permute-done.8.refs_0_, bf16[336,256]{1,0:T(8,128)(2,1)S(1)} %shard_map.129.refs_1_, bf16[336,256]{1,0:T(8,128)(2,1)S(1)} %collective-permute-done.10.refs_2_, ...), custom_call_target="tpu_custom_call" | custom-call | flops 4800000000 | bytes 1048576 | tf_op jit(solution)/shard_map/pallas_call | solution.py:259
  36.7 1.0 %collective-permute-done.15.refs_1_ = f32[2,64,256]{2,1,0:T(8,128)S(1)} collective-permute-done((f32[2,64,256]{2,1,0:T(8,128)S(1)}, f32[2,64,256]{2,1,0:T(8,128)S(1)}, u32[]{:S(2)}, u32[]{:S(2)}) %collective-permute-start.15) | collective-permute-done | bytes 131104 | tf_op jit(solution)/shard_map/ppermute | solution.py:204
  37.7 1.0 %collective-permute-start.17 = (bf16[3,64,256]{2,1,0:T(8,128)(2,1)S(1)}, bf16[3,64,256]{2,1,0:T(8,128)(2,1)S(1)}, u32[]{:S(2)}, u32[]{:S(2)}) collective-permute-start(bf16[3,64,256]{2,1,0:T(8,128)(2,1)S(1)} %shard_map.134), channel_id=1, source_target_pairs={{0,2},{1,3},{2,0},{3,1},{4,6},{5,7},{6,4},{7,5},{8,10},{9,11},{10,... | collective-permute-start | bytes 294920 | tf_op jit(solution)/shard_map/ppermute | solution.py:204
  38.7 3.4 %copy-done.1 = bf16[32,1024,128]{2,1,0:T(8,128)(2,1)S(1)} copy-done((bf16[32,1024,128]{2,1,0:T(8,128)(2,1)S(1)}, bf16[32,1024,128]{2,1,0:T(8,128)(2,1)}, u32[]{:S(2)}) %copy-start.1) | copy-done | bytes 8388632
  42.1 2.5 %shard_map.137 = (f32[1,64,256]{2,1,0:T(8,128)S(1)}, f32[1,64,256]{2,1,0:T(8,128)S(1)}, bf16[2,64,256]{2,1,0:T(8,128)(2,1)S(1)}) custom-call(bf16[336,256]{1,0:T(8,128)(2,1)S(1)} %shard_map.136.refs_0_, bf16[336,256]{1,0:T(8,128)(2,1)S(1)} %collective-permute-done.20.refs_1_, bf16[32,1024,128]{2,1,0:T(8,128)(2,1)S(1)} %copy-done.1, ...), custom_call_target="tpu_custom_call" | custom-call | flops 2400000000 | bytes 1048576 | tf_op jit(solution)/shard_map/pallas_call | solution.py:259
  44.8 1.9 %collective-permute-start.18 = (bf16[2,64,256]{2,1,0:T(8,128)(2,1)S(1)}, bf16[2,64,256]{2,1,0:T(8,128)(2,1)S(1)}, u32[]{:S(2)}, u32[]{:S(2)}) collective-permute-start(bf16[2,64,256]{2,1,0:T(8,128)(2,1)S(1)} %get-tuple-element.49), channel_id=1, source_target_pairs={{0,4},{1,5},{2,6},{3,7},{4,0},{5,1},{6,2},{7,3},{8,12},{9,13},{10,... | collective-permute-start | bytes 196616 | tf_op jit(solution)/shard_map/ppermute | solution.py:204
  46.7 2.6 %collective-permute-start.23 = (bf16[1,64,256]{2,1,0:T(8,128)(2,1)S(1)}, bf16[1,64,256]{2,1,0:T(8,128)(2,1)S(1)}, u32[]{:S(2)}, u32[]{:S(2)}) collective-permute-start(bf16[1,64,256]{2,1,0:T(8,128)(2,1)S(1)} %shard_map.139.refs_13_), channel_id=1, source_target_pairs={{0,14},{1,15},{2,12},{3,13},{4,10},{5,11},{6,8},{7,9},{8,6},{9,7},... | collective-permute-start | bytes 98312 | tf_op jit(solution)/shard_map/ppermute | solution.py:204
  49.3 1.9 %shard_map.140 = (f32[64,256]{1,0:T(8,128)S(1)}, f32[64,256]{1,0:T(8,128)S(1)}, f32[64,256]{1,0:T(8,128)S(1)}) custom-call(bf16[2,64,256]{2,1,0:T(8,128)(2,1)S(1)} %get-tuple-element.50.refs_0_, bf16[4,64,256]{2,1,0:T(8,128)(2,1)S(1)} %get-tuple-element.51.refs_1_, bf16[4,64,256]{2,1,0:T(8,128)(2,1)S(1)} %get-tuple-element.52.refs_2_, ...), custom_call_target="tpu_custom_call" | custom-call | flops 2400000000 | bytes 1048576 | tf_op jit(solution)/shard_map/pallas_call | solution.py:335
  51.3 1.3 %collective-permute-start.22 = (bf16[1,64,256]{2,1,0:T(8,128)(2,1)S(1)}, bf16[1,64,256]{2,1,0:T(8,128)(2,1)S(1)}, u32[]{:S(2)}, u32[]{:S(2)}) collective-permute-start(bf16[1,64,256]{2,1,0:T(8,128)(2,1)S(1)} %get-tuple-element.59), channel_id=1, source_target_pairs={{0,8},{1,9},{2,10},{3,11},{4,12},{5,13},{6,14},{7,15},{8,0},{9,1},... | collective-permute-start | bytes 98312 | tf_op jit(solution)/shard_map/ppermute | solution.py:204
  52.5 0.9 %collective-permute-done.23.late_ref = bf16[1,64,256]{2,1,0:T(8,128)(2,1)S(1)} collective-permute-done((bf16[1,64,256]{2,1,0:T(8,128)(2,1)S(1)}, bf16[1,64,256]{2,1,0:T(8,128)(2,1)S(1)}, u32[]{:S(2)}, u32[]{:S(2)}) %collective-permute-start.23) | collective-permute-done | bytes 32800 | tf_op jit(solution)/shard_map/ppermute | solution.py:204
  53.4 2.8 %collective-permute-done.22.came_ref = bf16[1,64,256]{2,1,0:T(8,128)(2,1)S(1)} collective-permute-done((bf16[1,64,256]{2,1,0:T(8,128)(2,1)S(1)}, bf16[1,64,256]{2,1,0:T(8,128)(2,1)S(1)}, u32[]{:S(2)}, u32[]{:S(2)}) %collective-permute-start.22) | collective-permute-done | bytes 32800 | tf_op jit(solution)/shard_map/ppermute | solution.py:204
  56.2 0.8 %shard_map.142 = (f32[4,64,64]{2,1,0:T(8,128)}, f32[4,64,64]{2,1,0:T(8,128)}) custom-call(f32[1,64,256]{2,1,0:T(8,128)S(1)} %get-tuple-element.58.own_ref, bf16[1,64,256]{2,1,0:T(8,128)(2,1)S(1)} %collective-permute-done.22.came_ref, bf16[1,64,256]{2,1,0:T(8,128)(2,1)S(1)} %collective-permute-done.23.late_ref, ...), custom_call_target="tpu_custom_call" | custom-call | tf_op jit(solution)/shard_map/pallas_call | solution.py:365
  (70 shorter events, 4.2 us)
Async XLA Ops:
  3.4 7.4 %collective-permute-start.3 = (bf16[336,256]{1,0:T(8,128)(2,1)S(1)}, bf16[336,256]{1,0:T(8,128)(2,1)S(1)}, u32[]{:S(2)}, u32[]{:S(2)}) collective-permute-start(bf16[336,256]{1,0:T(8,128)(2,1)S(1)} %shard_map.123.refs_0_), channel_id=1, source_target_pairs={{0,4},{1,5},{2,6},{3,7},{4,0},{5,1},{6,2},{7,3},{8,12},{9,13},{10,... | collective-permute-start | bytes 516104 | tf_op jit(solution)/shard_map/ppermute | solution.py:204
  6.4 6.1 %collective-permute-start.2 = (bf16[336,256]{1,0:T(8,128)(2,1)S(1)}, bf16[336,256]{1,0:T(8,128)(2,1)S(1)}, u32[]{:S(2)}, u32[]{:S(2)}) collective-permute-start(bf16[336,256]{1,0:T(8,128)(2,1)S(1)} %shard_map.123.refs_0_), channel_id=1, source_target_pairs={{0,2},{1,3},{2,0},{3,1},{4,6},{5,7},{6,4},{7,5},{8,10},{9,11},{10,... | collective-permute-start | bytes 516104 | tf_op jit(solution)/shard_map/ppermute | solution.py:204
  8.0 5.1 %collective-permute-start = (bf16[336,256]{1,0:T(8,128)(2,1)S(1)}, bf16[336,256]{1,0:T(8,128)(2,1)S(1)}, u32[]{:S(2)}, u32[]{:S(2)}) collective-permute-start(bf16[336,256]{1,0:T(8,128)(2,1)S(1)} %shard_map.123.refs_0_), channel_id=1, source_target_pairs={{0,1},{1,0},{2,3},{3,2},{4,5},{5,4},{6,7},{7,6},{8,9},{9,8},{10,11... | collective-permute-start | bytes 516104 | tf_op jit(solution)/shard_map/ppermute | solution.py:204
  8.0 11.3 %collective-permute-start.7 = (bf16[336,256]{1,0:T(8,128)(2,1)S(1)}, bf16[336,256]{1,0:T(8,128)(2,1)S(1)}, u32[]{:S(2)}, u32[]{:S(2)}) collective-permute-start(bf16[336,256]{1,0:T(8,128)(2,1)S(1)} %copy-done.11), channel_id=1, source_target_pairs={{0,8},{1,9},{2,10},{3,11},{4,12},{5,13},{6,14},{7,15},{8,0},{9,1},... | collective-permute-start | bytes 516104 | tf_op jit(solution)/shard_map/ppermute | solution.py:204
  10.8 8.5 %collective-permute-start.12 = (bf16[336,256]{1,0:T(8,128)(2,1)S(1)}, bf16[336,256]{1,0:T(8,128)(2,1)S(1)}, u32[]{:S(2)}, u32[]{:S(2)}) collective-permute-start(bf16[336,256]{1,0:T(8,128)(2,1)S(1)} %collective-permute-done.3.refs_1_), channel_id=1, source_target_pairs={{0,2},{1,3},{2,0},{3,1},{4,6},{5,7},{6,4},{7,5},{8,10},{9,11},{10,... | collective-permute-start | bytes 516104 | tf_op jit(solution)/shard_map/ppermute | solution.py:204
  12.5 7.4 %collective-permute-start.5 = (bf16[336,256]{1,0:T(8,128)(2,1)S(1)}, bf16[336,256]{1,0:T(8,128)(2,1)S(1)}, u32[]{:S(2)}, u32[]{:S(2)}) collective-permute-start(bf16[336,256]{1,0:T(8,128)(2,1)S(1)} %collective-permute-done.3.refs_1_), channel_id=1, source_target_pairs={{0,1},{1,0},{2,3},{3,2},{4,5},{5,4},{6,7},{7,6},{8,9},{9,8},{10,11... | collective-permute-start | bytes 516104 | tf_op jit(solution)/shard_map/ppermute | solution.py:204
  12.5 7.6 %collective-permute-start.4 = (bf16[336,256]{1,0:T(8,128)(2,1)S(1)}, bf16[336,256]{1,0:T(8,128)(2,1)S(1)}, u32[]{:S(2)}, u32[]{:S(2)}) collective-permute-start(bf16[336,256]{1,0:T(8,128)(2,1)S(1)} %collective-permute-done.2.refs_0_), channel_id=1, source_target_pairs={{0,1},{1,0},{2,3},{3,2},{4,5},{5,4},{6,7},{7,6},{8,9},{9,8},{10,11... | collective-permute-start | bytes 516104 | tf_op jit(solution)/shard_map/ppermute | solution.py:204
  19.3 7.9 %collective-permute-start.14 = (bf16[336,256]{1,0:T(8,128)(2,1)S(1)}, bf16[336,256]{1,0:T(8,128)(2,1)S(1)}, u32[]{:S(2)}, u32[]{:S(2)}) collective-permute-start(bf16[336,256]{1,0:T(8,128)(2,1)S(1)} %shard_map.128.refs_1_), channel_id=1, source_target_pairs={{0,1},{1,0},{2,3},{3,2},{4,5},{5,4},{6,7},{7,6},{8,9},{9,8},{10,11... | collective-permute-start | bytes 516104 | tf_op jit(solution)/shard_map/ppermute | solution.py:204
  19.3 6.8 %collective-permute-start.9 = (bf16[336,256]{1,0:T(8,128)(2,1)S(1)}, bf16[336,256]{1,0:T(8,128)(2,1)S(1)}, u32[]{:S(2)}, u32[]{:S(2)}) collective-permute-start(bf16[336,256]{1,0:T(8,128)(2,1)S(1)} %shard_map.128.refs_1_), channel_id=1, source_target_pairs={{0,4},{1,5},{2,6},{3,7},{4,0},{5,1},{6,2},{7,3},{8,12},{9,13},{10,... | collective-permute-start | bytes 516104 | tf_op jit(solution)/shard_map/ppermute | solution.py:204
  19.3 7.3 %collective-permute-start.8 = (bf16[336,256]{1,0:T(8,128)(2,1)S(1)}, bf16[336,256]{1,0:T(8,128)(2,1)S(1)}, u32[]{:S(2)}, u32[]{:S(2)}) collective-permute-start(bf16[336,256]{1,0:T(8,128)(2,1)S(1)} %shard_map.128.refs_1_), channel_id=1, source_target_pairs={{0,2},{1,3},{2,0},{3,1},{4,6},{5,7},{6,4},{7,5},{8,10},{9,11},{10,... | collective-permute-start | bytes 516104 | tf_op jit(solution)/shard_map/ppermute | solution.py:204
  19.9 4.5 %collective-permute-start.1 = (f32[1,64,256]{2,1,0:T(8,128)S(1)}, f32[1,64,256]{2,1,0:T(8,128)S(1)}, u32[]{:S(2)}, u32[]{:S(2)}) collective-permute-start(f32[1,64,256]{2,1,0:T(8,128)S(1)} %get-tuple-element.34), channel_id=1, source_target_pairs={{0,1},{1,0},{2,3},{3,2},{4,5},{5,4},{6,7},{7,6},{8,9},{9,8},{10,11... | collective-permute-start | bytes 196616 | tf_op jit(solution)/shard_map/ppermute | solution.py:204
  20.1 7.1 %collective-permute-start.13 = (bf16[336,256]{1,0:T(8,128)(2,1)S(1)}, bf16[336,256]{1,0:T(8,128)(2,1)S(1)}, u32[]{:S(2)}, u32[]{:S(2)}) collective-permute-start(bf16[336,256]{1,0:T(8,128)(2,1)S(1)} %collective-permute-done.12.refs_0_), channel_id=1, source_target_pairs={{0,1},{1,0},{2,3},{3,2},{4,5},{5,4},{6,7},{7,6},{8,9},{9,8},{10,11... | collective-permute-start | bytes 516104 | tf_op jit(solution)/shard_map/ppermute | solution.py:204
  24.4 2.2 %collective-permute-start.6 = (f32[2,64,256]{2,1,0:T(8,128)S(1)}, f32[2,64,256]{2,1,0:T(8,128)S(1)}, u32[]{:S(2)}, u32[]{:S(2)}) collective-permute-start(f32[2,64,256]{2,1,0:T(8,128)S(1)} %get-tuple-element.36), channel_id=1, source_target_pairs={{0,1},{1,0},{2,3},{3,2},{4,5},{5,4},{6,7},{7,6},{8,9},{9,8},{10,11... | collective-permute-start | bytes 393224 | tf_op jit(solution)/shard_map/ppermute | solution.py:204
  26.1 6.0 %collective-permute-start.19 = (bf16[336,256]{1,0:T(8,128)(2,1)S(1)}, bf16[336,256]{1,0:T(8,128)(2,1)S(1)}, u32[]{:S(2)}, u32[]{:S(2)}) collective-permute-start(bf16[336,256]{1,0:T(8,128)(2,1)S(1)} %shard_map.129.refs_1_), channel_id=1, source_target_pairs={{0,2},{1,3},{2,0},{3,1},{4,6},{5,7},{6,4},{7,5},{8,10},{9,11},{10,... | collective-permute-start | bytes 516104 | tf_op jit(solution)/shard_map/ppermute | solution.py:204
  26.6 5.5 %collective-permute-start.11 = (bf16[336,256]{1,0:T(8,128)(2,1)S(1)}, bf16[336,256]{1,0:T(8,128)(2,1)S(1)}, u32[]{:S(2)}, u32[]{:S(2)}) collective-permute-start(bf16[336,256]{1,0:T(8,128)(2,1)S(1)} %shard_map.129.refs_1_), channel_id=1, source_target_pairs={{0,1},{1,0},{2,3},{3,2},{4,5},{5,4},{6,7},{7,6},{8,9},{9,8},{10,11... | collective-permute-start | bytes 516104 | tf_op jit(solution)/shard_map/ppermute | solution.py:204
  26.7 5.5 %collective-permute-start.10 = (bf16[336,256]{1,0:T(8,128)(2,1)S(1)}, bf16[336,256]{1,0:T(8,128)(2,1)S(1)}, u32[]{:S(2)}, u32[]{:S(2)}) collective-permute-start(bf16[336,256]{1,0:T(8,128)(2,1)S(1)} %collective-permute-done.8.refs_0_), channel_id=1, source_target_pairs={{0,1},{1,0},{2,3},{3,2},{4,5},{5,4},{6,7},{7,6},{8,9},{9,8},{10,11... | collective-permute-start | bytes 516104 | tf_op jit(solution)/shard_map/ppermute | solution.py:204
  31.2 5.5 %collective-permute-start.16 = (f32[2,64,256]{2,1,0:T(8,128)S(1)}, f32[2,64,256]{2,1,0:T(8,128)S(1)}, u32[]{:S(2)}, u32[]{:S(2)}) collective-permute-start(f32[2,64,256]{2,1,0:T(8,128)S(1)} %get-tuple-element.44), channel_id=1, source_target_pairs={{0,1},{1,0},{2,3},{3,2},{4,5},{5,4},{6,7},{7,6},{8,9},{9,8},{10,11... | collective-permute-start | bytes 393224 | tf_op jit(solution)/shard_map/ppermute | solution.py:204
  32.1 6.6 %collective-permute-start.20 = (bf16[336,256]{1,0:T(8,128)(2,1)S(1)}, bf16[336,256]{1,0:T(8,128)(2,1)S(1)}, u32[]{:S(2)}, u32[]{:S(2)}) collective-permute-start(bf16[336,256]{1,0:T(8,128)(2,1)S(1)} %shard_map.136.refs_0_), channel_id=1, source_target_pairs={{0,1},{1,0},{2,3},{3,2},{4,5},{5,4},{6,7},{7,6},{8,9},{9,8},{10,11... | collective-permute-start | bytes 516104 | tf_op jit(solution)/shard_map/ppermute | solution.py:204
  36.1 1.6 %collective-permute-start.15 = (f32[2,64,256]{2,1,0:T(8,128)S(1)}, f32[2,64,256]{2,1,0:T(8,128)S(1)}, u32[]{:S(2)}, u32[]{:S(2)}) collective-permute-start(f32[2,64,256]{2,1,0:T(8,128)S(1)} %get-tuple-element.42), channel_id=1, source_target_pairs={{0,1},{1,0},{2,3},{3,2},{4,5},{5,4},{6,7},{7,6},{8,9},{9,8},{10,11... | collective-permute-start | bytes 393224 | tf_op jit(solution)/shard_map/ppermute | solution.py:204
  37.7 7.0 %collective-permute-start.17 = (bf16[3,64,256]{2,1,0:T(8,128)(2,1)S(1)}, bf16[3,64,256]{2,1,0:T(8,128)(2,1)S(1)}, u32[]{:S(2)}, u32[]{:S(2)}) collective-permute-start(bf16[3,64,256]{2,1,0:T(8,128)(2,1)S(1)} %shard_map.134), channel_id=1, source_target_pairs={{0,2},{1,3},{2,0},{3,1},{4,6},{5,7},{6,4},{7,5},{8,10},{9,11},{10,... | collective-permute-start | bytes 294920 | tf_op jit(solution)/shard_map/ppermute | solution.py:204
  44.6 2.0 %collective-permute-start.21 = (f32[1,64,256]{2,1,0:T(8,128)S(1)}, f32[1,64,256]{2,1,0:T(8,128)S(1)}, u32[]{:S(2)}, u32[]{:S(2)}) collective-permute-start(f32[1,64,256]{2,1,0:T(8,128)S(1)} %get-tuple-element.56), channel_id=1, source_target_pairs={{0,1},{1,0},{2,3},{3,2},{4,5},{5,4},{6,7},{7,6},{8,9},{9,8},{10,11... | collective-permute-start | bytes 196616 | tf_op jit(solution)/shard_map/ppermute | solution.py:204
  44.8 6.5 %collective-permute-start.18 = (bf16[2,64,256]{2,1,0:T(8,128)(2,1)S(1)}, bf16[2,64,256]{2,1,0:T(8,128)(2,1)S(1)}, u32[]{:S(2)}, u32[]{:S(2)}) collective-permute-start(bf16[2,64,256]{2,1,0:T(8,128)(2,1)S(1)} %get-tuple-element.49), channel_id=1, source_target_pairs={{0,4},{1,5},{2,6},{3,7},{4,0},{5,1},{6,2},{7,3},{8,12},{9,13},{10,... | collective-permute-start | bytes 196616 | tf_op jit(solution)/shard_map/ppermute | solution.py:204
  46.7 6.7 %collective-permute-start.23 = (bf16[1,64,256]{2,1,0:T(8,128)(2,1)S(1)}, bf16[1,64,256]{2,1,0:T(8,128)(2,1)S(1)}, u32[]{:S(2)}, u32[]{:S(2)}) collective-permute-start(bf16[1,64,256]{2,1,0:T(8,128)(2,1)S(1)} %shard_map.139.refs_13_), channel_id=1, source_target_pairs={{0,14},{1,15},{2,12},{3,13},{4,10},{5,11},{6,8},{7,9},{8,6},{9,7},... | collective-permute-start | bytes 98312 | tf_op jit(solution)/shard_map/ppermute | solution.py:204
  51.3 4.9 %collective-permute-start.22 = (bf16[1,64,256]{2,1,0:T(8,128)(2,1)S(1)}, bf16[1,64,256]{2,1,0:T(8,128)(2,1)S(1)}, u32[]{:S(2)}, u32[]{:S(2)}) collective-permute-start(bf16[1,64,256]{2,1,0:T(8,128)(2,1)S(1)} %get-tuple-element.59), channel_id=1, source_target_pairs={{0,8},{1,9},{2,10},{3,11},{4,12},{5,13},{6,14},{7,15},{8,0},{9,1},... | collective-permute-start | bytes 98312 | tf_op jit(solution)/shard_map/ppermute | solution.py:204
  (12 other events, 45.5 us)

commit v4 on v3

--- a/solution.py
+++ b/solution.py
@@ -324,11 +324,16 @@
 
     ready = add_up([[[mine[m]] for m in far[:-1]]], [SENT])[0]
     final = gate(mine[far[-1]][0], (), 32 * COST)
-    late = final
     terms = [[mine[m]] for m in own]
     ready, final = swap(ready, last), swap(final, far[-1])
     for k in range(len(own) - 1):
         terms[k].append((ready, k))
+
+    for mask in reversed(steps[:-1]):
+        half = len(terms) // 2
+        keep, send = add_up([terms[:half], terms[half:]], [jnp.float32, SENT])
+        send = swap(send, mask)
+        terms = [[(keep, k), (send, k)] for k in range(half)]
 
     away = jnp.bitwise_xor(cpl_pair // per, me)
     where = away * per + cpl_pair % per
@@ -353,14 +358,8 @@
         occ_energy,
         pno_energy,
         amps,
-        late,
+        keep,
     )
-
-    for mask in reversed(steps[:-1]):
-        half = len(terms) // 2
-        keep, send = add_up([terms[:half], terms[half:]], [jnp.float32, SENT], [kept] if mask == top else [])
-        send = swap(send, mask)
-        terms = [[(keep, k), (send, k)] for k in range(half)]
 
     return pl.pallas_call(
         finish_kernel,

time: 57.2 us -> 55.5 us (0.970)
  waiting for transfers between devices: 10.9 us -> 7.35 us
  starting transfers between devices: 19.2 us -> 21.1 us
    ppermute x24, waiting for transfers between devices: 10.9 us -> 7.35 us  [swap(): return lax.ppermute(array, 'pairs', [(d, d ^ mask) for d in range(ndev)])]
    ppermute x24, starting transfers between devices: 19.2 us -> 21.1 us  [swap(): return lax.ppermute(array, 'pairs', [(d, d ^ mask) for d in range(ndev)])]
  transfers between devices with their start and end apart: 24 -> 24, of which waited for: 7 -> 5; matrix products, arithmetic and copies ran while one was open for 0% -> 0% of each run, Pallas kernels for 33% -> 34%
where the time goes in v4:
time: 55.5 us; the launch traced here: 55.3 us
  Pallas kernels  21.5 us (39%)
  starting transfers between devices  21.1 us (38%)
  waiting for transfers between devices  7.35 us (13%)
  local copies, waits for them, and re-layouts  4.35 us (8%)
  between operations  0.93 us (2%)
    ppermute x24, starting transfers between devices, swap(): return lax.ppermute(array, 'pairs', [(d, d ^ mask) for d in range(ndev)])  21.1 us
    pallas_call x5, Pallas kernels, exchange(): pl.pallas_call(functools.partial(exch_kernel, count, per, npno), out_shap...  16.8 us
    ppermute x24, waiting for transfers between devices, swap(): return lax.ppermute(array, 'pairs', [(d, d ^ mask) for d in range(ndev)])  7.35 us
    unnamed x24, local copies, waits for them, and re-layouts  4.35 us
    pallas_call x1, Pallas kernels, shards(): pl.pallas_call(functools.partial(coupled_kernel, [order for _, order in a...  1.91 us
    pallas_call x1, Pallas kernels, shards(): pl.pallas_call(pack_kernel, out_shape=[jax.ShapeDtypeStruct(((per + 1) *...  1.86 us
  transfers between devices with their start and end apart: 24, of which 5 were waited for; matrix products, arithmetic and copies ran while one was open for 0% of the time, Pallas kernels for 34%

profile of v4, /device:TPU:0, one launch (start us, length us, event | category | flops | bytes accessed | tf_op | source)
XLA Modules:
  0.0 55.3 jit_solution(7000771335577294315)
XLA Ops:
  0.6 1.9 %shard_map.122 = (bf16[336,256]{1,0:T(8,128)(2,1)}, bf16[336,256]{1,0:T(8,128)(2,1)}) custom-call(bf16[4,64,256]{2,1,0:T(8,128)(2,1)} %bitcast.4, s32[4,256]{1,0:T(4,128)} %dom_ref.1, s32[2,4]{1,0:T(2,128)} %bitcast.2, f32[4,64,64]{2,1,0:T(8,128)} %refs_12_.1), custom_call_target="tpu_custom_call" | custom-call | tf_op jit(solution)/shard_map/pallas_call | solution.py:206
  2.5 0.9 %copy-done.2 = bf16[336,256]{1,0:T(8,128)(2,1)S(1)} copy-done((bf16[336,256]{1,0:T(8,128)(2,1)S(1)}, bf16[336,256]{1,0:T(8,128)(2,1)}, u32[]{:S(2)}) %copy-start.2) | copy-done | bytes 172056
  3.4 3.0 %collective-permute-start.3 = (bf16[336,256]{1,0:T(8,128)(2,1)S(1)}, bf16[336,256]{1,0:T(8,128)(2,1)S(1)}, u32[]{:S(2)}, u32[]{:S(2)}) collective-permute-start(bf16[336,256]{1,0:T(8,128)(2,1)S(1)} %shard_map.123.refs_0_), channel_id=1, source_target_pairs={{0,4},{1,5},{2,6},{3,7},{4,0},{5,1},{6,2},{7,3},{8,12},{9,13},{10,... | collective-permute-start | bytes 516104 | tf_op jit(solution)/shard_map/ppermute | solution.py:204
  6.4 1.5 %collective-permute-start.2 = (bf16[336,256]{1,0:T(8,128)(2,1)S(1)}, bf16[336,256]{1,0:T(8,128)(2,1)S(1)}, u32[]{:S(2)}, u32[]{:S(2)}) collective-permute-start(bf16[336,256]{1,0:T(8,128)(2,1)S(1)} %shard_map.123.refs_0_), channel_id=1, source_target_pairs={{0,2},{1,3},{2,0},{3,1},{4,6},{5,7},{6,4},{7,5},{8,10},{9,11},{10,... | collective-permute-start | bytes 516104 | tf_op jit(solution)/shard_map/ppermute | solution.py:204
  8.0 2.6 %collective-permute-start.7 = (bf16[336,256]{1,0:T(8,128)(2,1)S(1)}, bf16[336,256]{1,0:T(8,128)(2,1)S(1)}, u32[]{:S(2)}, u32[]{:S(2)}) collective-permute-start(bf16[336,256]{1,0:T(8,128)(2,1)S(1)} %copy-done.11), channel_id=1, source_target_pairs={{0,8},{1,9},{2,10},{3,11},{4,12},{5,13},{6,14},{7,15},{8,0},{9,1},... | collective-permute-start | bytes 516104 | tf_op jit(solution)/shard_map/ppermute | solution.py:204
  10.8 1.7 %collective-permute-start.12 = (bf16[336,256]{1,0:T(8,128)(2,1)S(1)}, bf16[336,256]{1,0:T(8,128)(2,1)S(1)}, u32[]{:S(2)}, u32[]{:S(2)}) collective-permute-start(bf16[336,256]{1,0:T(8,128)(2,1)S(1)} %collective-permute-done.3.refs_1_), channel_id=1, source_target_pairs={{0,2},{1,3},{2,0},{3,1},{4,6},{5,7},{6,4},{7,5},{8,10},{9,11},{10,... | collective-permute-start | bytes 516104 | tf_op jit(solution)/shard_map/ppermute | solution.py:204
  13.0 2.5 %shard_map.124 = (f32[1,64,256]{2,1,0:T(8,128)S(1)}, f32[1,64,256]{2,1,0:T(8,128)S(1)}, bf16[2,64,256]{2,1,0:T(8,128)(2,1)S(1)}) custom-call(bf16[336,256]{1,0:T(8,128)(2,1)S(1)} %shard_map.123.refs_0_, bf16[336,256]{1,0:T(8,128)(2,1)S(1)} %collective-permute-done.refs_1_, bf16[32,1024,128]{2,1,0:T(8,128)(2,1)S(1)} %copy-done), custom_call_target="tpu_custom_call" | custom-call | bytes 1048576 | tf_op jit(solution)/shard_map/pallas_call | solution.py:259
  15.5 3.8 %collective-permute-done.7.refs_0_ = bf16[336,256]{1,0:T(8,128)(2,1)S(1)} collective-permute-done((bf16[336,256]{1,0:T(8,128)(2,1)S(1)}, bf16[336,256]{1,0:T(8,128)(2,1)S(1)}, u32[]{:S(2)}, u32[]{:S(2)}) %collective-permute-start.7) | collective-permute-done | bytes 172064 | tf_op jit(solution)/shard_map/ppermute | solution.py:204
  19.3 0.6 %collective-permute-start.8 = (bf16[336,256]{1,0:T(8,128)(2,1)S(1)}, bf16[336,256]{1,0:T(8,128)(2,1)S(1)}, u32[]{:S(2)}, u32[]{:S(2)}) collective-permute-start(bf16[336,256]{1,0:T(8,128)(2,1)S(1)} %shard_map.128.refs_1_), channel_id=1, source_target_pairs={{0,2},{1,3},{2,0},{3,1},{4,6},{5,7},{6,4},{7,5},{8,10},{9,11},{10,... | collective-permute-start | bytes 516104 | tf_op jit(solution)/shard_map/ppermute | solution.py:204
  20.4 4.0 %shard_map.126 = (f32[2,64,256]{2,1,0:T(8,128)S(1)}, f32[2,64,256]{2,1,0:T(8,128)S(1)}, bf16[4,64,256]{2,1,0:T(8,128)(2,1)S(1)}) custom-call(bf16[336,256]{1,0:T(8,128)(2,1)S(1)} %collective-permute-done.2.refs_0_, bf16[336,256]{1,0:T(8,128)(2,1)S(1)} %collective-permute-done.3.refs_1_, bf16[336,256]{1,0:T(8,128)(2,1)S(1)} %collective-permute-done.4.refs_2_, ...), custom_call_target="tpu_custom_call" | custom-call | flops 4800000000 | bytes 1048576 | tf_op jit(solution)/shard_map/pallas_call | solution.py:259
  24.7 1.4 %collective-permute-done.9.refs_0_ = bf16[336,256]{1,0:T(8,128)(2,1)S(1)} collective-permute-done((bf16[336,256]{1,0:T(8,128)(2,1)S(1)}, bf16[336,256]{1,0:T(8,128)(2,1)S(1)}, u32[]{:S(2)}, u32[]{:S(2)}) %collective-permute-start.9) | collective-permute-done | bytes 172064 | tf_op jit(solution)/shard_map/ppermute | solution.py:204
  27.2 4.0 %shard_map.130 = (f32[2,64,256]{2,1,0:T(8,128)S(1)}, f32[2,64,256]{2,1,0:T(8,128)S(1)}, bf16[4,64,256]{2,1,0:T(8,128)(2,1)S(1)}) custom-call(bf16[336,256]{1,0:T(8,128)(2,1)S(1)} %collective-permute-done.12.refs_0_, bf16[336,256]{1,0:T(8,128)(2,1)S(1)} %shard_map.128.refs_1_, bf16[336,256]{1,0:T(8,128)(2,1)S(1)} %collective-permute-done.13.refs_2_, ...), custom_call_target="tpu_custom_call" | custom-call | flops 4800000000 | bytes 1048576 | tf_op jit(solution)/shard_map/pallas_call | solution.py:259
  31.3 0.8 %collective-permute-done.20.refs_0_ = bf16[336,256]{1,0:T(8,128)(2,1)S(1)} collective-permute-done((bf16[336,256]{1,0:T(8,128)(2,1)S(1)}, bf16[336,256]{1,0:T(8,128)(2,1)S(1)}, u32[]{:S(2)}, u32[]{:S(2)}) %collective-permute-start.20) | collective-permute-done | bytes 172064 | tf_op jit(solution)/shard_map/ppermute | solution.py:204
  32.1 4.0 %shard_map.131 = (f32[2,64,256]{2,1,0:T(8,128)S(1)}, f32[2,64,256]{2,1,0:T(8,128)S(1)}, bf16[4,64,256]{2,1,0:T(8,128)(2,1)S(1)}) custom-call(bf16[336,256]{1,0:T(8,128)(2,1)S(1)} %collective-permute-done.8.refs_0_, bf16[336,256]{1,0:T(8,128)(2,1)S(1)} %shard_map.129.refs_1_, bf16[336,256]{1,0:T(8,128)(2,1)S(1)} %collective-permute-done.10.refs_2_, ...), custom_call_target="tpu_custom_call" | custom-call | flops 4800000000 | bytes 1048576 | tf_op jit(solution)/shard_map/pallas_call | solution.py:259
  36.1 0.6 %collective-permute-start.15 = (f32[2,64,256]{2,1,0:T(8,128)S(1)}, f32[2,64,256]{2,1,0:T(8,128)S(1)}, u32[]{:S(2)}, u32[]{:S(2)}) collective-permute-start(f32[2,64,256]{2,1,0:T(8,128)S(1)} %get-tuple-element.42), channel_id=1, source_target_pairs={{0,1},{1,0},{2,3},{3,2},{4,5},{5,4},{6,7},{7,6},{8,9},{9,8},{10,11... | collective-permute-start | bytes 393224 | tf_op jit(solution)/shard_map/ppermute | solution.py:204
  36.7 1.0 %collective-permute-done.15.refs_1_ = f32[2,64,256]{2,1,0:T(8,128)S(1)} collective-permute-done((f32[2,64,256]{2,1,0:T(8,128)S(1)}, f32[2,64,256]{2,1,0:T(8,128)S(1)}, u32[]{:S(2)}, u32[]{:S(2)}) %collective-permute-start.15) | collective-permute-done | bytes 131104 | tf_op jit(solution)/shard_map/ppermute | solution.py:204
  37.7 1.0 %collective-permute-start.17 = (bf16[3,64,256]{2,1,0:T(8,128)(2,1)S(1)}, bf16[3,64,256]{2,1,0:T(8,128)(2,1)S(1)}, u32[]{:S(2)}, u32[]{:S(2)}) collective-permute-start(bf16[3,64,256]{2,1,0:T(8,128)(2,1)S(1)} %shard_map.134), channel_id=1, source_target_pairs={{0,2},{1,3},{2,0},{3,1},{4,6},{5,7},{6,4},{7,5},{8,10},{9,11},{10,... | collective-permute-start | bytes 294920 | tf_op jit(solution)/shard_map/ppermute | solution.py:204
  38.7 3.4 %copy-done.1 = bf16[32,1024,128]{2,1,0:T(8,128)(2,1)S(1)} copy-done((bf16[32,1024,128]{2,1,0:T(8,128)(2,1)S(1)}, bf16[32,1024,128]{2,1,0:T(8,128)(2,1)}, u32[]{:S(2)}) %copy-start.1) | copy-done | bytes 8388632
  42.1 2.5 %shard_map.138 = (f32[1,64,256]{2,1,0:T(8,128)S(1)}, f32[1,64,256]{2,1,0:T(8,128)S(1)}, bf16[2,64,256]{2,1,0:T(8,128)(2,1)S(1)}) custom-call(bf16[336,256]{1,0:T(8,128)(2,1)S(1)} %shard_map.137.refs_0_, bf16[336,256]{1,0:T(8,128)(2,1)S(1)} %collective-permute-done.21.refs_1_, bf16[32,1024,128]{2,1,0:T(8,128)(2,1)S(1)} %copy-done.1, ...), custom_call_target="tpu_custom_call" | custom-call | flops 2400000000 | bytes 1048576 | tf_op jit(solution)/shard_map/pallas_call | solution.py:259
  44.8 1.9 %collective-permute-start.18 = (bf16[2,64,256]{2,1,0:T(8,128)(2,1)S(1)}, bf16[2,64,256]{2,1,0:T(8,128)(2,1)S(1)}, u32[]{:S(2)}, u32[]{:S(2)}) collective-permute-start(bf16[2,64,256]{2,1,0:T(8,128)(2,1)S(1)} %get-tuple-element.49), channel_id=1, source_target_pairs={{0,4},{1,5},{2,6},{3,7},{4,0},{5,1},{6,2},{7,3},{8,12},{9,13},{10,... | collective-permute-start | bytes 196616 | tf_op jit(solution)/shard_map/ppermute | solution.py:204
  46.7 2.6 %collective-permute-start.23 = (bf16[1,64,256]{2,1,0:T(8,128)(2,1)S(1)}, bf16[1,64,256]{2,1,0:T(8,128)(2,1)S(1)}, u32[]{:S(2)}, u32[]{:S(2)}) collective-permute-start(bf16[1,64,256]{2,1,0:T(8,128)(2,1)S(1)} %shard_map.140), channel_id=1, source_target_pairs={{0,14},{1,15},{2,12},{3,13},{4,10},{5,11},{6,8},{7,9},{8,6},{9,7},... | collective-permute-start | bytes 98312 | tf_op jit(solution)/shard_map/ppermute | solution.py:204
  49.3 3.2 %collective-permute-start.19 = (bf16[1,64,256]{2,1,0:T(8,128)(2,1)S(1)}, bf16[1,64,256]{2,1,0:T(8,128)(2,1)S(1)}, u32[]{:S(2)}, u32[]{:S(2)}) collective-permute-start(bf16[1,64,256]{2,1,0:T(8,128)(2,1)S(1)} %get-tuple-element.51), channel_id=1, source_target_pairs={{0,8},{1,9},{2,10},{3,11},{4,12},{5,13},{6,14},{7,15},{8,0},{9,1},... | collective-permute-start | bytes 98312 | tf_op jit(solution)/shard_map/ppermute | solution.py:204
  52.6 1.9 %shard_map.141 = (f32[64,256]{1,0:T(8,128)S(1)}, f32[64,256]{1,0:T(8,128)S(1)}, f32[64,256]{1,0:T(8,128)S(1)}) custom-call(bf16[2,64,256]{2,1,0:T(8,128)(2,1)S(1)} %get-tuple-element.54.refs_0_, bf16[4,64,256]{2,1,0:T(8,128)(2,1)S(1)} %get-tuple-element.55.refs_1_, bf16[4,64,256]{2,1,0:T(8,128)(2,1)S(1)} %get-tuple-element.56.refs_2_, ...), custom_call_target="tpu_custom_call" | custom-call | flops 2400000000 | bytes 1048576 | tf_op jit(solution)/shard_map/pallas_call | solution.py:340
  54.5 0.8 %shard_map.142 = (f32[4,64,64]{2,1,0:T(8,128)}, f32[4,64,64]{2,1,0:T(8,128)}) custom-call(f32[1,64,256]{2,1,0:T(8,128)S(1)} %get-tuple-element.50.refs_13_.own_ref, bf16[1,64,256]{2,1,0:T(8,128)(2,1)S(1)} %collective-permute-done.19.came_ref, bf16[1,64,256]{2,1,0:T(8,128)(2,1)S(1)} %collective-permute-done.23.late_ref, ...), custom_call_target="tpu_custom_call" | custom-call | tf_op jit(solution)/shard_map/pallas_call | solution.py:364
  (70 shorter events, 3.0 us)
Async XLA Ops:
  3.4 7.4 %collective-permute-start.3 = (bf16[336,256]{1,0:T(8,128)(2,1)S(1)}, bf16[336,256]{1,0:T(8,128)(2,1)S(1)}, u32[]{:S(2)}, u32[]{:S(2)}) collective-permute-start(bf16[336,256]{1,0:T(8,128)(2,1)S(1)} %shard_map.123.refs_0_), channel_id=1, source_target_pairs={{0,4},{1,5},{2,6},{3,7},{4,0},{5,1},{6,2},{7,3},{8,12},{9,13},{10,... | collective-permute-start | bytes 516104 | tf_op jit(solution)/shard_map/ppermute | solution.py:204
  6.4 6.1 %collective-permute-start.2 = (bf16[336,256]{1,0:T(8,128)(2,1)S(1)}, bf16[336,256]{1,0:T(8,128)(2,1)S(1)}, u32[]{:S(2)}, u32[]{:S(2)}) collective-permute-start(bf16[336,256]{1,0:T(8,128)(2,1)S(1)} %shard_map.123.refs_0_), channel_id=1, source_target_pairs={{0,2},{1,3},{2,0},{3,1},{4,6},{5,7},{6,4},{7,5},{8,10},{9,11},{10,... | collective-permute-start | bytes 516104 | tf_op jit(solution)/shard_map/ppermute | solution.py:204
  8.0 5.1 %collective-permute-start = (bf16[336,256]{1,0:T(8,128)(2,1)S(1)}, bf16[336,256]{1,0:T(8,128)(2,1)S(1)}, u32[]{:S(2)}, u32[]{:S(2)}) collective-permute-start(bf16[336,256]{1,0:T(8,128)(2,1)S(1)} %shard_map.123.refs_0_), channel_id=1, source_target_pairs={{0,1},{1,0},{2,3},{3,2},{4,5},{5,4},{6,7},{7,6},{8,9},{9,8},{10,11... | collective-permute-start | bytes 516104 | tf_op jit(solution)/shard_map/ppermute | solution.py:204
  8.0 11.3 %collective-permute-start.7 = (bf16[336,256]{1,0:T(8,128)(2,1)S(1)}, bf16[336,256]{1,0:T(8,128)(2,1)S(1)}, u32[]{:S(2)}, u32[]{:S(2)}) collective-permute-start(bf16[336,256]{1,0:T(8,128)(2,1)S(1)} %copy-done.11), channel_id=1, source_target_pairs={{0,8},{1,9},{2,10},{3,11},{4,12},{5,13},{6,14},{7,15},{8,0},{9,1},... | collective-permute-start | bytes 516104 | tf_op jit(solution)/shard_map/ppermute | solution.py:204
  10.8 8.5 %collective-permute-start.12 = (bf16[336,256]{1,0:T(8,128)(2,1)S(1)}, bf16[336,256]{1,0:T(8,128)(2,1)S(1)}, u32[]{:S(2)}, u32[]{:S(2)}) collective-permute-start(bf16[336,256]{1,0:T(8,128)(2,1)S(1)} %collective-permute-done.3.refs_1_), channel_id=1, source_target_pairs={{0,2},{1,3},{2,0},{3,1},{4,6},{5,7},{6,4},{7,5},{8,10},{9,11},{10,... | collective-permute-start | bytes 516104 | tf_op jit(solution)/shard_map/ppermute | solution.py:204
  12.5 7.4 %collective-permute-start.5 = (bf16[336,256]{1,0:T(8,128)(2,1)S(1)}, bf16[336,256]{1,0:T(8,128)(2,1)S(1)}, u32[]{:S(2)}, u32[]{:S(2)}) collective-permute-start(bf16[336,256]{1,0:T(8,128)(2,1)S(1)} %collective-permute-done.3.refs_1_), channel_id=1, source_target_pairs={{0,1},{1,0},{2,3},{3,2},{4,5},{5,4},{6,7},{7,6},{8,9},{9,8},{10,11... | collective-permute-start | bytes 516104 | tf_op jit(solution)/shard_map/ppermute | solution.py:204
  12.5 7.6 %collective-permute-start.4 = (bf16[336,256]{1,0:T(8,128)(2,1)S(1)}, bf16[336,256]{1,0:T(8,128)(2,1)S(1)}, u32[]{:S(2)}, u32[]{:S(2)}) collective-permute-start(bf16[336,256]{1,0:T(8,128)(2,1)S(1)} %collective-permute-done.2.refs_0_), channel_id=1, source_target_pairs={{0,1},{1,0},{2,3},{3,2},{4,5},{5,4},{6,7},{7,6},{8,9},{9,8},{10,11... | collective-permute-start | bytes 516104 | tf_op jit(solution)/shard_map/ppermute | solution.py:204
  19.3 7.9 %collective-permute-start.14 = (bf16[336,256]{1,0:T(8,128)(2,1)S(1)}, bf16[336,256]{1,0:T(8,128)(2,1)S(1)}, u32[]{:S(2)}, u32[]{:S(2)}) collective-permute-start(bf16[336,256]{1,0:T(8,128)(2,1)S(1)} %shard_map.128.refs_1_), channel_id=1, source_target_pairs={{0,1},{1,0},{2,3},{3,2},{4,5},{5,4},{6,7},{7,6},{8,9},{9,8},{10,11... | collective-permute-start | bytes 516104 | tf_op jit(solution)/shard_map/ppermute | solution.py:204
  19.3 6.8 %collective-permute-start.9 = (bf16[336,256]{1,0:T(8,128)(2,1)S(1)}, bf16[336,256]{1,0:T(8,128)(2,1)S(1)}, u32[]{:S(2)}, u32[]{:S(2)}) collective-permute-start(bf16[336,256]{1,0:T(8,128)(2,1)S(1)} %shard_map.128.refs_1_), channel_id=1, source_target_pairs={{0,4},{1,5},{2,6},{3,7},{4,0},{5,1},{6,2},{7,3},{8,12},{9,13},{10,... | collective-permute-start | bytes 516104 | tf_op jit(solution)/shard_map/ppermute | solution.py:204
  19.3 7.3 %collective-permute-start.8 = (bf16[336,256]{1,0:T(8,128)(2,1)S(1)}, bf16[336,256]{1,0:T(8,128)(2,1)S(1)}, u32[]{:S(2)}, u32[]{:S(2)}) collective-permute-start(bf16[336,256]{1,0:T(8,128)(2,1)S(1)} %shard_map.128.refs_1_), channel_id=1, source_target_pairs={{0,2},{1,3},{2,0},{3,1},{4,6},{5,7},{6,4},{7,5},{8,10},{9,11},{10,... | collective-permute-start | bytes 516104 | tf_op jit(solution)/shard_map/ppermute | solution.py:204
  19.9 4.5 %collective-permute-start.1 = (f32[1,64,256]{2,1,0:T(8,128)S(1)}, f32[1,64,256]{2,1,0:T(8,128)S(1)}, u32[]{:S(2)}, u32[]{:S(2)}) collective-permute-start(f32[1,64,256]{2,1,0:T(8,128)S(1)} %get-tuple-element.34), channel_id=1, source_target_pairs={{0,1},{1,0},{2,3},{3,2},{4,5},{5,4},{6,7},{7,6},{8,9},{9,8},{10,11... | collective-permute-start | bytes 196616 | tf_op jit(solution)/shard_map/ppermute | solution.py:204
  20.1 7.1 %collective-permute-start.13 = (bf16[336,256]{1,0:T(8,128)(2,1)S(1)}, bf16[336,256]{1,0:T(8,128)(2,1)S(1)}, u32[]{:S(2)}, u32[]{:S(2)}) collective-permute-start(bf16[336,256]{1,0:T(8,128)(2,1)S(1)} %collective-permute-done.12.refs_0_), channel_id=1, source_target_pairs={{0,1},{1,0},{2,3},{3,2},{4,5},{5,4},{6,7},{7,6},{8,9},{9,8},{10,11... | collective-permute-start | bytes 516104 | tf_op jit(solution)/shard_map/ppermute | solution.py:204
  24.4 2.2 %collective-permute-start.6 = (f32[2,64,256]{2,1,0:T(8,128)S(1)}, f32[2,64,256]{2,1,0:T(8,128)S(1)}, u32[]{:S(2)}, u32[]{:S(2)}) collective-permute-start(f32[2,64,256]{2,1,0:T(8,128)S(1)} %get-tuple-element.36), channel_id=1, source_target_pairs={{0,1},{1,0},{2,3},{3,2},{4,5},{5,4},{6,7},{7,6},{8,9},{9,8},{10,11... | collective-permute-start | bytes 393224 | tf_op jit(solution)/shard_map/ppermute | solution.py:204
  26.1 6.0 %collective-permute-start.20 = (bf16[336,256]{1,0:T(8,128)(2,1)S(1)}, bf16[336,256]{1,0:T(8,128)(2,1)S(1)}, u32[]{:S(2)}, u32[]{:S(2)}) collective-permute-start(bf16[336,256]{1,0:T(8,128)(2,1)S(1)} %shard_map.129.refs_1_), channel_id=1, source_target_pairs={{0,2},{1,3},{2,0},{3,1},{4,6},{5,7},{6,4},{7,5},{8,10},{9,11},{10,... | collective-permute-start | bytes 516104 | tf_op jit(solution)/shard_map/ppermute | solution.py:204
  26.6 5.5 %collective-permute-start.11 = (bf16[336,256]{1,0:T(8,128)(2,1)S(1)}, bf16[336,256]{1,0:T(8,128)(2,1)S(1)}, u32[]{:S(2)}, u32[]{:S(2)}) collective-permute-start(bf16[336,256]{1,0:T(8,128)(2,1)S(1)} %shard_map.129.refs_1_), channel_id=1, source_target_pairs={{0,1},{1,0},{2,3},{3,2},{4,5},{5,4},{6,7},{7,6},{8,9},{9,8},{10,11... | collective-permute-start | bytes 516104 | tf_op jit(solution)/shard_map/ppermute | solution.py:204
  26.7 5.5 %collective-permute-start.10 = (bf16[336,256]{1,0:T(8,128)(2,1)S(1)}, bf16[336,256]{1,0:T(8,128)(2,1)S(1)}, u32[]{:S(2)}, u32[]{:S(2)}) collective-permute-start(bf16[336,256]{1,0:T(8,128)(2,1)S(1)} %collective-permute-done.8.refs_0_), channel_id=1, source_target_pairs={{0,1},{1,0},{2,3},{3,2},{4,5},{5,4},{6,7},{7,6},{8,9},{9,8},{10,11... | collective-permute-start | bytes 516104 | tf_op jit(solution)/shard_map/ppermute | solution.py:204
  31.2 5.5 %collective-permute-start.16 = (f32[2,64,256]{2,1,0:T(8,128)S(1)}, f32[2,64,256]{2,1,0:T(8,128)S(1)}, u32[]{:S(2)}, u32[]{:S(2)}) collective-permute-start(f32[2,64,256]{2,1,0:T(8,128)S(1)} %get-tuple-element.44), channel_id=1, source_target_pairs={{0,1},{1,0},{2,3},{3,2},{4,5},{5,4},{6,7},{7,6},{8,9},{9,8},{10,11... | collective-permute-start | bytes 393224 | tf_op jit(solution)/shard_map/ppermute | solution.py:204
  32.1 6.6 %collective-permute-start.21 = (bf16[336,256]{1,0:T(8,128)(2,1)S(1)}, bf16[336,256]{1,0:T(8,128)(2,1)S(1)}, u32[]{:S(2)}, u32[]{:S(2)}) collective-permute-start(bf16[336,256]{1,0:T(8,128)(2,1)S(1)} %shard_map.137.refs_0_), channel_id=1, source_target_pairs={{0,1},{1,0},{2,3},{3,2},{4,5},{5,4},{6,7},{7,6},{8,9},{9,8},{10,11... | collective-permute-start | bytes 516104 | tf_op jit(solution)/shard_map/ppermute | solution.py:204
  36.1 1.6 %collective-permute-start.15 = (f32[2,64,256]{2,1,0:T(8,128)S(1)}, f32[2,64,256]{2,1,0:T(8,128)S(1)}, u32[]{:S(2)}, u32[]{:S(2)}) collective-permute-start(f32[2,64,256]{2,1,0:T(8,128)S(1)} %get-tuple-element.42), channel_id=1, source_target_pairs={{0,1},{1,0},{2,3},{3,2},{4,5},{5,4},{6,7},{7,6},{8,9},{9,8},{10,11... | collective-permute-start | bytes 393224 | tf_op jit(solution)/shard_map/ppermute | solution.py:204
  37.7 7.0 %collective-permute-start.17 = (bf16[3,64,256]{2,1,0:T(8,128)(2,1)S(1)}, bf16[3,64,256]{2,1,0:T(8,128)(2,1)S(1)}, u32[]{:S(2)}, u32[]{:S(2)}) collective-permute-start(bf16[3,64,256]{2,1,0:T(8,128)(2,1)S(1)} %shard_map.134), channel_id=1, source_target_pairs={{0,2},{1,3},{2,0},{3,1},{4,6},{5,7},{6,4},{7,5},{8,10},{9,11},{10,... | collective-permute-start | bytes 294920 | tf_op jit(solution)/shard_map/ppermute | solution.py:204
  44.6 2.0 %collective-permute-start.22 = (f32[1,64,256]{2,1,0:T(8,128)S(1)}, f32[1,64,256]{2,1,0:T(8,128)S(1)}, u32[]{:S(2)}, u32[]{:S(2)}) collective-permute-start(f32[1,64,256]{2,1,0:T(8,128)S(1)} %get-tuple-element.53), channel_id=1, source_target_pairs={{0,1},{1,0},{2,3},{3,2},{4,5},{5,4},{6,7},{7,6},{8,9},{9,8},{10,11... | collective-permute-start | bytes 196616 | tf_op jit(solution)/shard_map/ppermute | solution.py:204
  44.8 4.6 %collective-permute-start.18 = (bf16[2,64,256]{2,1,0:T(8,128)(2,1)S(1)}, bf16[2,64,256]{2,1,0:T(8,128)(2,1)S(1)}, u32[]{:S(2)}, u32[]{:S(2)}) collective-permute-start(bf16[2,64,256]{2,1,0:T(8,128)(2,1)S(1)} %get-tuple-element.49), channel_id=1, source_target_pairs={{0,4},{1,5},{2,6},{3,7},{4,0},{5,1},{6,2},{7,3},{8,12},{9,13},{10,... | collective-permute-start | bytes 196616 | tf_op jit(solution)/shard_map/ppermute | solution.py:204
  46.7 7.8 %collective-permute-start.23 = (bf16[1,64,256]{2,1,0:T(8,128)(2,1)S(1)}, bf16[1,64,256]{2,1,0:T(8,128)(2,1)S(1)}, u32[]{:S(2)}, u32[]{:S(2)}) collective-permute-start(bf16[1,64,256]{2,1,0:T(8,128)(2,1)S(1)} %shard_map.140), channel_id=1, source_target_pairs={{0,14},{1,15},{2,12},{3,13},{4,10},{5,11},{6,8},{7,9},{8,6},{9,7},... | collective-permute-start | bytes 98312 | tf_op jit(solution)/shard_map/ppermute | solution.py:204
  49.3 5.2 %collective-permute-start.19 = (bf16[1,64,256]{2,1,0:T(8,128)(2,1)S(1)}, bf16[1,64,256]{2,1,0:T(8,128)(2,1)S(1)}, u32[]{:S(2)}, u32[]{:S(2)}) collective-permute-start(bf16[1,64,256]{2,1,0:T(8,128)(2,1)S(1)} %get-tuple-element.51), channel_id=1, source_target_pairs={{0,8},{1,9},{2,10},{3,11},{4,12},{5,13},{6,14},{7,15},{8,0},{9,1},... | collective-permute-start | bytes 98312 | tf_op jit(solution)/shard_map/ppermute | solution.py:204
  (12 other events, 68.3 us)

commit v5 on v4

--- a/solution.py
+++ b/solution.py
@@ -150,11 +150,12 @@
     col = lax.broadcasted_iota(jnp.int32, (npno, npno), 1)
     for p in range(per):
         total = jnp.zeros((npno, npno), jnp.float32)
-        for c in range(ncpl):
-            half = half_ref[p * ncpl + c]
+        for first in range(0, ncpl, 4):
+            some = range(first, min(first + 4, ncpl))
+            half = jnp.concatenate([half_ref[p * ncpl + c] for c in some], axis=1)
             high = half.astype(jnp.bfloat16)
             low = (half - high.astype(jnp.float32)).astype(jnp.bfloat16)
-            inter = inter_ref[p, c]
+            inter = jnp.concatenate([inter_ref[p, c] for c in some], axis=1)
             total = total + lax.dot_general(high, inter, NT, preferred_element_type=jnp.float32)
             total = total + lax.dot_general(low, inter, NT, preferred_element_type=jnp.float32)
         here = slice(p * npno, (p + 1) * npno)

time: 55.5 us -> 55.4 us (level)
  transfers between devices with their start and end apart: 24 -> 24, of which waited for: 5 -> 6; matrix products, arithmetic and copies ran while one was open for 0% -> 0% of each run, Pallas kernels for 34% -> 34%
where the time goes in v5:
time: 55.4 us; the launch traced here: 55.2 us
  Pallas kernels  21.3 us (38%)
  starting transfers between devices  21.1 us (38%)
  waiting for transfers between devices  7.48 us (14%)
  local copies, waits for them, and re-layouts  4.35 us (8%)
  between operations  0.91 us (2%)
    ppermute x24, starting transfers between devices, swap(): return lax.ppermute(array, 'pairs', [(d, d ^ mask) for d in range(ndev)])  21.1 us
    pallas_call x5, Pallas kernels, exchange(): pl.pallas_call(functools.partial(exch_kernel, count, per, npno), out_shap...  16.8 us
    ppermute x24, waiting for transfers between devices, swap(): return lax.ppermute(array, 'pairs', [(d, d ^ mask) for d in range(ndev)])  7.48 us
    unnamed x24, local copies, waits for them, and re-layouts  4.35 us
    pallas_call x1, Pallas kernels, shards(): pl.pallas_call(pack_kernel, out_shape=[jax.ShapeDtypeStruct(((per + 1) *...  1.86 us
    pallas_call x1, Pallas kernels, shards(): pl.pallas_call(functools.partial(coupled_kernel, [order for _, order in a...  1.7 us
  transfers between devices with their start and end apart: 24, of which 6 were waited for; matrix products, arithmetic and copies ran while one was open for 0% of the time, Pallas kernels for 34%

profile of v5, /device:TPU:0, one launch (start us, length us, event | category | flops | bytes accessed | tf_op | source)
XLA Modules:
  0.0 55.2 jit_solution(7482824413536135643)
XLA Ops:
  0.6 1.9 %shard_map.122 = (bf16[336,256]{1,0:T(8,128)(2,1)}, bf16[336,256]{1,0:T(8,128)(2,1)}) custom-call(bf16[4,64,256]{2,1,0:T(8,128)(2,1)} %bitcast.4, s32[4,256]{1,0:T(4,128)} %dom_ref.1, s32[2,4]{1,0:T(2,128)} %bitcast.2, f32[4,64,64]{2,1,0:T(8,128)} %refs_12_.1), custom_call_target="tpu_custom_call" | custom-call | tf_op jit(solution)/shard_map/pallas_call | solution.py:207
  2.5 0.9 %copy-done.2 = bf16[336,256]{1,0:T(8,128)(2,1)S(1)} copy-done((bf16[336,256]{1,0:T(8,128)(2,1)S(1)}, bf16[336,256]{1,0:T(8,128)(2,1)}, u32[]{:S(2)}) %copy-start.2) | copy-done | bytes 172056
  3.4 3.0 %collective-permute-start.3 = (bf16[336,256]{1,0:T(8,128)(2,1)S(1)}, bf16[336,256]{1,0:T(8,128)(2,1)S(1)}, u32[]{:S(2)}, u32[]{:S(2)}) collective-permute-start(bf16[336,256]{1,0:T(8,128)(2,1)S(1)} %shard_map.123.refs_0_), channel_id=1, source_target_pairs={{0,4},{1,5},{2,6},{3,7},{4,0},{5,1},{6,2},{7,3},{8,12},{9,13},{10,... | collective-permute-start | bytes 516104 | tf_op jit(solution)/shard_map/ppermute | solution.py:205
  6.4 1.5 %collective-permute-start.2 = (bf16[336,256]{1,0:T(8,128)(2,1)S(1)}, bf16[336,256]{1,0:T(8,128)(2,1)S(1)}, u32[]{:S(2)}, u32[]{:S(2)}) collective-permute-start(bf16[336,256]{1,0:T(8,128)(2,1)S(1)} %shard_map.123.refs_0_), channel_id=1, source_target_pairs={{0,2},{1,3},{2,0},{3,1},{4,6},{5,7},{6,4},{7,5},{8,10},{9,11},{10,... | collective-permute-start | bytes 516104 | tf_op jit(solution)/shard_map/ppermute | solution.py:205
  8.0 2.6 %collective-permute-start.7 = (bf16[336,256]{1,0:T(8,128)(2,1)S(1)}, bf16[336,256]{1,0:T(8,128)(2,1)S(1)}, u32[]{:S(2)}, u32[]{:S(2)}) collective-permute-start(bf16[336,256]{1,0:T(8,128)(2,1)S(1)} %copy-done.11), channel_id=1, source_target_pairs={{0,8},{1,9},{2,10},{3,11},{4,12},{5,13},{6,14},{7,15},{8,0},{9,1},... | collective-permute-start | bytes 516104 | tf_op jit(solution)/shard_map/ppermute | solution.py:205
  10.8 1.7 %collective-permute-start.12 = (bf16[336,256]{1,0:T(8,128)(2,1)S(1)}, bf16[336,256]{1,0:T(8,128)(2,1)S(1)}, u32[]{:S(2)}, u32[]{:S(2)}) collective-permute-start(bf16[336,256]{1,0:T(8,128)(2,1)S(1)} %collective-permute-done.3.refs_1_), channel_id=1, source_target_pairs={{0,2},{1,3},{2,0},{3,1},{4,6},{5,7},{6,4},{7,5},{8,10},{9,11},{10,... | collective-permute-start | bytes 516104 | tf_op jit(solution)/shard_map/ppermute | solution.py:205
  13.0 2.5 %shard_map.124 = (f32[1,64,256]{2,1,0:T(8,128)S(1)}, f32[1,64,256]{2,1,0:T(8,128)S(1)}, bf16[2,64,256]{2,1,0:T(8,128)(2,1)S(1)}) custom-call(bf16[336,256]{1,0:T(8,128)(2,1)S(1)} %shard_map.123.refs_0_, bf16[336,256]{1,0:T(8,128)(2,1)S(1)} %collective-permute-done.refs_1_, bf16[32,1024,128]{2,1,0:T(8,128)(2,1)S(1)} %copy-done), custom_call_target="tpu_custom_call" | custom-call | bytes 1048576 | tf_op jit(solution)/shard_map/pallas_call | solution.py:260
  15.5 3.8 %collective-permute-done.7.refs_0_ = bf16[336,256]{1,0:T(8,128)(2,1)S(1)} collective-permute-done((bf16[336,256]{1,0:T(8,128)(2,1)S(1)}, bf16[336,256]{1,0:T(8,128)(2,1)S(1)}, u32[]{:S(2)}, u32[]{:S(2)}) %collective-permute-start.7) | collective-permute-done | bytes 172064 | tf_op jit(solution)/shard_map/ppermute | solution.py:205
  19.3 0.6 %collective-permute-start.8 = (bf16[336,256]{1,0:T(8,128)(2,1)S(1)}, bf16[336,256]{1,0:T(8,128)(2,1)S(1)}, u32[]{:S(2)}, u32[]{:S(2)}) collective-permute-start(bf16[336,256]{1,0:T(8,128)(2,1)S(1)} %shard_map.128.refs_1_), channel_id=1, source_target_pairs={{0,2},{1,3},{2,0},{3,1},{4,6},{5,7},{6,4},{7,5},{8,10},{9,11},{10,... | collective-permute-start | bytes 516104 | tf_op jit(solution)/shard_map/ppermute | solution.py:205
  20.4 4.0 %shard_map.126 = (f32[2,64,256]{2,1,0:T(8,128)S(1)}, f32[2,64,256]{2,1,0:T(8,128)S(1)}, bf16[4,64,256]{2,1,0:T(8,128)(2,1)S(1)}) custom-call(bf16[336,256]{1,0:T(8,128)(2,1)S(1)} %collective-permute-done.2.refs_0_, bf16[336,256]{1,0:T(8,128)(2,1)S(1)} %collective-permute-done.3.refs_1_, bf16[336,256]{1,0:T(8,128)(2,1)S(1)} %collective-permute-done.4.refs_2_, ...), custom_call_target="tpu_custom_call" | custom-call | flops 4800000000 | bytes 1048576 | tf_op jit(solution)/shard_map/pallas_call | solution.py:260
  24.7 1.4 %collective-permute-done.9.refs_0_ = bf16[336,256]{1,0:T(8,128)(2,1)S(1)} collective-permute-done((bf16[336,256]{1,0:T(8,128)(2,1)S(1)}, bf16[336,256]{1,0:T(8,128)(2,1)S(1)}, u32[]{:S(2)}, u32[]{:S(2)}) %collective-permute-start.9) | collective-permute-done | bytes 172064 | tf_op jit(solution)/shard_map/ppermute | solution.py:205
  27.2 4.0 %shard_map.130 = (f32[2,64,256]{2,1,0:T(8,128)S(1)}, f32[2,64,256]{2,1,0:T(8,128)S(1)}, bf16[4,64,256]{2,1,0:T(8,128)(2,1)S(1)}) custom-call(bf16[336,256]{1,0:T(8,128)(2,1)S(1)} %collective-permute-done.12.refs_0_, bf16[336,256]{1,0:T(8,128)(2,1)S(1)} %shard_map.128.refs_1_, bf16[336,256]{1,0:T(8,128)(2,1)S(1)} %collective-permute-done.13.refs_2_, ...), custom_call_target="tpu_custom_call" | custom-call | flops 4800000000 | bytes 1048576 | tf_op jit(solution)/shard_map/pallas_call | solution.py:260
  31.3 0.8 %collective-permute-done.20.refs_0_ = bf16[336,256]{1,0:T(8,128)(2,1)S(1)} collective-permute-done((bf16[336,256]{1,0:T(8,128)(2,1)S(1)}, bf16[336,256]{1,0:T(8,128)(2,1)S(1)}, u32[]{:S(2)}, u32[]{:S(2)}) %collective-permute-start.20) | collective-permute-done | bytes 172064 | tf_op jit(solution)/shard_map/ppermute | solution.py:205
  32.1 4.0 %shard_map.131 = (f32[2,64,256]{2,1,0:T(8,128)S(1)}, f32[2,64,256]{2,1,0:T(8,128)S(1)}, bf16[4,64,256]{2,1,0:T(8,128)(2,1)S(1)}) custom-call(bf16[336,256]{1,0:T(8,128)(2,1)S(1)} %collective-permute-done.8.refs_0_, bf16[336,256]{1,0:T(8,128)(2,1)S(1)} %shard_map.129.refs_1_, bf16[336,256]{1,0:T(8,128)(2,1)S(1)} %collective-permute-done.10.refs_2_, ...), custom_call_target="tpu_custom_call" | custom-call | flops 4800000000 | bytes 1048576 | tf_op jit(solution)/shard_map/pallas_call | solution.py:260
  36.1 0.6 %collective-permute-start.15 = (f32[2,64,256]{2,1,0:T(8,128)S(1)}, f32[2,64,256]{2,1,0:T(8,128)S(1)}, u32[]{:S(2)}, u32[]{:S(2)}) collective-permute-start(f32[2,64,256]{2,1,0:T(8,128)S(1)} %get-tuple-element.42), channel_id=1, source_target_pairs={{0,1},{1,0},{2,3},{3,2},{4,5},{5,4},{6,7},{7,6},{8,9},{9,8},{10,11... | collective-permute-start | bytes 393224 | tf_op jit(solution)/shard_map/ppermute | solution.py:205
  36.7 1.0 %collective-permute-done.15.refs_1_ = f32[2,64,256]{2,1,0:T(8,128)S(1)} collective-permute-done((f32[2,64,256]{2,1,0:T(8,128)S(1)}, f32[2,64,256]{2,1,0:T(8,128)S(1)}, u32[]{:S(2)}, u32[]{:S(2)}) %collective-permute-start.15) | collective-permute-done | bytes 131104 | tf_op jit(solution)/shard_map/ppermute | solution.py:205
  37.7 1.0 %collective-permute-start.17 = (bf16[3,64,256]{2,1,0:T(8,128)(2,1)S(1)}, bf16[3,64,256]{2,1,0:T(8,128)(2,1)S(1)}, u32[]{:S(2)}, u32[]{:S(2)}) collective-permute-start(bf16[3,64,256]{2,1,0:T(8,128)(2,1)S(1)} %shard_map.134), channel_id=1, source_target_pairs={{0,2},{1,3},{2,0},{3,1},{4,6},{5,7},{6,4},{7,5},{8,10},{9,11},{10,... | collective-permute-start | bytes 294920 | tf_op jit(solution)/shard_map/ppermute | solution.py:205
  38.7 3.4 %copy-done.1 = bf16[32,1024,128]{2,1,0:T(8,128)(2,1)S(1)} copy-done((bf16[32,1024,128]{2,1,0:T(8,128)(2,1)S(1)}, bf16[32,1024,128]{2,1,0:T(8,128)(2,1)}, u32[]{:S(2)}) %copy-start.1) | copy-done | bytes 8388632
  42.1 2.5 %shard_map.138 = (f32[1,64,256]{2,1,0:T(8,128)S(1)}, f32[1,64,256]{2,1,0:T(8,128)S(1)}, bf16[2,64,256]{2,1,0:T(8,128)(2,1)S(1)}) custom-call(bf16[336,256]{1,0:T(8,128)(2,1)S(1)} %shard_map.137.refs_0_, bf16[336,256]{1,0:T(8,128)(2,1)S(1)} %collective-permute-done.21.refs_1_, bf16[32,1024,128]{2,1,0:T(8,128)(2,1)S(1)} %copy-done.1, ...), custom_call_target="tpu_custom_call" | custom-call | flops 2400000000 | bytes 1048576 | tf_op jit(solution)/shard_map/pallas_call | solution.py:260
  44.8 1.9 %collective-permute-start.18 = (bf16[2,64,256]{2,1,0:T(8,128)(2,1)S(1)}, bf16[2,64,256]{2,1,0:T(8,128)(2,1)S(1)}, u32[]{:S(2)}, u32[]{:S(2)}) collective-permute-start(bf16[2,64,256]{2,1,0:T(8,128)(2,1)S(1)} %get-tuple-element.49), channel_id=1, source_target_pairs={{0,4},{1,5},{2,6},{3,7},{4,0},{5,1},{6,2},{7,3},{8,12},{9,13},{10,... | collective-permute-start | bytes 196616 | tf_op jit(solution)/shard_map/ppermute | solution.py:205
  46.7 2.6 %collective-permute-start.23 = (bf16[1,64,256]{2,1,0:T(8,128)(2,1)S(1)}, bf16[1,64,256]{2,1,0:T(8,128)(2,1)S(1)}, u32[]{:S(2)}, u32[]{:S(2)}) collective-permute-start(bf16[1,64,256]{2,1,0:T(8,128)(2,1)S(1)} %shard_map.140), channel_id=1, source_target_pairs={{0,14},{1,15},{2,12},{3,13},{4,10},{5,11},{6,8},{7,9},{8,6},{9,7},... | collective-permute-start | bytes 98312 | tf_op jit(solution)/shard_map/ppermute | solution.py:205
  49.3 3.2 %collective-permute-start.19 = (bf16[1,64,256]{2,1,0:T(8,128)(2,1)S(1)}, bf16[1,64,256]{2,1,0:T(8,128)(2,1)S(1)}, u32[]{:S(2)}, u32[]{:S(2)}) collective-permute-start(bf16[1,64,256]{2,1,0:T(8,128)(2,1)S(1)} %get-tuple-element.51), channel_id=1, source_target_pairs={{0,8},{1,9},{2,10},{3,11},{4,12},{5,13},{6,14},{7,15},{8,0},{9,1},... | collective-permute-start | bytes 98312 | tf_op jit(solution)/shard_map/ppermute | solution.py:205
  52.6 1.7 %shard_map.141 = (f32[64,256]{1,0:T(8,128)S(1)}, f32[64,256]{1,0:T(8,128)S(1)}, f32[64,256]{1,0:T(8,128)S(1)}) custom-call(bf16[2,64,256]{2,1,0:T(8,128)(2,1)S(1)} %get-tuple-element.54.refs_0_, bf16[4,64,256]{2,1,0:T(8,128)(2,1)S(1)} %get-tuple-element.55.refs_1_, bf16[4,64,256]{2,1,0:T(8,128)(2,1)S(1)} %get-tuple-element.56.refs_2_, ...), custom_call_target="tpu_custom_call" | custom-call | flops 2400000000 | bytes 1048576 | tf_op jit(solution)/shard_map/pallas_call | solution.py:341
  54.4 0.8 %shard_map.142 = (f32[4,64,64]{2,1,0:T(8,128)}, f32[4,64,64]{2,1,0:T(8,128)}) custom-call(f32[1,64,256]{2,1,0:T(8,128)S(1)} %get-tuple-element.50.refs_13_.own_ref, bf16[1,64,256]{2,1,0:T(8,128)(2,1)S(1)} %collective-permute-done.19.came_ref, bf16[1,64,256]{2,1,0:T(8,128)(2,1)S(1)} %collective-permute-done.23.late_ref, ...), custom_call_target="tpu_custom_call" | custom-call | tf_op jit(solution)/shard_map/pallas_call | solution.py:365
  (70 shorter events, 3.2 us)
Async XLA Ops:
  3.4 7.4 %collective-permute-start.3 = (bf16[336,256]{1,0:T(8,128)(2,1)S(1)}, bf16[336,256]{1,0:T(8,128)(2,1)S(1)}, u32[]{:S(2)}, u32[]{:S(2)}) collective-permute-start(bf16[336,256]{1,0:T(8,128)(2,1)S(1)} %shard_map.123.refs_0_), channel_id=1, source_target_pairs={{0,4},{1,5},{2,6},{3,7},{4,0},{5,1},{6,2},{7,3},{8,12},{9,13},{10,... | collective-permute-start | bytes 516104 | tf_op jit(solution)/shard_map/ppermute | solution.py:205
  6.4 6.1 %collective-permute-start.2 = (bf16[336,256]{1,0:T(8,128)(2,1)S(1)}, bf16[336,256]{1,0:T(8,128)(2,1)S(1)}, u32[]{:S(2)}, u32[]{:S(2)}) collective-permute-start(bf16[336,256]{1,0:T(8,128)(2,1)S(1)} %shard_map.123.refs_0_), channel_id=1, source_target_pairs={{0,2},{1,3},{2,0},{3,1},{4,6},{5,7},{6,4},{7,5},{8,10},{9,11},{10,... | collective-permute-start | bytes 516104 | tf_op jit(solution)/shard_map/ppermute | solution.py:205
  8.0 5.1 %collective-permute-start = (bf16[336,256]{1,0:T(8,128)(2,1)S(1)}, bf16[336,256]{1,0:T(8,128)(2,1)S(1)}, u32[]{:S(2)}, u32[]{:S(2)}) collective-permute-start(bf16[336,256]{1,0:T(8,128)(2,1)S(1)} %shard_map.123.refs_0_), channel_id=1, source_target_pairs={{0,1},{1,0},{2,3},{3,2},{4,5},{5,4},{6,7},{7,6},{8,9},{9,8},{10,11... | collective-permute-start | bytes 516104 | tf_op jit(solution)/shard_map/ppermute | solution.py:205
  8.0 11.3 %collective-permute-start.7 = (bf16[336,256]{1,0:T(8,128)(2,1)S(1)}, bf16[336,256]{1,0:T(8,128)(2,1)S(1)}, u32[]{:S(2)}, u32[]{:S(2)}) collective-permute-start(bf16[336,256]{1,0:T(8,128)(2,1)S(1)} %copy-done.11), channel_id=1, source_target_pairs={{0,8},{1,9},{2,10},{3,11},{4,12},{5,13},{6,14},{7,15},{8,0},{9,1},... | collective-permute-start | bytes 516104 | tf_op jit(solution)/shard_map/ppermute | solution.py:205
  10.8 8.5 %collective-permute-start.12 = (bf16[336,256]{1,0:T(8,128)(2,1)S(1)}, bf16[336,256]{1,0:T(8,128)(2,1)S(1)}, u32[]{:S(2)}, u32[]{:S(2)}) collective-permute-start(bf16[336,256]{1,0:T(8,128)(2,1)S(1)} %collective-permute-done.3.refs_1_), channel_id=1, source_target_pairs={{0,2},{1,3},{2,0},{3,1},{4,6},{5,7},{6,4},{7,5},{8,10},{9,11},{10,... | collective-permute-start | bytes 516104 | tf_op jit(solution)/shard_map/ppermute | solution.py:205
  12.5 7.4 %collective-permute-start.5 = (bf16[336,256]{1,0:T(8,128)(2,1)S(1)}, bf16[336,256]{1,0:T(8,128)(2,1)S(1)}, u32[]{:S(2)}, u32[]{:S(2)}) collective-permute-start(bf16[336,256]{1,0:T(8,128)(2,1)S(1)} %collective-permute-done.3.refs_1_), channel_id=1, source_target_pairs={{0,1},{1,0},{2,3},{3,2},{4,5},{5,4},{6,7},{7,6},{8,9},{9,8},{10,11... | collective-permute-start | bytes 516104 | tf_op jit(solution)/shard_map/ppermute | solution.py:205
  12.5 7.6 %collective-permute-start.4 = (bf16[336,256]{1,0:T(8,128)(2,1)S(1)}, bf16[336,256]{1,0:T(8,128)(2,1)S(1)}, u32[]{:S(2)}, u32[]{:S(2)}) collective-permute-start(bf16[336,256]{1,0:T(8,128)(2,1)S(1)} %collective-permute-done.2.refs_0_), channel_id=1, source_target_pairs={{0,1},{1,0},{2,3},{3,2},{4,5},{5,4},{6,7},{7,6},{8,9},{9,8},{10,11... | collective-permute-start | bytes 516104 | tf_op jit(solution)/shard_map/ppermute | solution.py:205
  19.3 7.9 %collective-permute-start.14 = (bf16[336,256]{1,0:T(8,128)(2,1)S(1)}, bf16[336,256]{1,0:T(8,128)(2,1)S(1)}, u32[]{:S(2)}, u32[]{:S(2)}) collective-permute-start(bf16[336,256]{1,0:T(8,128)(2,1)S(1)} %shard_map.128.refs_1_), channel_id=1, source_target_pairs={{0,1},{1,0},{2,3},{3,2},{4,5},{5,4},{6,7},{7,6},{8,9},{9,8},{10,11... | collective-permute-start | bytes 516104 | tf_op jit(solution)/shard_map/ppermute | solution.py:205
  19.3 6.8 %collective-permute-start.9 = (bf16[336,256]{1,0:T(8,128)(2,1)S(1)}, bf16[336,256]{1,0:T(8,128)(2,1)S(1)}, u32[]{:S(2)}, u32[]{:S(2)}) collective-permute-start(bf16[336,256]{1,0:T(8,128)(2,1)S(1)} %shard_map.128.refs_1_), channel_id=1, source_target_pairs={{0,4},{1,5},{2,6},{3,7},{4,0},{5,1},{6,2},{7,3},{8,12},{9,13},{10,... | collective-permute-start | bytes 516104 | tf_op jit(solution)/shard_map/ppermute | solution.py:205
  19.3 7.3 %collective-permute-start.8 = (bf16[336,256]{1,0:T(8,128)(2,1)S(1)}, bf16[336,256]{1,0:T(8,128)(2,1)S(1)}, u32[]{:S(2)}, u32[]{:S(2)}) collective-permute-start(bf16[336,256]{1,0:T(8,128)(2,1)S(1)} %shard_map.128.refs_1_), channel_id=1, source_target_pairs={{0,2},{1,3},{2,0},{3,1},{4,6},{5,7},{6,4},{7,5},{8,10},{9,11},{10,... | collective-permute-start | bytes 516104 | tf_op jit(solution)/shard_map/ppermute | solution.py:205
  19.9 4.5 %collective-permute-start.1 = (f32[1,64,256]{2,1,0:T(8,128)S(1)}, f32[1,64,256]{2,1,0:T(8,128)S(1)}, u32[]{:S(2)}, u32[]{:S(2)}) collective-permute-start(f32[1,64,256]{2,1,0:T(8,128)S(1)} %get-tuple-element.34), channel_id=1, source_target_pairs={{0,1},{1,0},{2,3},{3,2},{4,5},{5,4},{6,7},{7,6},{8,9},{9,8},{10,11... | collective-permute-start | bytes 196616 | tf_op jit(solution)/shard_map/ppermute | solution.py:205
  20.1 7.1 %collective-permute-start.13 = (bf16[336,256]{1,0:T(8,128)(2,1)S(1)}, bf16[336,256]{1,0:T(8,128)(2,1)S(1)}, u32[]{:S(2)}, u32[]{:S(2)}) collective-permute-start(bf16[336,256]{1,0:T(8,128)(2,1)S(1)} %collective-permute-done.12.refs_0_), channel_id=1, source_target_pairs={{0,1},{1,0},{2,3},{3,2},{4,5},{5,4},{6,7},{7,6},{8,9},{9,8},{10,11... | collective-permute-start | bytes 516104 | tf_op jit(solution)/shard_map/ppermute | solution.py:205
  24.4 2.2 %collective-permute-start.6 = (f32[2,64,256]{2,1,0:T(8,128)S(1)}, f32[2,64,256]{2,1,0:T(8,128)S(1)}, u32[]{:S(2)}, u32[]{:S(2)}) collective-permute-start(f32[2,64,256]{2,1,0:T(8,128)S(1)} %get-tuple-element.36), channel_id=1, source_target_pairs={{0,1},{1,0},{2,3},{3,2},{4,5},{5,4},{6,7},{7,6},{8,9},{9,8},{10,11... | collective-permute-start | bytes 393224 | tf_op jit(solution)/shard_map/ppermute | solution.py:205
  26.1 6.0 %collective-permute-start.20 = (bf16[336,256]{1,0:T(8,128)(2,1)S(1)}, bf16[336,256]{1,0:T(8,128)(2,1)S(1)}, u32[]{:S(2)}, u32[]{:S(2)}) collective-permute-start(bf16[336,256]{1,0:T(8,128)(2,1)S(1)} %shard_map.129.refs_1_), channel_id=1, source_target_pairs={{0,2},{1,3},{2,0},{3,1},{4,6},{5,7},{6,4},{7,5},{8,10},{9,11},{10,... | collective-permute-start | bytes 516104 | tf_op jit(solution)/shard_map/ppermute | solution.py:205
  26.6 5.5 %collective-permute-start.11 = (bf16[336,256]{1,0:T(8,128)(2,1)S(1)}, bf16[336,256]{1,0:T(8,128)(2,1)S(1)}, u32[]{:S(2)}, u32[]{:S(2)}) collective-permute-start(bf16[336,256]{1,0:T(8,128)(2,1)S(1)} %shard_map.129.refs_1_), channel_id=1, source_target_pairs={{0,1},{1,0},{2,3},{3,2},{4,5},{5,4},{6,7},{7,6},{8,9},{9,8},{10,11... | collective-permute-start | bytes 516104 | tf_op jit(solution)/shard_map/ppermute | solution.py:205
  26.7 5.5 %collective-permute-start.10 = (bf16[336,256]{1,0:T(8,128)(2,1)S(1)}, bf16[336,256]{1,0:T(8,128)(2,1)S(1)}, u32[]{:S(2)}, u32[]{:S(2)}) collective-permute-start(bf16[336,256]{1,0:T(8,128)(2,1)S(1)} %collective-permute-done.8.refs_0_), channel_id=1, source_target_pairs={{0,1},{1,0},{2,3},{3,2},{4,5},{5,4},{6,7},{7,6},{8,9},{9,8},{10,11... | collective-permute-start | bytes 516104 | tf_op jit(solution)/shard_map/ppermute | solution.py:205
  31.2 5.5 %collective-permute-start.16 = (f32[2,64,256]{2,1,0:T(8,128)S(1)}, f32[2,64,256]{2,1,0:T(8,128)S(1)}, u32[]{:S(2)}, u32[]{:S(2)}) collective-permute-start(f32[2,64,256]{2,1,0:T(8,128)S(1)} %get-tuple-element.44), channel_id=1, source_target_pairs={{0,1},{1,0},{2,3},{3,2},{4,5},{5,4},{6,7},{7,6},{8,9},{9,8},{10,11... | collective-permute-start | bytes 393224 | tf_op jit(solution)/shard_map/ppermute | solution.py:205
  32.1 6.6 %collective-permute-start.21 = (bf16[336,256]{1,0:T(8,128)(2,1)S(1)}, bf16[336,256]{1,0:T(8,128)(2,1)S(1)}, u32[]{:S(2)}, u32[]{:S(2)}) collective-permute-start(bf16[336,256]{1,0:T(8,128)(2,1)S(1)} %shard_map.137.refs_0_), channel_id=1, source_target_pairs={{0,1},{1,0},{2,3},{3,2},{4,5},{5,4},{6,7},{7,6},{8,9},{9,8},{10,11... | collective-permute-start | bytes 516104 | tf_op jit(solution)/shard_map/ppermute | solution.py:205
  36.1 1.6 %collective-permute-start.15 = (f32[2,64,256]{2,1,0:T(8,128)S(1)}, f32[2,64,256]{2,1,0:T(8,128)S(1)}, u32[]{:S(2)}, u32[]{:S(2)}) collective-permute-start(f32[2,64,256]{2,1,0:T(8,128)S(1)} %get-tuple-element.42), channel_id=1, source_target_pairs={{0,1},{1,0},{2,3},{3,2},{4,5},{5,4},{6,7},{7,6},{8,9},{9,8},{10,11... | collective-permute-start | bytes 393224 | tf_op jit(solution)/shard_map/ppermute | solution.py:205
  37.7 7.0 %collective-permute-start.17 = (bf16[3,64,256]{2,1,0:T(8,128)(2,1)S(1)}, bf16[3,64,256]{2,1,0:T(8,128)(2,1)S(1)}, u32[]{:S(2)}, u32[]{:S(2)}) collective-permute-start(bf16[3,64,256]{2,1,0:T(8,128)(2,1)S(1)} %shard_map.134), channel_id=1, source_target_pairs={{0,2},{1,3},{2,0},{3,1},{4,6},{5,7},{6,4},{7,5},{8,10},{9,11},{10,... | collective-permute-start | bytes 294920 | tf_op jit(solution)/shard_map/ppermute | solution.py:205
  44.6 2.0 %collective-permute-start.22 = (f32[1,64,256]{2,1,0:T(8,128)S(1)}, f32[1,64,256]{2,1,0:T(8,128)S(1)}, u32[]{:S(2)}, u32[]{:S(2)}) collective-permute-start(f32[1,64,256]{2,1,0:T(8,128)S(1)} %get-tuple-element.53), channel_id=1, source_target_pairs={{0,1},{1,0},{2,3},{3,2},{4,5},{5,4},{6,7},{7,6},{8,9},{9,8},{10,11... | collective-permute-start | bytes 196616 | tf_op jit(solution)/shard_map/ppermute | solution.py:205
  44.8 4.6 %collective-permute-start.18 = (bf16[2,64,256]{2,1,0:T(8,128)(2,1)S(1)}, bf16[2,64,256]{2,1,0:T(8,128)(2,1)S(1)}, u32[]{:S(2)}, u32[]{:S(2)}) collective-permute-start(bf16[2,64,256]{2,1,0:T(8,128)(2,1)S(1)} %get-tuple-element.49), channel_id=1, source_target_pairs={{0,4},{1,5},{2,6},{3,7},{4,0},{5,1},{6,2},{7,3},{8,12},{9,13},{10,... | collective-permute-start | bytes 196616 | tf_op jit(solution)/shard_map/ppermute | solution.py:205
  46.7 7.6 %collective-permute-start.23 = (bf16[1,64,256]{2,1,0:T(8,128)(2,1)S(1)}, bf16[1,64,256]{2,1,0:T(8,128)(2,1)S(1)}, u32[]{:S(2)}, u32[]{:S(2)}) collective-permute-start(bf16[1,64,256]{2,1,0:T(8,128)(2,1)S(1)} %shard_map.140), channel_id=1, source_target_pairs={{0,14},{1,15},{2,12},{3,13},{4,10},{5,11},{6,8},{7,9},{8,6},{9,7},... | collective-permute-start | bytes 98312 | tf_op jit(solution)/shard_map/ppermute | solution.py:205
  49.3 5.1 %collective-permute-start.19 = (bf16[1,64,256]{2,1,0:T(8,128)(2,1)S(1)}, bf16[1,64,256]{2,1,0:T(8,128)(2,1)S(1)}, u32[]{:S(2)}, u32[]{:S(2)}) collective-permute-start(bf16[1,64,256]{2,1,0:T(8,128)(2,1)S(1)} %get-tuple-element.51), channel_id=1, source_target_pairs={{0,8},{1,9},{2,10},{3,11},{4,12},{5,13},{6,14},{7,15},{8,0},{9,1},... | collective-permute-start | bytes 98312 | tf_op jit(solution)/shard_map/ppermute | solution.py:205
  (12 other events, 68.3 us)
